TPU v7x, 32 devices: a whole 2x2x4 slice. The times are simulated.
32 devices in a mesh: dp: 8 (over z, x), group: 4 (over y, core).
Axes of the slice: x: 2, y: 2, z: 4, core: 2. Of those that a mesh axis runs over, the one named last changes fastest.
Arguments:
- tokens: bfloat16 [512, 144, 384], P('dp', 'group'), may hold values from -6 to 6
- keep_mask: int32 [512, 144], P(('dp', 'group')), may hold values from 0 to 1, as said below
- cotangent: bfloat16 [512, 144, 384], P('dp', 'group'), may hold values from -12 to 12
- qkv_weight: float32 [384, 1152], P('dp', 'group'), may hold values from -0.3125 to 0.3125
- proj_weight: float32 [384, 384], P('dp', 'group'), may hold values from -1.75 to 1.75
- up_weight: float32 [384, 1536], P('dp', 'group'), may hold values from -0.3125 to 0.3125
- down_weight: float32 [1536, 384], P('dp', 'group'), may hold values from -0.15625 to 0.15625
- vectors: float32 [12, 384], replicated, may hold values from -0.9 to 1.45
- qkv_rows: float32 [384], P('dp'), may hold values from 20643.84 to 81100.8
- qkv_cols: float32 [1152], P('group'), may hold values from 20643.84 to 81100.8
- proj_rows: float32 [384], P('dp'), may hold values from 2949.12 to 11059.2
- proj_cols: float32 [384], P('group'), may hold values from 2949.12 to 11059.2
- up_rows: float32 [384], P('dp'), may hold values from 23592.96 to 95846.4
- up_cols: float32 [1536], P('group'), may hold values from 23592.96 to 95846.4
- down_rows: float32 [1536], P('dp'), may hold values from 22118.4 to 88473.6
- down_cols: float32 [384], P('group'), may hold values from 22118.4 to 88473.6
- vector_moment: float32 [12, 384], replicated, may hold values from 28016.64 to 110592
Outputs:
- block_output: bfloat16 [512, 144, 384], P('dp', 'group')
- input_grad: bfloat16 [512, 144, 384], P('dp', 'group')
- qkv_grad: float32 [384, 1152], P('dp', 'group')
- qkv_rows_new: float32 [384], P('dp')
- qkv_cols_new: float32 [1152], P('group')
- qkv_new: float32 [384, 1152], P('dp', 'group')
- proj_grad: float32 [384, 384], P('dp', 'group')
- proj_rows_new: float32 [384], P('dp')
- proj_cols_new: float32 [384], P('group')
- proj_new: float32 [384, 384], P('dp', 'group')
- up_grad: float32 [384, 1536], P('dp', 'group')
- up_rows_new: float32 [384], P('dp')
- up_cols_new: float32 [1536], P('group')
- up_new: float32 [384, 1536], P('dp', 'group')
- down_grad: float32 [1536, 384], P('dp', 'group')
- down_rows_new: float32 [1536], P('dp')
- down_cols_new: float32 [384], P('group')
- down_new: float32 [1536, 384], P('dp', 'group')
- vector_grad: float32 [12, 384], replicated
- vector_moment_new: float32 [12, 384], replicated
- vector_new: float32 [12, 384], replicated
Inputs may be any that keep to these rules, and one draw needn't show every extreme that they name: `keep_mask`: each image keeps its slot 0 and at least half of its 144 slots.
All inputs are finite; a program needn't handle non-finite values.
Results may differ from a plain program's by a relative error of at most 0.012.
Values may be sent and summed in bfloat16 or wider, within the bound.
No kernel may reach another device: no remote copies, remote signals or barrier semaphores. Data moves between devices by JAX's collectives and lax.ppermute only.
A program may use at most 192 MiB of HBM per device.

v0:
```python
import functools
import math

import jax
import jax.numpy as jnp
from jax import lax
from jax.experimental import pallas as pl
from jax.experimental.pallas import tpu as pltpu
from jax.sharding import PartitionSpec as P

HEAD_DIM = 64
STEP_NUMBER = 10


step_rate = 0.3
norm_epsilon = 1e-06
tiny_square = 1e-30
decay_rate = 1.0 - STEP_NUMBER ** (-0.8)
LOG2_E = 1.4426950408889634


def axis_bits(name):
    count = lax.axis_size(name)
    return [(name, 1 << place) for place in range(count.bit_length() - 1)]


def swap_partner(array, step):
    name, bit = step
    count = lax.axis_size(name)
    return lax.ppermute(array, name, [(rank, rank ^ bit) for rank in range(count)])


def upper_side(step):
    name, bit = step
    return (lax.axis_index(name) & bit) != 0


def gather_blocks(array, steps):
    for step in steps:
        arrived = swap_partner(array, step)
        upper = upper_side(step)
        array = jnp.stack([jnp.where(upper, arrived, array), jnp.where(upper, array, arrived)])
    return array


def scatter_sum(array, steps):
    for step in steps:
        upper = upper_side(step)
        leaving = jnp.where(upper, array[0], array[1]).astype(jnp.bfloat16)
        arrived = swap_partner(leaving, step)
        array = jnp.where(upper, array[1], array[0]).astype(jnp.float32) + arrived.astype(jnp.float32)
    return array


def sum_everywhere(array, steps):
    for step in steps:
        array = array + swap_partner(array, step)
    return array


def sum_parts(parts, steps):
    flat = [part.reshape(-1) for part in parts]
    total = sum_everywhere(jnp.concatenate(flat), steps)
    result, start = [], 0
    for part in parts:
        result.append(total[start : start + part.size].reshape(part.shape))
        start += part.size
    return result


def block_order(steps):
    order = []
    for name in ("dp", "group"):
        bits = sorted((step for step in steps if step[0] == name), key=lambda step: -step[1])
        order.append([steps.index(step) for step in bits])
    return order


def blocks_to_whole(blocks, steps):
    count = len(steps)
    rows, cols = blocks.shape[count:]
    dp_axes, group_axes = block_order(steps)
    dp_axes = [count - 1 - axis for axis in dp_axes]
    group_axes = [count - 1 - axis for axis in group_axes]
    whole = blocks.transpose(dp_axes + [count] + group_axes + [count + 1])
    return whole.reshape(rows << len(dp_axes), cols << len(group_axes))


def whole_to_blocks(whole, steps):
    dp_axes, group_axes = block_order(steps)
    rows = whole.shape[0] >> len(dp_axes)
    cols = whole.shape[1] >> len(group_axes)
    split = whole.reshape([2] * len(dp_axes) + [rows] + [2] * len(group_axes) + [cols])
    places = dp_axes + [len(steps)] + group_axes + [len(steps) + 1]
    return split.transpose([places.index(axis) for axis in range(len(places))])


PER_STEP = 4
FF_PER_STEP = 2
SLICE = 48
FF_CHUNK = 256
vmem_bytes = 60 * 1024 * 1024


def dot(left, right, left_axis=1, right_axis=0):
    return lax.dot_general(
        left, right, (((left_axis,), (right_axis,)), ((), ())), preferred_element_type=jnp.float32
    )


def normal_form(values):
    center = jnp.mean(values, axis=-1, keepdims=True)
    centered = values - center
    spread = jnp.mean(centered * centered, axis=-1, keepdims=True)
    scale = lax.rsqrt(spread + norm_epsilon)
    return centered * scale, scale


def norm_back(grad, unit, scale, gain):
    weighted = grad * gain
    along = jnp.mean(weighted * unit, axis=-1, keepdims=True)
    level = jnp.mean(weighted, axis=-1, keepdims=True)
    return scale * (weighted - level - unit * along)


def slices_of(count):
    return [slice(start, start + SLICE) for start in range(0, count, SLICE)]


def fold_rows(values):
    return jnp.sum(values.reshape(values.shape[0] // 8, 8, values.shape[1]), axis=0)


def column_sum(values):
    return jnp.sum(values, axis=0, keepdims=True)


def pair_mask(length):
    return lax.broadcasted_iota(jnp.int32, (length, 2 * HEAD_DIM), 1) < HEAD_DIM


def lane_tiles(count):
    return [slice(start, min(start + 128, count)) for start in range(0, count, 128)]


def stack_heads(pair, first):
    none = jnp.zeros_like(pair)
    return jnp.concatenate([jnp.where(first, pair, none), jnp.where(first, none, pair)], axis=0)


def join_heads(rows, first):
    length = rows.shape[0] // 2
    return jnp.where(first, rows[:length], rows[length:])


def gelu_and_slope(pre):
    bell = jnp.exp2(pre * pre * (-0.5 * LOG2_E))
    base = 1.0 + (0.3275911 * 0.5**0.5) * jnp.abs(pre)
    inverse = pl.reciprocal(base, approx=True)
    inverse = inverse * (2.0 - base * inverse)
    poly = inverse * (
        0.5 * 0.254829592
        + inverse
        * (
            0.5 * -0.284496736
            + inverse
            * (0.5 * 1.421413741 + inverse * (0.5 * -1.453152027 + inverse * (0.5 * 1.061405429)))
        )
    )
    tail = poly * bell
    below = jnp.where(pre >= 0, 1.0 - tail, tail)
    return pre * below, below + pre * bell * 0.3989422804014327


def widen(source_ref, wide_ref, images):
    tiles, total, lanes = wide_ref.shape
    rows_at_once = 8 * images

    @pl.loop(0, total // rows_at_once)
    def _(part):
        rows = pl.ds(pl.multiple_of(part * rows_at_once, rows_at_once), rows_at_once)
        for tile in range(tiles):
            cols = slice(tile * lanes, (tile + 1) * lanes)
            wide_ref[tile, rows, :] = source_ref[rows, cols].astype(jnp.float32)


def narrow(wide_ref, target_ref, images):
    tiles, total, lanes = wide_ref.shape
    rows_at_once = 8 * images

    @pl.loop(0, total // rows_at_once)
    def _(part):
        rows = pl.ds(pl.multiple_of(part * rows_at_once, rows_at_once), rows_at_once)
        for tile in range(tiles):
            cols = slice(tile * lanes, (tile + 1) * lanes)
            target_ref[rows, cols] = wide_ref[tile, rows, :].astype(target_ref.dtype)


def take_image(wide_ref, image, images):
    tiles, total, _ = wide_ref.shape
    rows = pl.ds(image, total // images, images)
    return jnp.concatenate([wide_ref[tile, rows, :] for tile in range(tiles)], axis=1)


def put_image(wide_ref, image, images, values):
    tiles, total, lanes = wide_ref.shape
    rows = pl.ds(image, total // images, images)
    for tile in range(tiles):
        wide_ref[tile, rows, :] = values[:, tile * lanes : (tile + 1) * lanes]


def attention_kernel(
    images, tokens_ref, bias_ref, w_qkv_ref, w_proj_ref, vectors_ref,
    x_ref, qkv_ref, probs_ref, attended_ref, middle_ref, wide_ref, normed_ref,
):
    @pl.when(pl.program_id(0) == 0)
    def _():
        widen(tokens_ref, wide_ref, images)
        to_image_rows(wide_ref, x_ref, images)

    attention_steps(
        x_ref, lambda image: bias_ref[image], w_qkv_ref, w_proj_ref, vectors_ref,
        qkv_ref, probs_ref, attended_ref, middle_ref, normed_ref,
    )


def to_image_rows(wide_ref, x_ref, images):
    length = wide_ref.shape[1] // images

    @pl.loop(0, images)
    def _(image):
        rows = pl.ds(pl.multiple_of(image * length, length), length)
        x_ref[rows, :] = take_image(wide_ref, image, images).astype(jnp.bfloat16)


def attention_steps(
    x_ref, bias_column, w_qkv_ref, w_proj_ref, vectors_ref,
    qkv_ref, probs_ref, attended_ref, middle_ref, normed_ref,
):
    per_step, _, length, _ = probs_ref.shape
    step_rows, width = middle_ref.shape
    base = 0 if x_ref.shape[0] == step_rows else pl.program_id(0) * step_rows

    for rows in slices_of(step_rows):
        x = x_ref[pl.ds(pl.multiple_of(base + rows.start, SLICE), SLICE), :].astype(jnp.float32)
        unit, _ = normal_form(x)
        normed_ref[rows, :] = (unit * vectors_ref[0:1] + vectors_ref[1:2]).astype(jnp.bfloat16)
    for part in range(3):
        cols = slice(part * width, (part + 1) * width)
        projected = dot(normed_ref[...], w_qkv_ref[:, cols])
        if part != 1:
            row = 2 if part == 0 else 3
            projected = projected + vectors_ref[row : row + 1]
        qkv_ref[:, cols] = projected.astype(jnp.bfloat16)

    pairs = width // (2 * HEAD_DIM)
    first = pair_mask(length)
    place = lax.broadcasted_iota(jnp.int32, (length, 2 * length), 0)
    asker = lax.broadcasted_iota(jnp.int32, (length, 2 * length), 1)
    own = place == jnp.where(asker >= length, asker - length, asker)

    def scores_of(image):
        rows = slice(image * length, (image + 1) * length)
        result = []
        for pair in range(pairs):
            low = pair * 2 * HEAD_DIM
            queries = stack_heads(qkv_ref[rows, low : low + 2 * HEAD_DIM], first)
            result.append(dot(qkv_ref[rows, width + low : width + low + 2 * HEAD_DIM], queries, 1, 1))
        return result

    next_scores = scores_of(0)
    for image in range(per_step):
        rows = slice(image * length, (image + 1) * length)
        all_scores = next_scores
        if image + 1 < per_step:
            next_scores = scores_of(image + 1)
        column = bias_column(image)
        for cols in lane_tiles(2 * length):
            bias = jnp.where(own[:, cols], 0.0, column)
            for pair in range(pairs):
                scores = all_scores[pair][:, cols] * (HEAD_DIM**-0.5 * LOG2_E) + bias
                weights = jnp.exp2(scores - jnp.max(scores, axis=0, keepdims=True))
                probs = weights * (1.0 / jnp.sum(weights, axis=0, keepdims=True))
                probs_ref[image, pair, :, cols] = probs.astype(jnp.bfloat16)
        for pair in range(pairs):
            low = pair * 2 * HEAD_DIM
            values = qkv_ref[rows, 2 * width + low : 2 * width + low + 2 * HEAD_DIM]
            attended = join_heads(dot(probs_ref[image, pair], values, 0, 0), first)
            attended_ref[rows, low : low + 2 * HEAD_DIM] = attended.astype(jnp.bfloat16)

    middle_ref[...] = (
        x_ref[pl.ds(pl.multiple_of(base, length), step_rows), :].astype(jnp.float32)
        + dot(attended_ref[...], w_proj_ref[...])
        + vectors_ref[4:5]
    )


def feed_forward_kernel(
    images, middle_ref, cotangent_ref, attended_ref, w_up_ref, w_down_ref, proj_t_ref, vectors_ref, bias_up_ref,
    output_ref, d_middle_ref, d_attended_ref, up_grad_ref, down_grad_ref, proj_grad_ref, vector_sums_ref, up_sums_ref,
    wide_ref, *scratches,
):
    up_total_ref, down_total_ref, proj_total_ref = scratches[-3:]

    @pl.when(pl.program_id(0) == 0)
    def _():
        widen(cotangent_ref, wide_ref, images)

    feed_forward_steps(
        images, middle_ref, attended_ref, w_up_ref, w_down_ref, proj_t_ref, vectors_ref, bias_up_ref,
        d_middle_ref, d_attended_ref, vector_sums_ref, up_sums_ref, wide_ref, *scratches,
    )

    @pl.when(pl.program_id(0) == pl.num_programs(0) - 1)
    def _():
        narrow(wide_ref, output_ref, images)
        up_grad_ref[...] = up_total_ref[...].astype(jnp.bfloat16)
        down_grad_ref[...] = down_total_ref[...].T.astype(jnp.bfloat16)
        proj_grad_ref[...] = proj_total_ref[...].astype(jnp.bfloat16)


def feed_forward_steps(
    images, middle_ref, attended_ref, w_up_ref, w_down_ref, proj_t_ref, vectors_ref, bias_up_ref,
    d_middle_ref, d_attended_ref, vector_sums_ref, up_sums_ref,
    wide_ref, normed_ref, normed_t_ref, dy_ref, dy_t_ref, unit_ref, scale_ref, ahead_ref, back_ref,
    up_t_ref, down_t_ref, up_total_ref, down_total_ref, proj_total_ref,
):
    step = pl.program_id(0)
    length = wide_ref.shape[1] // images
    hidden = w_up_ref.shape[1]
    per_step = middle_ref.shape[0] // length

    @pl.when(step == 0)
    def _():
        for total in (up_total_ref, down_total_ref, proj_total_ref, vector_sums_ref, up_sums_ref):
            total[...] = jnp.zeros_like(total)
        up_t_ref[...] = w_up_ref[...].T
        down_t_ref[...] = w_down_ref[...].T

    for image in range(per_step):
        rows = slice(image * length, (image + 1) * length)
        dy = take_image(wide_ref, step * per_step + image, images)
        dy_ref[rows, :] = dy.astype(jnp.bfloat16)
        vector_sums_ref[3:4] += column_sum(dy)
        unit, scale = normal_form(middle_ref[rows, :])
        unit_ref[rows, :] = unit
        scale_ref[rows, :] = jnp.broadcast_to(scale, (length, scale_ref.shape[1]))
        normed_ref[rows, :] = (unit * vectors_ref[5:6] + vectors_ref[6:7]).astype(jnp.bfloat16)
    normed_t_ref[...] = normed_ref[...].T
    dy_t_ref[...] = dy_ref[...].T
    chunks = hidden // FF_CHUNK

    def cols_of(chunk):
        return slice(chunk * FF_CHUNK, (chunk + 1) * FF_CHUNK)

    def into(chunk):
        cols = cols_of(chunk)
        pre = dot(normed_ref[...], w_up_ref[:, cols])
        return pre + bias_up_ref[:, cols], dot(dy_ref[...], down_t_ref[:, cols])

    def across(pre, d_active):
        active, slope = gelu_and_slope(pre)
        return active.astype(jnp.bfloat16), (d_active * slope).astype(jnp.bfloat16)

    def out_of(chunk, active, d_hidden):
        cols = cols_of(chunk)
        ahead, back = dot(active, w_down_ref[cols, :]), dot(d_hidden, up_t_ref[cols, :])
        if chunk == 0:
            ahead_ref[...] = ahead
            back_ref[...] = back
        else:
            ahead_ref[...] += ahead
            back_ref[...] += back
        down_total_ref[:, cols] += dot(dy_t_ref[...], active)
        up_total_ref[:, cols] += dot(normed_t_ref[...], d_hidden)
        up_sums_ref[:, cols] += column_sum(d_hidden.astype(jnp.float32))

    entered, crossed = into(0), None
    for chunk in range(chunks + 1):
        next_entered = into(chunk + 1) if chunk + 1 < chunks else None
        next_crossed = across(*entered) if chunk < chunks else None
        if crossed is not None:
            out_of(chunk - 1, *crossed)
        entered, crossed = next_entered, next_crossed

    for image in range(per_step):
        rows = slice(image * length, (image + 1) * length)
        output = middle_ref[rows, :] + ahead_ref[rows, :] + vectors_ref[11:12]
        put_image(wide_ref, step * per_step + image, images, output)
        unit = unit_ref[rows, :]
        grad = back_ref[rows, :]
        vector_sums_ref[1:2] += column_sum(grad * unit)
        vector_sums_ref[2:3] += column_sum(grad)
        d_middle = dy_ref[rows, :].astype(jnp.float32) + norm_back(
            grad, unit, scale_ref[rows, 0:1], vectors_ref[5:6]
        )
        d_middle_ref[rows, :] = d_middle
        d_branch = d_middle.astype(jnp.bfloat16)
        dy_ref[rows, :] = d_branch
        vector_sums_ref[0:1] += column_sum(d_branch.astype(jnp.float32))
    proj_total_ref[...] += dot(attended_ref[...], dy_ref[...], 0, 0)
    d_attended_ref[...] = dot(dy_ref[...], proj_t_ref[...]).astype(jnp.bfloat16)


def attention_back_kernel(
    images, x_ref, qkv_ref, probs_ref, d_attended_ref, d_middle_ref, qkv_t_ref, vectors_ref,
    input_grad_ref, qkv_grad_ref, vector_sums_ref, wide_ref, normed_ref, d_projected_ref, back_ref, qkv_total_ref,
):
    @pl.when(pl.program_id(0) == 0)
    def _():
        qkv_total_ref[...] = jnp.zeros_like(qkv_total_ref)
        vector_sums_ref[...] = jnp.zeros_like(vector_sums_ref)

    def put(image, rows, values):
        put_image(wide_ref, image, images, values)

    attention_back_steps(
        x_ref, qkv_ref, probs_ref, d_attended_ref, vectors_ref, vector_sums_ref, normed_ref, d_projected_ref, qkv_total_ref
    )
    input_back_steps(
        put, probs_ref.shape[2], x_ref, d_projected_ref, d_middle_ref, qkv_t_ref, vectors_ref, vector_sums_ref, back_ref
    )

    @pl.when(pl.program_id(0) == pl.num_programs(0) - 1)
    def _():
        narrow(wide_ref, input_grad_ref, images)
        qkv_grad_ref[...] = qkv_total_ref[...].astype(jnp.bfloat16)


def attention_back_steps(
    x_ref, qkv_ref, probs_ref, d_attended_ref, vectors_ref, vector_sums_ref, normed_ref, d_projected_ref, qkv_total_ref
):
    width = x_ref.shape[1]
    length = probs_ref.shape[2]
    per_step = probs_ref.shape[0]

    pairs = width // (2 * HEAD_DIM)
    first = pair_mask(length)
    scale = HEAD_DIM**-0.5

    def places(image, pair):
        low = pair * 2 * HEAD_DIM
        rows = slice(image * length, (image + 1) * length)
        return rows, [slice(part * width + low, part * width + low + 2 * HEAD_DIM) for part in range(3)]

    def entering(image):
        result = []
        for pair in range(pairs):
            rows, cols = places(image, pair)
            d_attended = stack_heads(d_attended_ref[rows, cols[0]], first)
            d_values = dot(probs_ref[image, pair], d_attended)
            d_projected_ref[rows, cols[2]] = d_values.astype(jnp.bfloat16)
            result.append(dot(qkv_ref[rows, cols[2]], d_attended, 1, 1))
        return result

    next_probs = entering(0)
    for image in range(per_step):
        all_d_probs = next_probs
        if image + 1 < per_step:
            next_probs = entering(image + 1)
        all_d_scores = []
        for pair in range(pairs):
            parts = []
            for cols in lane_tiles(2 * length):
                probs, d_probs = probs_ref[image, pair, :, cols].astype(jnp.float32), all_d_probs[pair][:, cols]
                along = jnp.sum(d_probs * probs, axis=0, keepdims=True)
                parts.append((probs * (d_probs - along)).astype(jnp.bfloat16))
            all_d_scores.append(jnp.concatenate(parts, axis=1))
        for pair in range(pairs):
            rows, cols = places(image, pair)
            d_scores = all_d_scores[pair]
            queries = stack_heads(qkv_ref[rows, cols[0]], first)
            d_queries = join_heads(dot(d_scores, qkv_ref[rows, cols[1]], 0, 0), first) * scale
            d_projected_ref[rows, cols[0]] = d_queries.astype(jnp.bfloat16)
            d_projected_ref[rows, cols[1]] = (dot(d_scores, queries) * scale).astype(jnp.bfloat16)

    query_sums = value_sums = jnp.zeros((8, width), jnp.float32)
    for rows in slices_of(x_ref.shape[0]):
        query_sums += fold_rows(d_projected_ref[rows, :width].astype(jnp.float32))
        value_sums += fold_rows(d_projected_ref[rows, 2 * width :].astype(jnp.float32))
        unit, _ = normal_form(x_ref[rows, :].astype(jnp.float32))
        normed_ref[rows, :] = (unit * vectors_ref[0:1] + vectors_ref[1:2]).astype(jnp.bfloat16)
    vector_sums_ref[2:3] += column_sum(query_sums)
    vector_sums_ref[3:4] += column_sum(value_sums)
    qkv_total_ref[...] += dot(normed_ref[...], d_projected_ref[...], 0, 0)


def input_back_steps(
    put, length, x_ref, d_projected_ref, d_middle_ref, qkv_t_ref, vectors_ref, vector_sums_ref, back_ref
):
    step = pl.program_id(0)
    per_step = x_ref.shape[0] // length
    back_ref[...] = dot(d_projected_ref[...], qkv_t_ref[...])
    gain_sums = shift_sums = jnp.zeros((8, x_ref.shape[1]), jnp.float32)
    for rows in slices_of(x_ref.shape[0]):
        unit, scale = normal_form(x_ref[rows, :].astype(jnp.float32))
        grad = back_ref[rows, :]
        gain_sums += fold_rows(grad * unit)
        shift_sums += fold_rows(grad)
        back_ref[rows, :] = d_middle_ref[rows, :] + norm_back(grad, unit, scale, vectors_ref[0:1])
    vector_sums_ref[0:1] += column_sum(gain_sums)
    vector_sums_ref[1:2] += column_sum(shift_sums)
    for image in range(per_step):
        rows = slice(image * length, (image + 1) * length)
        put(step * per_step + image, rows, back_ref[rows, :])


def whole_block(shape):
    return pl.BlockSpec(shape, lambda step: (0,) * len(shape))


def step_block(shape, first=0):
    return pl.BlockSpec(shape, lambda step: (first + step,) + (0,) * (len(shape) - 1))


def scratch(*shape, dtype=jnp.float32):
    return pltpu.VMEM(shape, dtype)


def call_kernel(kernel, statics, steps, ins, outs, scratches, operands, flops, transcendentals=0, first_step=0, aliases={}):
    in_specs = [
        pl.BlockSpec(memory_space=pltpu.SMEM)
        if block == "place"
        else pl.BlockSpec(memory_space=pl.ANY)
        if block == "await"
        else whole_block(op.shape) if block is None else step_block(block, first_step)
        for op, block in zip(operands, ins)
    ]
    out_specs = [
        whole_block(shape) if block is None else step_block(block, first_step) for shape, dtype, block in outs
    ]
    moved = sum(op.size * op.dtype.itemsize for op in operands) + sum(
        math.prod(shape) * jnp.dtype(dtype).itemsize for shape, dtype, block in outs
    )
    return pl.pallas_call(
        functools.partial(kernel, *statics),
        grid=(steps,),
        in_specs=in_specs,
        out_specs=out_specs,
        out_shape=[jax.ShapeDtypeStruct(shape, dtype) for shape, dtype, block in outs],
        scratch_shapes=scratches,
        input_output_aliases=aliases,
        compiler_params=pltpu.CompilerParams(vmem_limit_bytes=vmem_bytes),
        cost_estimate=pl.CostEstimate(
            flops=flops * 8, bytes_accessed=moved, transcendentals=transcendentals
        ),
    )(*operands)


def attention_forward(tokens, bias, w_qkv, w_proj, vectors):
    images, length, _ = bias.shape
    total, width = tokens.shape
    pairs = width // (2 * HEAD_DIM)
    rows = PER_STEP * length
    low, high = jnp.bfloat16, jnp.float32
    outs = [
        ((total, width), low, None),
        ((total, 3 * width), low, (rows, 3 * width)),
        ((images, pairs, length, 2 * length), low, (PER_STEP, pairs, length, 2 * length)),
        ((total, width), low, (rows, width)),
        ((total, width), high, (rows, width)),
    ]
    return call_kernel(
        attention_kernel, (images,), images // PER_STEP,
        [None, (PER_STEP, length, 1), None, None, None], outs,
        [scratch(width // 128, total, 128), scratch(rows, width, dtype=low)],
        (tokens, bias, w_qkv, w_proj, vectors),
        2 * total * width * 4 * width + 8 * total * length * width,
    )


def feed_forward(images, middle, cotangent, attended, w_up, w_down, w_proj, vectors):
    total, width = middle.shape
    hidden = w_up.shape[1]
    rows = total // images * FF_PER_STEP
    low, high = jnp.bfloat16, jnp.float32
    block = (rows, width)
    outs = [
        ((total, width), low, None),
        ((total, width), high, block),
        ((total, width), low, block),
        ((width, hidden), low, None),
        ((hidden, width), low, None),
        ((width, width), low, None),
        ((8, width), high, None),
        ((1, hidden), high, None),
    ]
    scratches = [
        scratch(width // 128, total, 128),
        scratch(rows, width, dtype=low),
        scratch(width, rows, dtype=low),
        scratch(rows, width, dtype=low),
        scratch(width, rows, dtype=low),
        scratch(rows, width),
        scratch(rows, 128),
        scratch(rows, width),
        scratch(rows, width),
        scratch(hidden, width, dtype=low),
        scratch(width, hidden, dtype=low),
        scratch(width, hidden),
        scratch(width, hidden),
        scratch(width, width),
    ]
    return call_kernel(
        feed_forward_kernel, (images,), images // FF_PER_STEP,
        [block, None, block, None, None, None, None, None], outs, scratches,
        (middle, cotangent, attended, w_up, w_down, w_proj.T, vectors, vectors[7:11].reshape(1, hidden)),
        12 * total * width * hidden + 4 * total * width * width, total * hidden,
    )


def attention_back(x, qkv, probs, d_attended, d_middle, w_qkv, vectors):
    images, pairs, length, _ = probs.shape
    total, width = x.shape
    rows = PER_STEP * length
    low, high = jnp.bfloat16, jnp.float32
    block = (rows, width)
    outs = [
        ((total, width), low, None),
        ((width, 3 * width), low, None),
        ((8, width), high, None),
    ]
    scratches = [
        scratch(width // 128, total, 128),
        scratch(rows, width, dtype=low),
        scratch(rows, 3 * width, dtype=low),
        scratch(rows, width),
        scratch(width, 3 * width),
    ]
    return call_kernel(
        attention_back_kernel, (images,), images // PER_STEP,
        [block, (rows, 3 * width), (PER_STEP, pairs, length, 2 * length), block, block, None, None],
        outs, scratches, (x, qkv, probs, d_attended, d_middle, w_qkv.T, vectors),
        4 * total * width * 3 * width + 16 * total * length * width,
    )

def linear_place():
    return lax.axis_index("dp") * lax.axis_size("group") + lax.axis_index("group")


def permute(array, mask):
    count = lax.axis_size("dp") * lax.axis_size("group")
    return lax.ppermute(array, ("dp", "group"), [(rank, rank ^ mask) for rank in range(count)])


def direct_masks(bits):
    masks = [0]
    for bit in bits:
        masks = masks + [mask | bit for mask in masks]
    return masks[1:]


def add_wide(first, *rest):
    total = first.astype(jnp.float32)
    for part in rest:
        total = total + part.astype(jnp.float32)
    return total


def packed_place(mask, spread, count):
    return ((mask >> 1) & (spread - 1)) * (count // (2 * spread)) + (mask >> (spread.bit_length()))


def scatter_step(held, bits):
    masks = direct_masks(bits)
    size = held.shape[0] // (len(masks) + 1)
    parts = [
        permute(held[size * (at + 1) : size * (at + 2)].astype(jnp.bfloat16), mask)
        for at, mask in enumerate(masks)
    ]
    return held[:size], parts


def add_wide(first, *rest):
    total = first.astype(jnp.float32)
    for part in rest:
        total = total + part.astype(jnp.float32)
    return total


def packed_place(mask, spread, count):
    return ((mask >> 1) & (spread - 1)) * (count // (2 * spread)) + (mask >> (spread.bit_length()))


def gather_step(held, bits):
    return held + [permute(part, mask) for mask in direct_masks(bits) for part in held]


def gathered_place(mask, count):
    return (mask & 1) * (count // 2) + ((mask >> 2) & 1) * (count // 4) + (mask >> 3) * 2 + ((mask >> 1) & 1)


def unpack(place_ref, block_refs, packed_ref, put, dp_size, spread):
    place = place_ref[0]
    size = block_refs[0].shape[0]
    for at, block_ref in enumerate(block_refs):
        packed_ref[at * size : (at + 1) * size] = block_ref[...]
    count = dp_size * spread
    for row in range(dp_size):
        for col in range(spread):
            put(row, col, packed_ref[gathered_place((row * spread + col) ^ place, count)])


def pack(place_ref, take, keep_ref, leave_ref, dp_size, spread):
    place = place_ref[0]
    odd = (place & 1) == 1
    for row in range(dp_size):
        for col in range(0, spread, 2):
            at = packed_place((row * spread + col) ^ place, spread, dp_size * spread)
            even_block, odd_block = take(row, col), take(row, col + 1)
            keep_ref[at] = jnp.where(odd, odd_block, even_block)
            leave_ref[at] = jnp.where(odd, even_block, odd_block)


def narrow_pieces(place_ref, wide_ref, piece_refs, spread):
    tiles, _, lanes = wide_ref.shape
    rows_of_piece = piece_refs[0].shape[0]
    step = 64
    group = place_ref[0] & (spread - 1)
    for relative, piece_ref in enumerate(piece_refs):
        base = (group ^ relative) * rows_of_piece

        @pl.loop(0, rows_of_piece // step)
        def _(part):
            target = pl.ds(pl.multiple_of(part * step, step), step)
            source = pl.ds(pl.multiple_of(base + part * step, step), step)
            for tile in range(tiles):
                cols = slice(tile * lanes, (tile + 1) * lanes)
                piece_ref[target, cols] = wide_ref[tile, source, :].astype(jnp.bfloat16)


def general_body(
    tokens,
    keep_mask,
    cotangent,
    qkv_weight,
    proj_weight,
    up_weight,
    down_weight,
    vectors,
    qkv_rows,
    qkv_cols,
    proj_rows,
    proj_cols,
    up_rows,
    up_cols,
    down_rows,
    down_cols,
    vector_moment,
):
    masters = (qkv_weight, proj_weight, up_weight, down_weight)
    lowered = tuple((master.astype(jnp.bfloat16) for master in masters))
    dp_bits, group_bits = axis_bits("dp"), axis_bits("group")
    gather_steps = dp_bits[1:] + group_bits[1:] + dp_bits[:1] + group_bits[:1]
    scatter_steps = gather_steps[::-1]
    w_qkv, w_proj, w_up, w_down = tuple(
        blocks_to_whole(gather_blocks(part, gather_steps), gather_steps) for part in lowered
    )
    spread = lax.axis_size("group")

    def slots_in(array):
        held, slots, width = array.shape
        parts = array.transpose(1, 0, 2).reshape(slots, spread, held // spread, width)
        parts = lax.all_to_all(
            parts.transpose(1, 0, 2, 3), "group", split_axis=0, concat_axis=0, tiled=True
        )
        return parts.reshape(spread * slots * (held // spread), width)

    def slots_out(array):
        held, slots, width = tokens.shape
        parts = array.reshape(spread, slots, held // spread, width)
        parts = lax.all_to_all(parts, "group", split_axis=0, concat_axis=0, tiled=True)
        return parts.transpose(1, 0, 2, 3).reshape(slots, held, width).transpose(1, 0, 2)

    images = keep_mask.shape[0]
    bias = jnp.where(keep_mask > 0, 0.0, -1e30)[:, :, None]
    x, qkv, probs, attended, middle = attention_forward(
        slots_in(tokens), bias, w_qkv, w_proj, vectors
    )
    output, d_middle, d_attended, up_grad, down_grad, proj_grad, ff_sums, up_sums = feed_forward(
        images, middle, slots_in(cotangent), attended, w_up, w_down, w_proj, vectors
    )
    block_output = slots_out(output)
    d_input, qkv_grad, att_sums = attention_back(
        x, qkv, probs, d_attended, d_middle, w_qkv, vectors
    )
    input_grad = slots_out(d_input)
    local_vectors = jnp.concatenate(
        [att_sums[:4], ff_sums[:3], up_sums.reshape(4, -1), ff_sums[3:4]], axis=0
    )
    vector_grad = sum_everywhere(local_vectors, group_bits + dp_bits)
    local_grads = (qkv_grad, proj_grad, up_grad, down_grad)
    owned = tuple(
        scatter_sum(whole_to_blocks(part, scatter_steps), scatter_steps) for part in local_grads
    )
    squares = tuple((gradient * gradient + tiny_square for gradient in owned))
    row_parts = tuple((jnp.sum(square, axis=1) for square in squares)) + tuple(
        (jnp.sum(master * master, axis=1) for master in masters)
    )
    row_sums = sum_parts(row_parts, group_bits)
    rows_old = (qkv_rows, proj_rows, up_rows, down_rows)
    cols_old = (qkv_cols, proj_cols, up_cols, down_cols)
    total_cols = tuple((gradient.shape[1] * lax.axis_size("group") for gradient in owned))
    total_rows = tuple((gradient.shape[0] * lax.axis_size("dp") for gradient in owned))
    rows_new = tuple(
        (
            decay_rate * rows_old[which] + (1.0 - decay_rate) * row_sums[which] / total_cols[which]
            for which in range(4)
        )
    )
    col_parts = (
        tuple((jnp.sum(square, axis=0) for square in squares))
        + tuple((jnp.sum(row_stat) for row_stat in rows_new))
        + tuple((jnp.sum(row_sums[4 + which]) for which in range(4)))
    )
    col_sums = sum_parts(col_parts, dp_bits)
    results = []
    for which in range(4):
        cols_new = (
            decay_rate * cols_old[which] + (1.0 - decay_rate) * col_sums[which] / total_rows[which]
        )
        mean_rows = col_sums[4 + which] / total_rows[which]
        spread = jnp.sqrt(col_sums[8 + which] / (total_rows[which] * total_cols[which]))
        second = rows_new[which][:, None] * cols_new[None, :] / mean_rows
        updated = masters[which] - step_rate * spread * owned[which] * lax.rsqrt(second)
        results.append((owned[which], rows_new[which], cols_new, updated))
    vector_moment_new = decay_rate * vector_moment + (1.0 - decay_rate) * (
        vector_grad * vector_grad + tiny_square
    )
    row_spread = jnp.sqrt(jnp.mean(vectors * vectors, axis=1, keepdims=True))
    vector_new = vectors - step_rate * row_spread * vector_grad * lax.rsqrt(vector_moment_new)
    return (
        block_output,
        input_grad,
        results[0][0],
        results[0][1],
        results[0][2],
        results[0][3],
        results[1][0],
        results[1][1],
        results[1][2],
        results[1][3],
        results[2][0],
        results[2][1],
        results[2][2],
        results[2][3],
        results[3][0],
        results[3][1],
        results[3][2],
        results[3][3],
        vector_grad,
        vector_moment_new,
        vector_new,
    )


def first_attention_kernel(images, dp_size, spread, place_ref, tokens_ref, *refs):
    blocks, refs = refs[:4], refs[4:]
    keep_ref, vectors_ref, *outs, x_ref, w_qkv_ref, w_proj_ref, qkv_t_ref, proj_t_ref = refs[:-4]
    packed_ref, wide_ref, bias_ref, normed_ref = refs[-4:]
    rows = packed_ref.shape[1]
    qkv_cols, proj_cols = w_qkv_ref.shape[1] // spread, w_proj_ref.shape[1] // spread

    @pl.when(pl.program_id(0) == 0)
    def _():
        widen(tokens_ref, wide_ref, images)
        to_image_rows(wide_ref, x_ref, images)

        def put(row, col, block):
            down = slice(row * rows, (row + 1) * rows)
            w_qkv_ref[down, col * qkv_cols : (col + 1) * qkv_cols] = block[:, :qkv_cols]
            w_proj_ref[down, col * proj_cols : (col + 1) * proj_cols] = block[:, qkv_cols:]

        unpack(place_ref, blocks, packed_ref, put, dp_size, spread)
        qkv_t_ref[...] = w_qkv_ref[...].T
        proj_t_ref[...] = w_proj_ref[...].T

    attention_part(0, x_ref, keep_ref, w_qkv_ref, w_proj_ref, vectors_ref, *outs, bias_ref, normed_ref)


def next_attention_kernel(start, x_ref, keep_ref, w_qkv_ref, w_proj_ref, vectors_ref, *refs):
    attention_part(start, x_ref, keep_ref, w_qkv_ref, w_proj_ref, vectors_ref, *refs[-6:])


def attention_part(
    start, x_ref, keep_ref, w_qkv_ref, w_proj_ref, vectors_ref,
    qkv_ref, probs_ref, attended_ref, middle_ref, bias_ref, normed_ref,
):
    @pl.when(pl.program_id(0) == 0)
    def _():
        bias_ref[...] = jnp.where(keep_ref[...] > 0, 0.0, -1e30).T

    def bias_column(image):
        here = start + pl.program_id(0) * probs_ref.shape[0] + image
        lane = lax.broadcasted_iota(jnp.int32, bias_ref.shape, 1)
        return row_sum(jnp.where(lane == here, bias_ref[...], 0.0))

    attention_steps(
        x_ref, bias_column, w_qkv_ref, w_proj_ref, vectors_ref,
        qkv_ref, probs_ref, attended_ref, middle_ref, normed_ref,
    )


def feed_forward_packed_kernel(images, dp_size, spread, place_ref, *refs):
    cotangent_ref, blocks, refs = refs[0], refs[1:5], refs[5:]
    middle_ref, attended_ref, proj_t_ref, vectors_ref = refs[:4]
    outputs, refs = refs[4 : 4 + spread], refs[4 + spread :]
    d_middle_ref, d_attended_ref, keep_ref, leave_ref, proj_total_ref, vector_sums_ref, up_sums_ref = refs[:7]
    w_up_ref, w_down_ref, down_low_ref, packed_ref, bias_up_ref, wide_ref = refs[7:13]
    scratches = refs[13:]
    width = w_up_ref.shape[0]
    up_total_ref, down_total_ref = scratches[-2:]
    rows = packed_ref.shape[1]
    up_cols = w_up_ref.shape[1] // spread
    out_cols = w_down_ref.shape[1] // spread
    folds = w_down_ref.shape[0] // w_up_ref.shape[0]

    @pl.when(pl.program_id(0) == 0)
    def _():
        widen(cotangent_ref, wide_ref, images)
        for fold in range(bias_up_ref.shape[1] // width):
            bias_up_ref[:, fold * width : (fold + 1) * width] = vectors_ref[7 + fold : 8 + fold]

        def put(row, col, block):
            w_up_ref[row * rows : (row + 1) * rows, col * up_cols : (col + 1) * up_cols] = block[:, :up_cols]
            for fold in range(folds):
                down = (row * folds + fold) * rows
                start = up_cols + fold * out_cols
                w_down_ref[down : down + rows, col * out_cols : (col + 1) * out_cols] = block[
                    :, start : start + out_cols
                ]

        unpack(place_ref, blocks, packed_ref, put, dp_size, spread)

    feed_forward_steps(
        images, middle_ref, attended_ref, w_up_ref, w_down_ref, proj_t_ref, vectors_ref, bias_up_ref,
        d_middle_ref, d_attended_ref, vector_sums_ref, up_sums_ref, wide_ref, *scratches, proj_total_ref,
    )

    @pl.when(pl.program_id(0) == pl.num_programs(0) - 1)
    def _():
        narrow_pieces(place_ref, wide_ref, outputs, spread)
        down_low_ref[...] = down_total_ref[...].T.astype(jnp.bfloat16)

        def take(row, col):
            across = slice(row * rows, (row + 1) * rows)
            cols = slice(col * out_cols, (col + 1) * out_cols)
            parts = [up_total_ref[across, col * up_cols : (col + 1) * up_cols].astype(jnp.bfloat16)]
            for fold in range(folds):
                down = (row * folds + fold) * rows
                parts.append(down_low_ref[down : down + rows, cols])
            return jnp.concatenate(parts, axis=1)

        pack(place_ref, take, keep_ref, leave_ref, dp_size, spread)


def attention_back_packed_kernel(
    dp_size, spread, place_ref, x_ref, qkv_ref, probs_ref, d_attended_ref, vectors_ref, proj_total_ref, _,
    d_projected_ref, keep_ref, leave_ref, vector_sums_ref, normed_ref, total_ref,
):
    @pl.when(pl.program_id(0) == 0)
    def _():
        total_ref[...] = jnp.zeros_like(total_ref)
        vector_sums_ref[...] = jnp.zeros_like(vector_sums_ref)

    attention_back_steps(
        x_ref, qkv_ref, probs_ref, d_attended_ref, vectors_ref, vector_sums_ref, normed_ref, d_projected_ref, total_ref
    )

    @pl.when(pl.program_id(0) == pl.num_programs(0) - 1)
    def _():
        rows = keep_ref.shape[1]
        qkv_cols, proj_cols = total_ref.shape[1] // spread, proj_total_ref.shape[1] // spread

        def take(row, col):
            down = slice(row * rows, (row + 1) * rows)
            parts = [
                total_ref[down, col * qkv_cols : (col + 1) * qkv_cols],
                proj_total_ref[down, col * proj_cols : (col + 1) * proj_cols],
            ]
            return jnp.concatenate(parts, axis=1).astype(jnp.bfloat16)

        pack(place_ref, take, keep_ref, leave_ref, dp_size, spread)


def first_input_kernel(
    length, x_ref, d_projected_ref, d_middle_ref, qkv_t_ref, vectors_ref, before_ref, *refs
):
    d_input_ref, vector_sums_ref, back_ref = refs[-3:]

    @pl.when(pl.program_id(0) == 0)
    def _():
        vector_sums_ref[...] = before_ref[...]

    def put(image, rows, values):
        d_input_ref[rows, :] = values.astype(jnp.bfloat16)

    input_back_steps(
        put, length, x_ref, d_projected_ref, d_middle_ref, qkv_t_ref, vectors_ref, vector_sums_ref, back_ref
    )


def last_input_kernel(
    images, spread, length, first, place_ref, x_ref, d_projected_ref, d_middle_ref, qkv_t_ref, vectors_ref, before_ref,
    d_input_ref, _, *refs,
):
    pieces, (vector_sums_ref, wide_ref, back_ref) = refs[:spread], refs[spread:]

    @pl.when(pl.program_id(0) == 0)
    def _():
        vector_sums_ref[...] = before_ref[...]
        for image in range(first):
            rows = slice(image * length, (image + 1) * length)
            put_image(wide_ref, image, images, d_input_ref[rows, :].astype(jnp.float32))

    def put(image, rows, values):
        put_image(wide_ref, first + image, images, values)

    input_back_steps(
        put, length, x_ref, d_projected_ref, d_middle_ref, qkv_t_ref, vectors_ref, vector_sums_ref, back_ref
    )

    @pl.when(pl.program_id(0) == pl.num_programs(0) - 1)
    def _():
        narrow_pieces(place_ref, wide_ref, pieces, spread)


def cut(array_ref, parts_ref):
    count = parts_ref.shape[2]
    for member in range(parts_ref.shape[0]):
        parts_ref[member] = array_ref[:, member * count : (member + 1) * count, :]


def pack_kernel(qkv_ref, proj_ref, up_ref, down_ref, pack_ref):
    rows, start = pack_ref.shape[0], 0
    parts = [qkv_ref[...], proj_ref[...], up_ref[...]]
    parts += [down_ref[fold * rows : (fold + 1) * rows, :] for fold in range(down_ref.shape[0] // rows)]
    for part in parts:
        pack_ref[:, start : start + part.shape[1]] = part.astype(jnp.bfloat16)
        start += part.shape[1]


def token_kernel(array_ref, own_ref, arrived_ref, _, parts_ref, first_ref, second_ref):
    start = first_ref.shape[2]
    for at, pack_ref in enumerate((own_ref, arrived_ref)):
        first_ref[at] = pack_ref[:, :start]
        second_ref[at] = pack_ref[:, start:]
    cut(array_ref, parts_ref)


def join_kernel(count, *refs):
    size = refs[0].shape[0]
    for at, part_ref in enumerate(refs[:count]):
        refs[-1][at * size : (at + 1) * size] = part_ref[...]


def settle_kernel(spread, place_ref, *refs):
    lists, (output_ref, token_ref) = refs[:-2], refs[-2:]
    token_ref[...] = jnp.zeros_like(token_ref)
    group = place_ref[0] & (spread - 1)
    count = lists[0].shape[1]
    share = len(lists) // spread * count
    for at, piece_ref in enumerate(lists):
        relative, part = at % spread, at // spread
        start = pl.multiple_of((group ^ relative) * share + part * count, count)
        output_ref[:, pl.ds(start, count), :] = piece_ref[...]


def lane_table(rows, columns):
    lane = lax.broadcasted_iota(jnp.int32, (rows, 128), 1)
    table = jnp.zeros((rows, 128), jnp.float32)
    for at, column in enumerate(columns):
        table = jnp.where(lane == at, column, table)
    return table


def added(parts):
    while len(parts) > 1:
        parts = [sum(parts[at : at + 2][1:], parts[at]) for at in range(0, len(parts), 2)]
    return parts[0]


def row_sum(values):
    return jnp.sum(values, axis=1, keepdims=True)


def after_kernel(*refs):
    pass


def add_kernel(count, keep_ref, arrived_ref, *refs):
    parts = refs[-count:]
    size = parts[0].shape[0]
    for at, part_ref in enumerate(parts):
        rows = slice(at * size, (at + 1) * size)
        total = keep_ref[rows].astype(jnp.float32) + arrived_ref[rows].astype(jnp.float32)
        part_ref[...] = total.astype(part_ref.dtype)


def gradient_kernel(count, *refs):
    block_parts, sums, refs = refs[:count], refs[count : count + 3], refs[count + 3 :]
    masters, rows_old, refs = refs[:4], refs[4:8], refs[8:]
    grads, (row_ref, message_ref) = refs[:4], refs[4:]
    blocks = added([part[0].astype(jnp.float32) for part in block_parts])
    rows, up_cols = grads[2].shape
    qkv_cols, out_cols = grads[0].shape[1], grads[1].shape[1]
    folds = grads[3].shape[0] // rows
    up = blocks[:, :up_cols]
    downs = [blocks[:, up_cols + fold * out_cols :][:, :out_cols] for fold in range(folds)]
    start = up_cols + folds * out_cols
    qkv = blocks[:, start : start + qkv_cols]
    proj = blocks[:, start + qkv_cols :]
    grads[0][...] = qkv
    grads[1][...] = proj
    grads[2][...] = up
    for fold in range(folds):
        grads[3][fold * rows : (fold + 1) * rows, :] = downs[fold]
    squares = [part * part + tiny_square for part in (qkv, proj, up, *downs)]
    row_ref[...] = lane_table(rows, [row_sum(square) for square in squares]).T[: row_ref.shape[0], :]
    width = message_ref.shape[1]
    message_ref[...] = jnp.zeros_like(message_ref)
    for at, square in enumerate((*squares[:3], added(squares[3:]))):
        message_ref[at : at + 1, : square.shape[1]] = column_sum(square)
    scalars = [column_sum(row_sum(master[...] * master[...])) for master in masters]
    scalars += [row_sum(part[...].reshape(1, part.shape[0])) for part in rows_old]
    message_ref[4:5, :128] = lane_table(1, scalars)
    att_ref, ff_ref, up_ref = sums
    count = up_ref.shape[1] // width
    message_ref[8:12, :] = att_ref[:4]
    message_ref[12:15, :] = ff_ref[:3]
    for at in range(count):
        message_ref[15 + at : 16 + at, :] = up_ref[:, at * width : (at + 1) * width]
    message_ref[15 + count : 16 + count, :] = ff_ref[3:4]


def column_kernel(row_ref, *refs):
    parts, (cols_ref, message_ref) = refs[:-3], refs[-2:]
    total = added([part[...] for part in parts])
    cols_ref[...] = total[:8]
    width = total.shape[1]
    rows = row_ref.shape[1]
    message_ref[...] = jnp.zeros_like(message_ref)
    message_ref[:8, :rows] = row_ref[...]
    columns = [row_sum(total[which : which + 1]) for which in range(4)]
    squares = [total[4:5, which : which + 1] for which in range(4)]
    message_ref[8:9, :] = lane_table(1, columns + squares)
    for tile in range(width // 128):
        message_ref[16 * (tile + 1) : 16 * (tile + 2), :] = total[8:, tile * 128 : (tile + 1) * 128]


def update_kernel(count, heights, widths, *refs):
    messages, refs = refs[:count], refs[count:]
    cols_ref, vectors_ref, moment_ref, refs = refs[0], refs[1], refs[2], refs[3:]
    grads, masters, rows_old, cols_old, refs = refs[:4], refs[4:8], refs[8:12], refs[12:16], refs[17:]
    news, cols_new, rows_out, refs = refs[:4], refs[4:8], refs[8:12], refs[12:]
    vector_grad_ref, moment_new_ref, vector_new_ref = refs
    sums = added([message[...] for message in messages])
    height = grads[0].shape[0]
    folds = grads[3].shape[0] // height
    lanes = [[0], [1], [2], list(range(3, 3 + folds))]
    share = 1.0 - decay_rate
    for which in range(4):
        entries = heights[which] * widths[which]
        cols = cols_old[which].shape[0]
        new = decay_rate * cols_old[which][...].reshape(1, cols) + share / heights[which] * cols_ref[
            which : which + 1, :cols
        ]
        cols_new[which][...] = new[0]
        old_total = cols_ref[4:5, 4 + which : 5 + which]
        mean_rows = (decay_rate * old_total + share / widths[which] * sums[8:9, which : which + 1]) / heights[which]
        rate = step_rate * jnp.sqrt(sums[8:9, 4 + which : 5 + which] / entries)
        across = new / mean_rows
        old = rows_old[which][...].reshape(1, len(lanes[which]) * height)
        row_sums = jnp.concatenate([sums[lane : lane + 1, :height] for lane in lanes[which]], axis=1)
        row = decay_rate * old + share / widths[which] * row_sums
        rows_out[which][...] = row[0]
        for fold in range(len(lanes[which])):
            part = slice(fold * height, (fold + 1) * height)
            column = jnp.broadcast_to(row[:, part], (8, height)).T[:, :1]
            news[which][part, :] = masters[which][part, :] - rate * grads[which][part, :] * lax.rsqrt(column * across)
    vectors = vectors_ref[...]
    count = vectors.shape[0]
    gradient = jnp.concatenate(
        [sums[16 * (tile + 1) : 16 * (tile + 1) + count] for tile in range(vectors.shape[1] // 128)], axis=1
    )
    vector_grad_ref[...] = gradient
    moment = decay_rate * moment_ref[...] + share * (gradient * gradient + tiny_square)
    moment_new_ref[...] = moment
    spread = jnp.sqrt(jnp.mean(vectors * vectors, axis=1, keepdims=True))
    vector_new_ref[...] = vectors - step_rate * spread * gradient * lax.rsqrt(moment)


def packed_body(
    tokens, keep_mask, cotangent, qkv_weight, proj_weight, up_weight, down_weight, vectors,
    qkv_rows, qkv_cols, proj_rows, proj_cols, up_rows, up_cols, down_rows, down_cols, vector_moment,
):
    spread, dp_size = lax.axis_size("group"), lax.axis_size("dp")
    low, high = jnp.bfloat16, jnp.float32
    place = linear_place().astype(jnp.int32).reshape(1)
    group = lax.axis_index("group")
    held, slots, width = tokens.shape
    images, length = keep_mask.shape
    hidden = up_weight.shape[1] * spread
    total = images * length
    rows = qkv_weight.shape[0]
    folds = down_weight.shape[0] // rows
    core_bits = (1,)
    near_bits = tuple(1 << at for at in range(1, spread.bit_length()))
    far_bits = tuple(spread << at for at in range(1, dp_size.bit_length() - 1))
    half = spread * dp_size // 2

    anywhere = pl.BlockSpec(memory_space=pl.ANY)
    in_smem = pl.BlockSpec(memory_space=pltpu.SMEM)

    in_vmem = pl.BlockSpec(memory_space=pltpu.VMEM)
    small = functools.partial(
        pl.pallas_call, compiler_params=pltpu.CompilerParams(vmem_limit_bytes=vmem_bytes)
    )
    masters = (qkv_weight, proj_weight, up_weight, down_weight)
    parted = jax.ShapeDtypeStruct((spread, slots, images, width), low)

    def after(array, awaited):
        return small(
            after_kernel,
            in_specs=[anywhere] * (1 + len(awaited)),
            out_specs=anywhere,
            out_shape=jax.ShapeDtypeStruct(array.shape, array.dtype),
            input_output_aliases={0: 0},
        )(array, *awaited)

    def to_group(parts):
        return lax.all_to_all(parts, "group", split_axis=0, concat_axis=0, tiled=True)

    def to_images(parts):
        return to_group(parts).reshape(total, width)

    def exchange(parts):
        return [parts[0]] + [permute(part, relative) for relative, part in enumerate(parts) if relative]

    def settle(parts):
        parts = [part.reshape(slots, -1, width) for part in parts]
        whole, token = small(
            functools.partial(settle_kernel, spread),
            in_specs=[in_smem] + [in_vmem] * len(parts),
            out_specs=[in_vmem] * 2,
            out_shape=[
                jax.ShapeDtypeStruct((slots, held, width), low),
                jax.ShapeDtypeStruct((8, 128), high),
            ],
        )(place, *parts)
        return whole.transpose(1, 0, 2), token

    first_cols = qkv_weight.shape[1] + proj_weight.shape[1]
    second_cols = up_weight.shape[1] + folds * down_weight.shape[1]
    pack_own = small(pack_kernel, out_shape=jax.ShapeDtypeStruct((rows, first_cols + second_cols), low))(*masters)
    across_y, across_x = near_bits
    pack_arrived = permute(pack_own, across_y)
    cotangent_cut = small(cut, out_shape=parted)(cotangent.transpose(1, 0, 2))
    token_cut, first_pair, second_pair = small(
        token_kernel,
        in_specs=[in_vmem] * 3 + [anywhere],
        out_shape=[
            parted,
            jax.ShapeDtypeStruct((2, rows, first_cols), low),
            jax.ShapeDtypeStruct((2, rows, second_cols), low),
        ],
    )(tokens.transpose(1, 0, 2), pack_own, pack_arrived, cotangent_cut)
    inputs = to_images(token_cut)

    def gather_far(pair):
        return [pair] + [permute(pair, mask) for mask in direct_masks(far_bits)]

    def join(parts, awaited=()):
        count = len(parts) * parts[0].shape[0]
        return small(
            functools.partial(join_kernel, len(parts)),
            in_specs=[in_vmem] * len(parts) + [anywhere] * len(awaited),
            out_shape=jax.ShapeDtypeStruct((count, *parts[0].shape[1:]), low),
        )(*parts, *awaited)

    def gather_rest(held):
        arrived = permute(held, across_x)
        return [held, arrived, permute(held, core_bits[0]), permute(arrived, core_bits[0])]

    first_far = join(gather_far(first_pair))
    upstream = to_images(cotangent_cut)
    first_blocks = gather_rest(first_far)
    second_far = gather_far(second_pair)

    step_rows = PER_STEP * length
    block = (step_rows, width)
    pairs = width // (2 * HEAD_DIM)
    steps = images // PER_STEP
    statics = (images, dp_size, spread)
    wide = scratch(width // 128, total, 128)
    probs_block = (PER_STEP, pairs, length, 2 * length)
    attention_outs = [
        ((total, 3 * width), low, (step_rows, 3 * width)),
        ((images, *probs_block[1:]), low, probs_block),
        ((total, width), low, block),
        ((total, width), high, block),
    ]
    attention_flops = (2 * total * width * 4 * width + 8 * total * length * width) // steps
    attention_scratches = [scratch(length, images), scratch(step_rows, width, dtype=low)]
    *attention, x, w_qkv, w_proj, qkv_t, proj_t = call_kernel(
        first_attention_kernel, statics, 1,
        ["place"] + [None] * 7,
        attention_outs
        + [
            ((total, width), low, None),
            ((width, 3 * width), low, None),
            ((width, width), low, None),
            ((3 * width, width), low, None),
            ((width, width), low, None),
        ],
        [scratch(dp_size * spread, rows, first_cols, dtype=low), wide] + attention_scratches,
        (place, inputs, *first_blocks, keep_mask, vectors),
        attention_flops,
    )
    second_blocks = gather_rest(join(second_far, attention[:1]))
    for first_step, count in ((1, steps - 2), (steps - 1, 1)):
        attention = call_kernel(
            next_attention_kernel, (first_step * PER_STEP,), count,
            [block] + [None] * 4 + ["await"] * len(attention),
            attention_outs, attention_scratches,
            (x, keep_mask, w_qkv, w_proj, vectors, *attention),
            attention_flops * count, first_step=first_step,
            aliases={5 + at: at for at in range(len(attention))},
        )
    qkv, probs, attended, middle = attention
    piece = ((slots * images, width), low, None)
    ff_rows = FF_PER_STEP * length
    ff_block = (ff_rows, width)
    results = call_kernel(
        feed_forward_packed_kernel, statics, images // FF_PER_STEP,
        ["place"] + [None] * 5 + [ff_block, ff_block] + [None] * 2,
        [piece] * spread
        + [
            ((total, width), high, ff_block),
            ((total, width), low, ff_block),
            ((half, rows, second_cols), low, None),
            ((half, rows, second_cols), low, None),
            ((width, width), high, None),
            ((8, width), high, None),
            ((1, hidden), high, None),
        ],
        [
            scratch(width, hidden, dtype=low),
            scratch(hidden, width, dtype=low),
            scratch(hidden, width, dtype=low),
            scratch(dp_size * spread, rows, second_cols, dtype=low),
            scratch(1, hidden),
            wide,
            scratch(ff_rows, width, dtype=low),
            scratch(width, ff_rows, dtype=low),
            scratch(ff_rows, width, dtype=low),
            scratch(width, ff_rows, dtype=low),
            scratch(ff_rows, width),
            scratch(ff_rows, 128),
            scratch(ff_rows, width),
            scratch(ff_rows, width),
            scratch(hidden, width, dtype=low),
            scratch(width, hidden, dtype=low),
            scratch(width, hidden),
            scratch(width, hidden),
        ],
        (
            place, upstream, *second_blocks, middle, attended, proj_t, vectors,
        ),
        12 * total * width * hidden + 4 * total * width * width, total * hidden,
    )
    d_middle, d_attended, ff_keep, ff_leave, proj_total, ff_sums, up_sums = results[spread:]

    def add_parts(count, keep, arrived, awaited):
        part = (keep.shape[0] // count, *keep.shape[1:])
        return small(
            functools.partial(add_kernel, count),
            in_specs=[in_vmem] * 2 + [anywhere] * len(awaited),
            out_specs=[in_vmem] * count,
            out_shape=[jax.ShapeDtypeStruct(part, high)]
            + [jax.ShapeDtypeStruct(part, low)] * (count - 1),
        )(keep, arrived, *awaited)

    ff_first = permute(ff_leave, core_bits[0])
    ff_count = half // 2
    ff_next = add_wide(ff_keep[ff_count:], ff_first[ff_count:]).astype(low)
    ff_arrived = permute(ff_next, across_x)
    output_parts = exchange(results[:spread])
    pack_half = ((half, rows, first_cols), low, None)
    wide_rows = (step_rows, 3 * width)
    d_projected, qkv_keep, qkv_leave, att_sums = call_kernel(
        attention_back_packed_kernel, (dp_size, spread), steps,
        ["place", block, wide_rows, probs_block, block, None, None, "await"],
        [((total, 3 * width), low, wide_rows), pack_half, pack_half, ((8, width), high, None)],
        [scratch(step_rows, width, dtype=low), scratch(width, 3 * width)],
        (place, x, qkv, probs, d_attended, vectors, proj_total, ff_next),
        2 * total * width * 3 * width + 16 * total * length * width,
    )
    qkv_arrived = permute(after(qkv_leave, output_parts[1:]), core_bits[0])
    input_flops = 2 * total * width * 3 * width
    input_ins = [block, wide_rows, block, None, None, None]
    input_outs = [((total, width), low, block), ((8, width), high, None)]
    d_input, att_sums = call_kernel(
        first_input_kernel, (length,), 1, input_ins, input_outs, [scratch(step_rows, width)],
        (x, d_projected, d_middle, qkv_t, vectors, att_sums), input_flops // steps,
    )
    ff_quarter = half // 4
    ff_last = add_wide(
        ff_keep[ff_quarter:ff_count], ff_first[ff_quarter:ff_count], ff_arrived[ff_quarter:]
    ).astype(low)
    ff_last_arrived = permute(ff_last, across_y)
    qkv_held, *leaving = add_parts(4, qkv_keep, qkv_arrived, [ff_last])
    qkv_parts = [permute(part, mask) for part, mask in zip(leaving, direct_masks(near_bits))]
    d_input, att_sums = call_kernel(
        first_input_kernel, (length,), 1, input_ins + ["await"] * 2, input_outs, [scratch(step_rows, width)],
        (x, d_projected, d_middle, qkv_t, vectors, att_sums, d_input, leaving[0]), input_flops // steps,
        first_step=1, aliases={6: 0},
    )
    ff_held = add_wide(
        ff_keep[:ff_quarter], ff_first[:ff_quarter], ff_arrived[:ff_quarter], ff_last_arrived
    )
    qkv_held = add_wide(qkv_held, *qkv_parts)
    blocks = jnp.concatenate([ff_held, qkv_held], axis=2)
    far_leaving = [blocks[at : at + 1].astype(low) for at in range(1, blocks.shape[0])]
    block_parts = [blocks[:1]] + [permute(part, mask) for part, mask in zip(far_leaving, direct_masks(far_bits))]
    results = call_kernel(
        last_input_kernel, (images, spread, length, 2 * PER_STEP), steps - 2,
        ["place"] + input_ins + [None, "await"],
        [piece] * spread + [((8, width), high, None)],
        [wide, scratch(step_rows, width)],
        (place, x, d_projected, d_middle, qkv_t, vectors, att_sums, d_input, far_leaving[0]), input_flops // steps * (steps - 2),
        first_step=2,
    )
    att_sums = results[spread]
    input_pieces = list(results[:spread])
    heights = [master.shape[0] * dp_size for master in masters]
    widths = [master.shape[1] * spread for master in masters]
    rows_old, cols_old = [qkv_rows, proj_rows, up_rows, down_rows], [qkv_cols, proj_cols, up_cols, down_cols]

    def like(*arrays):
        return [jax.ShapeDtypeStruct(array.shape, high) for array in arrays]

    operands = (*block_parts, att_sums, ff_sums, up_sums, *masters, *rows_old)
    *grads, row_sums, message = small(
        functools.partial(gradient_kernel, len(block_parts)),
        out_shape=like(*masters) + [jax.ShapeDtypeStruct((8, rows), high), jax.ShapeDtypeStruct((24, width), high)],
    )(*operands)
    input_pieces[1] = after(input_pieces[1], [row_sums])
    output_parts[0] = after(output_parts[0], [row_sums])
    block_output, settled = settle(output_parts)
    input_grad, input_settled = settle(exchange(input_pieces))
    message = added([message] + [permute(message, mask) for mask in direct_masks((across_x, far_bits[0]))])
    for bit in far_bits[1:-1]:
        message = message + permute(message, bit)
    messages = [message, permute(message, far_bits[-1])]
    col_sums, message = small(
        column_kernel,
        in_specs=[in_vmem] * (1 + len(messages)) + [anywhere],
        out_shape=[
            jax.ShapeDtypeStruct((8, width), high),
            jax.ShapeDtypeStruct((16 + width // 8, 128), high),
        ],
    )(row_sums, *messages, settled)
    messages = [message] + [permute(message, mask) for mask in range(1, spread)]
    operands = (*messages, col_sums, vectors, vector_moment, *grads, *masters, *rows_old, *cols_old)
    results = small(
        functools.partial(update_kernel, len(messages), heights, widths),
        in_specs=[in_vmem] * len(operands) + [anywhere],
        out_shape=like(*masters, *cols_old, *rows_old, vectors, vectors, vectors),
    )(*operands, input_settled)
    news, cols_new, rows_out = results[:4], results[4:8], results[8:12]
    vector_grad, vector_moment_new, vector_new = results[12:]
    factored = []
    for which in range(4):
        factored += [grads[which], rows_out[which], cols_new[which], news[which]]
    return (block_output, input_grad, *factored, vector_grad, vector_moment_new, vector_new)


def body(*arrays):
    spread, dp_size = lax.axis_size("group"), lax.axis_size("dp")
    rows, images = arrays[3].shape[0], arrays[1].shape[0]
    slots, width = arrays[0].shape[1:]
    folds = arrays[6].shape[0] // rows
    powers = all(size & (size - 1) == 0 for size in (spread, dp_size))
    fits = powers and spread == 4 and dp_size > 2
    fits = fits and arrays[5].shape[1] <= width and folds <= 5
    fits = fits and rows % 16 == 0 and images % FF_PER_STEP == 0 and images > 2 * PER_STEP and images % 16 == 0 and slots % 4 == 0
    return packed_body(*arrays) if fits else general_body(*arrays)


def solution(mesh):
    in_specs = (
        P("dp", "group", None),
        P(("dp", "group"), None),
        P("dp", "group", None),
        P("dp", "group"),
        P("dp", "group"),
        P("dp", "group"),
        P("dp", "group"),
        P(),
        P("dp"),
        P("group"),
        P("dp"),
        P("group"),
        P("dp"),
        P("group"),
        P("dp"),
        P("group"),
        P(),
    )
    out_specs = (
        P("dp", "group", None),
        P("dp", "group", None),
        P("dp", "group"),
        P("dp"),
        P("group"),
        P("dp", "group"),
        P("dp", "group"),
        P("dp"),
        P("group"),
        P("dp", "group"),
        P("dp", "group"),
        P("dp"),
        P("group"),
        P("dp", "group"),
        P("dp", "group"),
        P("dp"),
        P("group"),
        P("dp", "group"),
        P(),
        P(),
        P(),
    )
    return jax.shard_map(body, mesh=mesh, in_specs=in_specs, out_specs=out_specs, check_vma=False)
```

profile of v0, /device:TPU:0, one launch (start us, length us, event | category | flops | bytes accessed | tf_op | source)
XLA Modules:
  0.0 220.5 jit_solution(5653601389300898948)
XLA Ops:
  0.7 1.7 shard_map.329.own_ref
  2.4 3.0 %collective-permute-start = (bf16[48,1152]{1,0:T(8,128)(2,1)}, bf16[48,1152]{1,0:T(8,128)(2,1)S(1)}, u32[]{:S(2)}, u32[]{:S(2)}) collective-permute-start(bf16[48,1152]{1,0:T(8,128)(2,1)} %shard_map.329.own_ref), channel_id=1, source_target_pairs={{0,2},{1,3},{2,0},{3,1},{4,6},{5,7},{6,4},{7,5},{8,10},{9,11},{10,... | collective-permute-start | bytes 331784 | tf_op jit(solution)/shard_map/ppermute | solution.py:643
  5.3 2.8 %shard_map.328._ = bf16[4,36,16,384]{3,2,1,0:T(8,128)(2,1)} custom-call(bf16[36,64,384]{2,1,0:T(8,128)(2,1)} %bitcast.16), custom_call_target="tpu_custom_call" | custom-call | tf_op jit(solution)/shard_map/pallas_call | solution.py:1258
  9.2 2.9 %shard_map.330 = (bf16[4,36,16,384]{3,2,1,0:T(8,128)(2,1)}, bf16[2,48,384]{2,1,0:T(8,128)(2,1)}, bf16[2,48,768]{2,1,0:T(8,128)(2,1)}) custom-call(bf16[36,64,384]{2,1,0:T(8,128)(2,1)} %bitcast.15, bf16[48,1152]{1,0:T(8,128)(2,1)} %shard_map.329.own_ref, bf16[48,1152]{1,0:T(8,128)(2,1)} %copy-done.15, bf16[4,36,16,384]{3,2,1,0:T(8,128)(2,1)} %shard_map.328._), custom_call_target="tpu_custom_call" | custom-call | tf_op jit(solution)/shard_map/pallas_call | solution.py:1259
  12.2 3.7 %all-to-all-start.1 = ((bf16[4,36,16,384]{3,2,1,0:T(8,128)(2,1)}), bf16[4,36,16,384]{3,2,1,0:T(8,128)(2,1)S(1)}, u32[]{:S(2)}, u32[]{:S(2)}) async-start(bf16[4,36,16,384]{3,2,1,0:T(8,128)(2,1)} %get-tuple-element.97), calls=%async_computation.1 | async-start | bytes 3538944 | tf_op jit(solution)/shard_map/all_to_all | solution.py:1232
  15.9 3.9 %collective-permute-start.6 = (bf16[2,48,384]{2,1,0:T(8,128)(2,1)S(1)}, bf16[2,48,384]{2,1,0:T(8,128)(2,1)S(1)}, u32[]{:S(2)}, u32[]{:S(2)}) collective-permute-start(bf16[2,48,384]{2,1,0:T(8,128)(2,1)S(1)} %copy-done.20), channel_id=1, source_target_pairs={{0,24},{1,25},{2,26},{3,27},{4,28},{5,29},{6,30},{7,31},{8,16},{9,... | collective-permute-start | bytes 221192 | tf_op jit(solution)/shard_map/ppermute | solution.py:643
  20.4 2.5 %collective-permute-done.6.refs_3_ = bf16[2,48,384]{2,1,0:T(8,128)(2,1)S(1)} collective-permute-done((bf16[2,48,384]{2,1,0:T(8,128)(2,1)S(1)}, bf16[2,48,384]{2,1,0:T(8,128)(2,1)S(1)}, u32[]{:S(2)}, u32[]{:S(2)}) %collective-permute-start.6) | collective-permute-done | bytes 73760 | tf_op jit(solution)/shard_map/ppermute | solution.py:643
  23.0 3.6 %collective-permute-done.5.refs_2_ = bf16[2,48,384]{2,1,0:T(8,128)(2,1)S(1)} collective-permute-done((bf16[2,48,384]{2,1,0:T(8,128)(2,1)S(1)}, bf16[2,48,384]{2,1,0:T(8,128)(2,1)S(1)}, u32[]{:S(2)}, u32[]{:S(2)}) %collective-permute-start.5) | collective-permute-done | bytes 73760 | tf_op jit(solution)/shard_map/ppermute | solution.py:643
  27.8 1.7 shard_map.331.refs_0_
  29.6 1.5 collective-permute-start.7
  31.0 7.4 %collective-permute-done.7.refs_1_ = bf16[8,48,384]{2,1,0:T(8,128)(2,1)} collective-permute-done((bf16[8,48,384]{2,1,0:T(8,128)(2,1)}, bf16[8,48,384]{2,1,0:T(8,128)(2,1)}, u32[]{:S(2)}, u32[]{:S(2)}) %collective-permute-start.7) | collective-permute-done | bytes 294944 | tf_op jit(solution)/shard_map/ppermute | solution.py:643
  38.4 2.5 %collective-permute-start.3 = (bf16[2,48,768]{2,1,0:T(8,128)(2,1)}, bf16[2,48,768]{2,1,0:T(8,128)(2,1)}, u32[]{:S(2)}, u32[]{:S(2)}) collective-permute-start(bf16[2,48,768]{2,1,0:T(8,128)(2,1)} %get-tuple-element.96.refs_0_), channel_id=1, source_target_pairs={{0,24},{1,25},{2,26},{3,27},{4,28},{5,29},{6,30},{7,31},{8,16},{9,... | collective-permute-start | bytes 442376 | tf_op jit(solution)/shard_map/ppermute | solution.py:643
  40.9 1.9 collective-permute-start.1
  42.8 1.2 copy-done
  44.0 3.6 %all-to-all-start = ((bf16[4,36,16,384]{3,2,1,0:T(8,128)(2,1)}), bf16[4,36,16,384]{3,2,1,0:T(8,128)(2,1)S(1)}, u32[]{:S(2)}, u32[]{:S(2)}) async-start(bf16[4,36,16,384]{3,2,1,0:T(8,128)(2,1)} %shard_map.328._), calls=%async_computation | async-start | bytes 3538944 | tf_op jit(solution)/shard_map/all_to_all | solution.py:1232
  47.6 10.5 %shard_map.332 = (bf16[2304,1152]{1,0:T(8,128)(2,1)}, bf16[16,3,144,288]{3,2,1,0:T(8,128)(2,1)}, bf16[2304,384]{1,0:T(8,128)(2,1)}, f32[2304,384]{1,0:T(8,128)},...) custom-call(s32[1]{0:T(128)} %bitcast.place_ref, ...), custom_call_target="tpu_custom_call" | custom-call | flops 7474249728 | bytes 21703684 | tf_op jit(solution)/shard_map/pallas_call | solution.py:535
  58.1 2.0 shard_map.333.refs_1_
  60.6 1.5 collective-permute-start.10
  62.1 9.4 %shard_map.334 = (bf16[2304,1152]{1,0:T(8,128)(2,1)}, bf16[16,3,144,288]{3,2,1,0:T(8,128)(2,1)}, bf16[2304,384]{1,0:T(8,128)(2,1)}, f32[2304,384]{1,0:T(8,128)}) custom-call(bf16[2304,384]{1,0:T(8,128)(2,1)} %get-tuple-element.100.x_ref, s32[16,144]{1,0:T(8,128)} %keep_ref.3, ...), custom_call_target="tpu_custom_call", output_to_operand_aliasing={{0}: (5, {}), {1}: (6, {}), {2}: (7, {}), {3}: (8, {})} | custom-call | flops 14948499456 | bytes 32173056 | tf_op jit(solution)/shard_map/pallas_call | solution.py:535
  71.5 4.6 %collective-permute-done.10.refs_2_ = bf16[8,48,768]{2,1,0:T(8,128)(2,1)S(1)} collective-permute-done((bf16[8,48,768]{2,1,0:T(8,128)(2,1)}, bf16[8,48,768]{2,1,0:T(8,128)(2,1)S(1)}, u32[]{:S(2)}, u32[]{:S(2)}) %collective-permute-start.10) | collective-permute-done | bytes 589856 | tf_op jit(solution)/shard_map/ppermute | solution.py:643
  76.1 5.9 %shard_map.335 = (bf16[2304,1152]{1,0:T(8,128)(2,1)}, bf16[16,3,144,288]{3,2,1,0:T(8,128)(2,1)}, bf16[2304,384]{1,0:T(8,128)(2,1)}, f32[2304,384]{1,0:T(8,128)}) custom-call(bf16[2304,384]{1,0:T(8,128)(2,1)} %get-tuple-element.100.x_ref, s32[16,144]{1,0:T(8,128)} %keep_ref.3, ...), custom_call_target="tpu_custom_call", output_to_operand_aliasing={{0}: (5, {}), {1}: (6, {}), {2}: (7, {}), {3}: (8, {})} | custom-call | flops 7474249728 | bytes 32173056 | tf_op jit(solution)/shard_map/pallas_call | solution.py:535
  82.0 1.2 copy-done.1
  83.6 45.3 %shard_map.336 = (bf16[576,384]{1,0:T(8,128)(2,1)}, bf16[576,384]{1,0:T(8,128)(2,1)}, bf16[576,384]{1,0:T(8,128)(2,1)}, bf16[576,384]{1,0:T(8,128)(2,1)}, f32[23...) custom-call(s32[1]{0:T(128)} %bitcast.place_ref, ...), custom_call_target="tpu_custom_call" | custom-call | flops 141331267584 | bytes 19795972 | tf_op jit(solution)/shard_map/pallas_call | solution.py:535
  129.5 1.9 collective-permute-start.17
  132.0 1.2 add_convert_fusion._
  133.2 1.6 collective-permute-start.14
  134.8 16.5 %shard_map.337 = (bf16[2304,1152]{1,0:T(8,128)(2,1)}, bf16[16,48,384]{2,1,0:T(8,128)(2,1)}, bf16[16,48,384]{2,1,0:T(8,128)(2,1)}, f32[8,384]{1,0:T(8,128)}) custom-call(s32[1]{0:T(128)} %bitcast.place_ref, bf16[2304,384]{1,0:T(8,128)(2,1)} %get-tuple-element.100.x_ref, bf16[2304,1152]{1,0:T(8,128)(2,1)} %get-tuple-element.116.qkv_ref, ...), custom_call_target="tpu_custom_call" | custom-call | flops 32614907904 | bytes 20527108 | tf_op jit(solution)/shard_map/pallas_call | solution.py:535
  152.4 4.0 %shard_map.340 = (bf16[2304,384]{1,0:T(8,128)(2,1)}, f32[8,384]{1,0:T(8,128)}) custom-call(bf16[2304,384]{1,0:T(8,128)(2,1)} %get-tuple-element.100.x_ref, bf16[2304,1152]{1,0:T(8,128)(2,1)} %get-tuple-element.129.d_projected_ref, f32[2304,384]{1,0:T(8,128)} %get-tuple-element.130.d_middle_ref, bf16[1152,384]{1,0:T(8,128)(2,1)} %get-tuple-element.131.qkv_t_ref, ...), custom_call_target="tpu_custom_call" | custom-call | flops 4076863488 | bytes 13314048 | tf_op jit(solution)/shard_map/pallas_call | solution.py:535
  156.6 2.0 collective-permute-start.15
  159.4 2.2 shard_map.339
  161.6 1.2 collective-permute-start.21
  163.1 1.9 collective-permute-start.20
  165.1 4.0 %shard_map.341 = (bf16[2304,384]{1,0:T(8,128)(2,1)}, f32[8,384]{1,0:T(8,128)}) custom-call(bf16[2304,384]{1,0:T(8,128)(2,1)} %get-tuple-element.100.x_ref, bf16[2304,1152]{1,0:T(8,128)(2,1)} %get-tuple-element.129.d_projected_ref, f32[2304,384]{1,0:T(8,128)} %get-tuple-element.130.d_middle_ref, ...), custom_call_target="tpu_custom_call", output_to_operand_aliasing={{0}: (6, {})} | custom-call | flops 4076863488 | bytes 15230976 | tf_op jit(solution)/shard_map/pallas_call | solution.py:535
  169.0 1.7 collective-permute-done.22
  170.8 1.8 collective-permute-done.20
  175.4 2.5 %collective-permute-start.25 = (bf16[1,48,1152]{2,1,0:T(8,128)(2,1)S(1)}, bf16[1,48,1152]{2,1,0:T(8,128)(2,1)S(1)}, u32[]{:S(2)}, u32[]{:S(2)}) collective-permute-start(bf16[1,48,1152]{2,1,0:T(8,128)(2,1)S(1)} %get-tuple-element.171), channel_id=1, source_target_pairs={{0,24},{1,25},{2,26},{3,27},{4,28},{5,29},{6,30},{7,31},{8,16},{9,... | collective-permute-start | bytes 331784 | tf_op jit(solution)/shard_map/ppermute | solution.py:643
  178.0 1.9 collective-permute-start.23
  179.9 8.6 %shard_map.342 = (bf16[576,384]{1,0:T(8,128)(2,1)}, bf16[576,384]{1,0:T(8,128)(2,1)}, bf16[576,384]{1,0:T(8,128)(2,1)}, bf16[576,384]{1,0:T(8,128)(2,1)}, f32[8,384]{1,0:T(8,128)}) custom-call(s32[1]{0:T(128)} %bitcast.place_ref, bf16[2304,384]{1,0:T(8,128)(2,1)} %get-tuple-element.100.x_ref, bf16[2304,1152]{1,0:T(8,128)(2,1)} %get-tuple-element.129.d_projected_ref, ...), custom_call_target="tpu_custom_call" | custom-call | flops 8153726976 | bytes 15194116 | tf_op jit(solution)/shard_map/pallas_call | solution.py:535
  188.5 1.7 collective-permute-start.27
  191.7 2.6 %shard_map.343 = (f32[48,288]{1,0:T(8,128)}, f32[48,96]{1,0:T(8,128)}, f32[48,384]{1,0:T(8,128)}, f32[192,96]{1,0:T(8,128)}, f32[8,48]{1,0:T(8,128)}, /*index=5*/f32[24,384]{1,0:T(8,128)}) custom-call(f32[1,48,1152]{2,1,0:T(8,128)} %fusion.1.refs_0_, bf16[1,48,1152]{2,1,0:T(8,128)(2,1)} %copy-done.18, bf16[1,48,1152]{2,1,0:T(8,128)(2,1)} %copy-done.17, ...), custom_call_target="tpu_custom_call" | custom-call | tf_op jit(solution)/shard_map/pallas_call | solution.py:1444
  195.2 1.9 collective-permute-start.30
  197.1 2.6 %collective-permute-done.31 = f32[24,384]{1,0:T(8,128)S(1)} collective-permute-done((f32[24,384]{1,0:T(8,128)}, f32[24,384]{1,0:T(8,128)S(1)}, u32[]{:S(2)}, u32[]{:S(2)}) %collective-permute-start.31) | collective-permute-done | bytes 36896 | tf_op jit(solution)/shard_map/ppermute | solution.py:643
  200.7 3.2 %collective-permute-done.29 = f32[24,384]{1,0:T(8,128)S(1)} collective-permute-done((f32[24,384]{1,0:T(8,128)}, f32[24,384]{1,0:T(8,128)S(1)}, u32[]{:S(2)}, u32[]{:S(2)}) %collective-permute-start.29) | collective-permute-done | bytes 36896 | tf_op jit(solution)/shard_map/ppermute | solution.py:643
  205.7 2.8 %shard_map.345 = (bf16[36,64,384]{2,1,0:T(8,128)(2,1)}, f32[8,128]{1,0:T(8,128)}) custom-call(s32[1]{0:T(128)} %bitcast.place_ref, bf16[36,16,384]{2,1,0:T(8,128)(2,1)} %bitcast.19, bf16[36,16,384]{2,1,0:T(8,128)(2,1)} %bitcast.20, bf16[36,16,384]{2,1,0:T(8,128)(2,1)} %bitcast.21, bf16[36,16,384]{2,1,0:T(8,128)(2,1)} %bitcast.22), custom_call_target="tpu_custom_call" | custom-call | tf_op jit(solution)/shard_map/pallas_call | solution.py:1242
  210.2 1.5 shard_map.348
  211.7 1.8 collective-permute-start.34
  214.6 2.8 %shard_map.347 = (bf16[36,64,384]{2,1,0:T(8,128)(2,1)}, f32[8,128]{1,0:T(8,128)}) custom-call(s32[1]{0:T(128)} %bitcast.place_ref, bf16[36,16,384]{2,1,0:T(8,128)(2,1)} %bitcast.23, bf16[36,16,384]{2,1,0:T(8,128)(2,1)} %bitcast.26, bf16[36,16,384]{2,1,0:T(8,128)(2,1)} %bitcast.24, bf16[36,16,384]{2,1,0:T(8,128)(2,1)} %bitcast.25), custom_call_target="tpu_custom_call" | custom-call | tf_op jit(solution)/shard_map/pallas_call | solution.py:1242
  218.0 2.3 %shard_map.349 = (f32[48,288]{1,0:T(8,128)}, f32[48,96]{1,0:T(8,128)}, f32[48,384]{1,0:T(8,128)}, f32[192,96]{1,0:T(8,128)}, f32[288]{0:T(512)}, /*index=5*/f32[...) custom-call(f32[64,128]{1,0:T(8,128)} %get-tuple-element.150.refs_0_, ...), custom_call_target="tpu_custom_call" | custom-call | tf_op jit(solution)/shard_map/pallas_call | solution.py:1466
  (120 shorter events, 18.7 us)
Async XLA Ops:
  2.4 6.2 %collective-permute-start = (bf16[48,1152]{1,0:T(8,128)(2,1)}, bf16[48,1152]{1,0:T(8,128)(2,1)S(1)}, u32[]{:S(2)}, u32[]{:S(2)}) collective-permute-start(bf16[48,1152]{1,0:T(8,128)(2,1)} %shard_map.329.own_ref), channel_id=1, source_target_pairs={{0,2},{1,3},{2,0},{3,1},{4,6},{5,7},{6,4},{7,5},{8,10},{9,11},{10,... | collective-permute-start | bytes 331784 | tf_op jit(solution)/shard_map/ppermute | solution.py:643
  12.2 3.7 %copy-start.20 = (bf16[2,48,384]{2,1,0:T(8,128)(2,1)S(1)}, bf16[2,48,384]{2,1,0:T(8,128)(2,1)}, u32[]{:S(2)}) copy-start(bf16[2,48,384]{2,1,0:T(8,128)(2,1)} %get-tuple-element.98.refs_0_) | copy-start | bytes 221188
  12.2 30.6 %all-to-all-start.1 = ((bf16[4,36,16,384]{3,2,1,0:T(8,128)(2,1)}), bf16[4,36,16,384]{3,2,1,0:T(8,128)(2,1)S(1)}, u32[]{:S(2)}, u32[]{:S(2)}) async-start(bf16[4,36,16,384]{3,2,1,0:T(8,128)(2,1)} %get-tuple-element.97), calls=%async_computation.1 | async-start | bytes 3538944 | tf_op jit(solution)/shard_map/all_to_all | solution.py:1232
  15.9 7.1 %collective-permute-start.6 = (bf16[2,48,384]{2,1,0:T(8,128)(2,1)S(1)}, bf16[2,48,384]{2,1,0:T(8,128)(2,1)S(1)}, u32[]{:S(2)}, u32[]{:S(2)}) collective-permute-start(bf16[2,48,384]{2,1,0:T(8,128)(2,1)S(1)} %copy-done.20), channel_id=1, source_target_pairs={{0,24},{1,25},{2,26},{3,27},{4,28},{5,29},{6,30},{7,31},{8,16},{9,... | collective-permute-start | bytes 221192 | tf_op jit(solution)/shard_map/ppermute | solution.py:643
  19.8 6.8 %collective-permute-start.5 = (bf16[2,48,384]{2,1,0:T(8,128)(2,1)S(1)}, bf16[2,48,384]{2,1,0:T(8,128)(2,1)S(1)}, u32[]{:S(2)}, u32[]{:S(2)}) collective-permute-start(bf16[2,48,384]{2,1,0:T(8,128)(2,1)S(1)} %copy-done.20), channel_id=1, source_target_pairs={{0,16},{1,17},{2,18},{3,19},{4,20},{5,21},{6,22},{7,23},{8,24},{9,... | collective-permute-start | bytes 221192 | tf_op jit(solution)/shard_map/ppermute | solution.py:643
  19.8 6.8 %collective-permute-start.4 = (bf16[2,48,384]{2,1,0:T(8,128)(2,1)S(1)}, bf16[2,48,384]{2,1,0:T(8,128)(2,1)S(1)}, u32[]{:S(2)}, u32[]{:S(2)}) collective-permute-start(bf16[2,48,384]{2,1,0:T(8,128)(2,1)S(1)} %copy-done.20), channel_id=1, source_target_pairs={{0,8},{1,9},{2,10},{3,11},{4,12},{5,13},{6,14},{7,15},{8,0},{9,1},... | collective-permute-start | bytes 221192 | tf_op jit(solution)/shard_map/ppermute | solution.py:643
  23.0 3.6 %copy-start.21 = (bf16[2,48,384]{2,1,0:T(8,128)(2,1)}, bf16[2,48,384]{2,1,0:T(8,128)(2,1)S(1)}, u32[]{:S(2)}) copy-start(bf16[2,48,384]{2,1,0:T(8,128)(2,1)S(1)} %collective-permute-done.6.refs_3_) | copy-start | bytes 221188
  29.6 8.9 %collective-permute-start.7 = (bf16[8,48,384]{2,1,0:T(8,128)(2,1)}, bf16[8,48,384]{2,1,0:T(8,128)(2,1)}, u32[]{:S(2)}, u32[]{:S(2)}) collective-permute-start(bf16[8,48,384]{2,1,0:T(8,128)(2,1)} %shard_map.331.refs_0_), channel_id=1, source_target_pairs={{0,4},{1,5},{2,6},{3,7},{4,0},{5,1},{6,2},{7,3},{8,12},{9,13},{10,... | collective-permute-start | bytes 884744 | tf_op jit(solution)/shard_map/ppermute | solution.py:643
  31.0 16.6 %collective-permute-start.8 = (bf16[8,48,384]{2,1,0:T(8,128)(2,1)}, bf16[8,48,384]{2,1,0:T(8,128)(2,1)}, u32[]{:S(2)}, u32[]{:S(2)}) collective-permute-start(bf16[8,48,384]{2,1,0:T(8,128)(2,1)} %shard_map.331.refs_0_), channel_id=1, source_target_pairs={{0,1},{1,0},{2,3},{3,2},{4,5},{5,4},{6,7},{7,6},{8,9},{9,8},{10,11... | collective-permute-start | bytes 884744 | tf_op jit(solution)/shard_map/ppermute | solution.py:643
  38.4 9.2 %collective-permute-start.9 = (bf16[8,48,384]{2,1,0:T(8,128)(2,1)}, bf16[8,48,384]{2,1,0:T(8,128)(2,1)}, u32[]{:S(2)}, u32[]{:S(2)}) collective-permute-start(bf16[8,48,384]{2,1,0:T(8,128)(2,1)} %collective-permute-done.7.refs_1_), channel_id=1, source_target_pairs={{0,1},{1,0},{2,3},{3,2},{4,5},{5,4},{6,7},{7,6},{8,9},{9,8},{10,11... | collective-permute-start | bytes 884744 | tf_op jit(solution)/shard_map/ppermute | solution.py:643
  38.4 19.7 %collective-permute-start.3 = (bf16[2,48,768]{2,1,0:T(8,128)(2,1)}, bf16[2,48,768]{2,1,0:T(8,128)(2,1)}, u32[]{:S(2)}, u32[]{:S(2)}) collective-permute-start(bf16[2,48,768]{2,1,0:T(8,128)(2,1)} %get-tuple-element.96.refs_0_), channel_id=1, source_target_pairs={{0,24},{1,25},{2,26},{3,27},{4,28},{5,29},{6,30},{7,31},{8,16},{9,... | collective-permute-start | bytes 442376 | tf_op jit(solution)/shard_map/ppermute | solution.py:643
  40.9 17.2 %collective-permute-start.2 = (bf16[2,48,768]{2,1,0:T(8,128)(2,1)}, bf16[2,48,768]{2,1,0:T(8,128)(2,1)}, u32[]{:S(2)}, u32[]{:S(2)}) collective-permute-start(bf16[2,48,768]{2,1,0:T(8,128)(2,1)} %get-tuple-element.96.refs_0_), channel_id=1, source_target_pairs={{0,16},{1,17},{2,18},{3,19},{4,20},{5,21},{6,22},{7,23},{8,24},{9,... | collective-permute-start | bytes 442376 | tf_op jit(solution)/shard_map/ppermute | solution.py:643
  40.9 17.2 %collective-permute-start.1 = (bf16[2,48,768]{2,1,0:T(8,128)(2,1)}, bf16[2,48,768]{2,1,0:T(8,128)(2,1)}, u32[]{:S(2)}, u32[]{:S(2)}) collective-permute-start(bf16[2,48,768]{2,1,0:T(8,128)(2,1)} %get-tuple-element.96.refs_0_), channel_id=1, source_target_pairs={{0,8},{1,9},{2,10},{3,11},{4,12},{5,13},{6,14},{7,15},{8,0},{9,1},... | collective-permute-start | bytes 442376 | tf_op jit(solution)/shard_map/ppermute | solution.py:643
  44.0 38.0 %all-to-all-start = ((bf16[4,36,16,384]{3,2,1,0:T(8,128)(2,1)}), bf16[4,36,16,384]{3,2,1,0:T(8,128)(2,1)S(1)}, u32[]{:S(2)}, u32[]{:S(2)}) async-start(bf16[4,36,16,384]{3,2,1,0:T(8,128)(2,1)} %shard_map.328._), calls=%async_computation | async-start | bytes 3538944 | tf_op jit(solution)/shard_map/all_to_all | solution.py:1232
  60.2 21.8 %collective-permute-start.11 = (bf16[8,48,768]{2,1,0:T(8,128)(2,1)}, bf16[8,48,768]{2,1,0:T(8,128)(2,1)S(1)}, u32[]{:S(2)}, u32[]{:S(2)}) collective-permute-start(bf16[8,48,768]{2,1,0:T(8,128)(2,1)} %shard_map.333.refs_1_), channel_id=1, source_target_pairs={{0,1},{1,0},{2,3},{3,2},{4,5},{5,4},{6,7},{7,6},{8,9},{9,8},{10,11... | collective-permute-start | bytes 1769480 | tf_op jit(solution)/shard_map/ppermute | solution.py:643
  60.6 15.5 %collective-permute-start.10 = (bf16[8,48,768]{2,1,0:T(8,128)(2,1)}, bf16[8,48,768]{2,1,0:T(8,128)(2,1)S(1)}, u32[]{:S(2)}, u32[]{:S(2)}) collective-permute-start(bf16[8,48,768]{2,1,0:T(8,128)(2,1)} %shard_map.333.refs_1_), channel_id=1, source_target_pairs={{0,4},{1,5},{2,6},{3,7},{4,0},{5,1},{6,2},{7,3},{8,12},{9,13},{10,... | collective-permute-start | bytes 1769480 | tf_op jit(solution)/shard_map/ppermute | solution.py:643
  76.1 5.9 %copy-start.29 = (bf16[8,48,768]{2,1,0:T(8,128)(2,1)}, bf16[8,48,768]{2,1,0:T(8,128)(2,1)S(1)}, u32[]{:S(2)}) copy-start(bf16[8,48,768]{2,1,0:T(8,128)(2,1)S(1)} %collective-permute-done.10.refs_2_) | copy-start | bytes 1769476
  76.1 5.9 %collective-permute-start.12 = (bf16[8,48,768]{2,1,0:T(8,128)(2,1)S(1)}, bf16[8,48,768]{2,1,0:T(8,128)(2,1)S(1)}, u32[]{:S(2)}, u32[]{:S(2)}) collective-permute-start(bf16[8,48,768]{2,1,0:T(8,128)(2,1)S(1)} %collective-permute-done.10.refs_2_), channel_id=1, source_target_pairs={{0,1},{1,0},{2,3},{3,2},{4,5},{5,4},{6,7},{7,6},{8,9},{9,8},{10,11... | collective-permute-start | bytes 1769480 | tf_op jit(solution)/shard_map/ppermute | solution.py:643
  82.0 1.5 copy-start.30
  128.9 3.1 %collective-permute-start.13 = (bf16[16,48,768]{2,1,0:T(8,128)(2,1)}, bf16[16,48,768]{2,1,0:T(8,128)(2,1)S(1)}, u32[]{:S(2)}, u32[]{:S(2)}) collective-permute-start(bf16[16,48,768]{2,1,0:T(8,128)(2,1)} %get-tuple-element.115), channel_id=1, source_target_pairs={{0,1},{1,0},{2,3},{3,2},{4,5},{5,4},{6,7},{7,6},{8,9},{9,8},{10,11... | collective-permute-start | bytes 3538952 | tf_op jit(solution)/shard_map/ppermute | solution.py:643
  129.2 22.1 %collective-permute-start.16 = (bf16[576,384]{1,0:T(8,128)(2,1)}, bf16[576,384]{1,0:T(8,128)(2,1)S(1)}, u32[]{:S(2)}, u32[]{:S(2)}) collective-permute-start(bf16[576,384]{1,0:T(8,128)(2,1)} %get-tuple-element.122), channel_id=1, source_target_pairs={{0,1},{1,0},{2,3},{3,2},{4,5},{5,4},{6,7},{7,6},{8,9},{9,8},{10,11... | collective-permute-start | bytes 1327112 | tf_op jit(solution)/shard_map/ppermute | solution.py:643
  129.5 21.9 %collective-permute-start.17 = (bf16[576,384]{1,0:T(8,128)(2,1)}, bf16[576,384]{1,0:T(8,128)(2,1)S(1)}, u32[]{:S(2)}, u32[]{:S(2)}) collective-permute-start(bf16[576,384]{1,0:T(8,128)(2,1)} %get-tuple-element.123), channel_id=1, source_target_pairs={{0,2},{1,3},{2,0},{3,1},{4,6},{5,7},{6,4},{7,5},{8,10},{9,11},{10,... | collective-permute-start | bytes 1327112 | tf_op jit(solution)/shard_map/ppermute | solution.py:643
  131.4 19.9 %collective-permute-start.18 = (bf16[576,384]{1,0:T(8,128)(2,1)}, bf16[576,384]{1,0:T(8,128)(2,1)S(1)}, u32[]{:S(2)}, u32[]{:S(2)}) collective-permute-start(bf16[576,384]{1,0:T(8,128)(2,1)} %get-tuple-element.124), channel_id=1, source_target_pairs={{0,3},{1,2},{2,1},{3,0},{4,7},{5,6},{6,5},{7,4},{8,11},{9,10},{10,... | collective-permute-start | bytes 1327112 | tf_op jit(solution)/shard_map/ppermute | solution.py:643
  133.2 1.6 copy-start.7
  133.2 23.2 %collective-permute-start.14 = (bf16[8,48,768]{2,1,0:T(8,128)(2,1)S(1)}, bf16[8,48,768]{2,1,0:T(8,128)(2,1)S(1)}, u32[]{:S(2)}, u32[]{:S(2)}) collective-permute-start(bf16[8,48,768]{2,1,0:T(8,128)(2,1)S(1)} %add_convert_fusion._), channel_id=1, source_target_pairs={{0,4},{1,5},{2,6},{3,7},{4,0},{5,1},{6,2},{7,3},{8,12},{9,13},{10,... | collective-permute-start | bytes 1769480 | tf_op jit(solution)/shard_map/ppermute | solution.py:643
  152.4 6.2 %collective-permute-start.19 = (bf16[16,48,384]{2,1,0:T(8,128)(2,1)}, bf16[16,48,384]{2,1,0:T(8,128)(2,1)S(1)}, u32[]{:S(2)}, u32[]{:S(2)}) collective-permute-start(bf16[16,48,384]{2,1,0:T(8,128)(2,1)} %shard_map.338), channel_id=1, source_target_pairs={{0,1},{1,0},{2,3},{3,2},{4,5},{5,4},{6,7},{7,6},{8,9},{9,8},{10,11... | collective-permute-start | bytes 1769480 | tf_op jit(solution)/shard_map/ppermute | solution.py:643
  152.4 4.0 %copy-start.5 = (bf16[16,48,768]{2,1,0:T(8,128)(2,1)S(1)}, bf16[16,48,768]{2,1,0:T(8,128)(2,1)}, u32[]{:S(2)}) copy-start(bf16[16,48,768]{2,1,0:T(8,128)(2,1)} %get-tuple-element.114) | copy-start | bytes 3538948
  156.6 2.0 copy-start.6
  156.6 17.6 %collective-permute-start.15 = (bf16[4,48,768]{2,1,0:T(8,128)(2,1)S(1)}, bf16[4,48,768]{2,1,0:T(8,128)(2,1)}, u32[]{:S(2)}, u32[]{:S(2)}) collective-permute-start(bf16[4,48,768]{2,1,0:T(8,128)(2,1)S(1)} %add_convert_fusion.1.refs_0_), channel_id=1, source_target_pairs={{0,2},{1,3},{2,0},{3,1},{4,6},{5,7},{6,4},{7,5},{8,10},{9,11},{10,... | collective-permute-start | bytes 884744 | tf_op jit(solution)/shard_map/ppermute | solution.py:643
  161.6 7.5 %collective-permute-start.21 = (bf16[4,48,384]{2,1,0:T(8,128)(2,1)}, bf16[4,48,384]{2,1,0:T(8,128)(2,1)S(1)}, u32[]{:S(2)}, u32[]{:S(2)}) collective-permute-start(bf16[4,48,384]{2,1,0:T(8,128)(2,1)} %get-tuple-element.127), channel_id=1, source_target_pairs={{0,4},{1,5},{2,6},{3,7},{4,0},{5,1},{6,2},{7,3},{8,12},{9,13},{10,... | collective-permute-start | bytes 442376 | tf_op jit(solution)/shard_map/ppermute | solution.py:643
  162.7 8.0 %collective-permute-start.22 = (bf16[4,48,384]{2,1,0:T(8,128)(2,1)}, bf16[4,48,384]{2,1,0:T(8,128)(2,1)S(1)}, u32[]{:S(2)}, u32[]{:S(2)}) collective-permute-start(bf16[4,48,384]{2,1,0:T(8,128)(2,1)} %get-tuple-element.128), channel_id=1, source_target_pairs={{0,6},{1,7},{2,4},{3,5},{4,2},{5,3},{6,0},{7,1},{8,14},{9,15},{10,... | collective-permute-start | bytes 442376 | tf_op jit(solution)/shard_map/ppermute | solution.py:643
  163.1 9.5 %collective-permute-start.20 = (bf16[4,48,384]{2,1,0:T(8,128)(2,1)}, bf16[4,48,384]{2,1,0:T(8,128)(2,1)S(1)}, u32[]{:S(2)}, u32[]{:S(2)}) collective-permute-start(bf16[4,48,384]{2,1,0:T(8,128)(2,1)} %get-tuple-element.126.refs_1_), channel_id=1, source_target_pairs={{0,2},{1,3},{2,0},{3,1},{4,6},{5,7},{6,4},{7,5},{8,10},{9,11},{10,... | collective-permute-start | bytes 442376 | tf_op jit(solution)/shard_map/ppermute | solution.py:643
  165.1 8.2 %copy-start.12 = (f32[4,48,384]{2,1,0:T(8,128)S(1)}, f32[4,48,384]{2,1,0:T(8,128)}, u32[]{:S(2)}) copy-start(f32[4,48,384]{2,1,0:T(8,128)} %get-tuple-element.125) | copy-start | bytes 884740
  175.4 4.5 %copy-start.19 = (bf16[1,48,1152]{2,1,0:T(8,128)(2,1)}, bf16[1,48,1152]{2,1,0:T(8,128)(2,1)S(1)}, u32[]{:S(2)}) copy-start(bf16[1,48,1152]{2,1,0:T(8,128)(2,1)S(1)} %get-tuple-element.173._) | copy-start | bytes 331780
  175.4 15.5 %collective-permute-start.25 = (bf16[1,48,1152]{2,1,0:T(8,128)(2,1)S(1)}, bf16[1,48,1152]{2,1,0:T(8,128)(2,1)S(1)}, u32[]{:S(2)}, u32[]{:S(2)}) collective-permute-start(bf16[1,48,1152]{2,1,0:T(8,128)(2,1)S(1)} %get-tuple-element.171), channel_id=1, source_target_pairs={{0,24},{1,25},{2,26},{3,27},{4,28},{5,29},{6,30},{7,31},{8,16},{9,... | collective-permute-start | bytes 331784 | tf_op jit(solution)/shard_map/ppermute | solution.py:643
  178.0 13.0 %collective-permute-start.24 = (bf16[1,48,1152]{2,1,0:T(8,128)(2,1)S(1)}, bf16[1,48,1152]{2,1,0:T(8,128)(2,1)S(1)}, u32[]{:S(2)}, u32[]{:S(2)}) collective-permute-start(bf16[1,48,1152]{2,1,0:T(8,128)(2,1)S(1)} %get-tuple-element.172), channel_id=1, source_target_pairs={{0,16},{1,17},{2,18},{3,19},{4,20},{5,21},{6,22},{7,23},{8,24},{9,... | collective-permute-start | bytes 331784 | tf_op jit(solution)/shard_map/ppermute | solution.py:643
  178.0 13.0 %collective-permute-start.23 = (bf16[1,48,1152]{2,1,0:T(8,128)(2,1)S(1)}, bf16[1,48,1152]{2,1,0:T(8,128)(2,1)S(1)}, u32[]{:S(2)}, u32[]{:S(2)}) collective-permute-start(bf16[1,48,1152]{2,1,0:T(8,128)(2,1)S(1)} %get-tuple-element.173._), channel_id=1, source_target_pairs={{0,8},{1,9},{2,10},{3,11},{4,12},{5,13},{6,14},{7,15},{8,0},{9,1},... | collective-permute-start | bytes 331784 | tf_op jit(solution)/shard_map/ppermute | solution.py:643
  188.5 25.0 %collective-permute-start.27 = (bf16[576,384]{1,0:T(8,128)(2,1)}, bf16[576,384]{1,0:T(8,128)(2,1)S(1)}, u32[]{:S(2)}, u32[]{:S(2)}) collective-permute-start(bf16[576,384]{1,0:T(8,128)(2,1)} %get-tuple-element.144), channel_id=1, source_target_pairs={{0,2},{1,3},{2,0},{3,1},{4,6},{5,7},{6,4},{7,5},{8,10},{9,11},{10,... | collective-permute-start | bytes 1327112 | tf_op jit(solution)/shard_map/ppermute | solution.py:643
  190.9 22.7 %collective-permute-start.28 = (bf16[576,384]{1,0:T(8,128)(2,1)}, bf16[576,384]{1,0:T(8,128)(2,1)S(1)}, u32[]{:S(2)}, u32[]{:S(2)}) collective-permute-start(bf16[576,384]{1,0:T(8,128)(2,1)} %get-tuple-element.145), channel_id=1, source_target_pairs={{0,3},{1,2},{2,1},{3,0},{4,7},{5,6},{6,5},{7,4},{8,11},{9,10},{10,... | collective-permute-start | bytes 1327112 | tf_op jit(solution)/shard_map/ppermute | solution.py:643
  194.2 19.4 %collective-permute-start.26 = (bf16[576,384]{1,0:T(8,128)(2,1)}, bf16[576,384]{1,0:T(8,128)(2,1)S(1)}, u32[]{:S(2)}, u32[]{:S(2)}) collective-permute-start(bf16[576,384]{1,0:T(8,128)(2,1)} %shard_map.346), channel_id=1, source_target_pairs={{0,1},{1,0},{2,3},{3,2},{4,5},{5,4},{6,7},{7,6},{8,9},{9,8},{10,11... | collective-permute-start | bytes 1327112 | tf_op jit(solution)/shard_map/ppermute | solution.py:643
  194.6 5.1 %collective-permute-start.31 = (f32[24,384]{1,0:T(8,128)}, f32[24,384]{1,0:T(8,128)S(1)}, u32[]{:S(2)}, u32[]{:S(2)}) collective-permute-start(f32[24,384]{1,0:T(8,128)} %get-tuple-element.148), channel_id=1, source_target_pairs={{0,12},{1,13},{2,14},{3,15},{4,8},{5,9},{6,10},{7,11},{8,4},{9,5},... | collective-permute-start | bytes 110600 | tf_op jit(solution)/shard_map/ppermute | solution.py:643
  195.2 5.5 %collective-permute-start.30 = (f32[24,384]{1,0:T(8,128)}, f32[24,384]{1,0:T(8,128)S(1)}, u32[]{:S(2)}, u32[]{:S(2)}) collective-permute-start(f32[24,384]{1,0:T(8,128)} %get-tuple-element.148), channel_id=1, source_target_pairs={{0,8},{1,9},{2,10},{3,11},{4,12},{5,13},{6,14},{7,15},{8,0},{9,1},... | collective-permute-start | bytes 110600 | tf_op jit(solution)/shard_map/ppermute | solution.py:643
  199.7 4.2 %collective-permute-start.29 = (f32[24,384]{1,0:T(8,128)}, f32[24,384]{1,0:T(8,128)S(1)}, u32[]{:S(2)}, u32[]{:S(2)}) collective-permute-start(f32[24,384]{1,0:T(8,128)} %get-tuple-element.148), channel_id=1, source_target_pairs={{0,4},{1,5},{2,6},{3,7},{4,0},{5,1},{6,2},{7,3},{8,12},{9,13},{10,... | collective-permute-start | bytes 110600 | tf_op jit(solution)/shard_map/ppermute | solution.py:643
  204.7 4.9 %copy-start.13 = (f32[24,384]{1,0:T(8,128)}, f32[24,384]{1,0:T(8,128)S(1)}, u32[]{:S(2)}) copy-start(f32[24,384]{1,0:T(8,128)S(1)} %add_add_fusion.refs_0_) | copy-start | bytes 110596
  204.7 4.9 %collective-permute-start.32 = (f32[24,384]{1,0:T(8,128)S(1)}, f32[24,384]{1,0:T(8,128)S(1)}, u32[]{:S(2)}, u32[]{:S(2)}) collective-permute-start(f32[24,384]{1,0:T(8,128)S(1)} %add_add_fusion.refs_0_), channel_id=1, source_target_pairs={{0,16},{1,17},{2,18},{3,19},{4,20},{5,21},{6,22},{7,23},{8,24},{9,... | collective-permute-start | bytes 110600 | tf_op jit(solution)/shard_map/ppermute | solution.py:643
  211.7 5.6 %collective-permute-start.35 = (f32[64,128]{1,0:T(8,128)}, f32[64,128]{1,0:T(8,128)S(1)}, u32[]{:S(2)}, u32[]{:S(2)}) collective-permute-start(f32[64,128]{1,0:T(8,128)} %get-tuple-element.150.refs_0_), channel_id=1, source_target_pairs={{0,3},{1,2},{2,1},{3,0},{4,7},{5,6},{6,5},{7,4},{8,11},{9,10},{10,... | collective-permute-start | bytes 98312 | tf_op jit(solution)/shard_map/ppermute | solution.py:643
  211.7 5.6 %collective-permute-start.34 = (f32[64,128]{1,0:T(8,128)}, f32[64,128]{1,0:T(8,128)S(1)}, u32[]{:S(2)}, u32[]{:S(2)}) collective-permute-start(f32[64,128]{1,0:T(8,128)} %get-tuple-element.150.refs_0_), channel_id=1, source_target_pairs={{0,2},{1,3},{2,0},{3,1},{4,6},{5,7},{6,4},{7,5},{8,10},{9,11},{10,... | collective-permute-start | bytes 98312 | tf_op jit(solution)/shard_map/ppermute | solution.py:643
  213.5 3.9 %collective-permute-start.33 = (f32[64,128]{1,0:T(8,128)}, f32[64,128]{1,0:T(8,128)S(1)}, u32[]{:S(2)}, u32[]{:S(2)}) collective-permute-start(f32[64,128]{1,0:T(8,128)} %get-tuple-element.150.refs_0_), channel_id=1, source_target_pairs={{0,1},{1,0},{2,3},{3,2},{4,5},{5,4},{6,7},{7,6},{8,9},{9,8},{10,11... | collective-permute-start | bytes 98312 | tf_op jit(solution)/shard_map/ppermute | solution.py:643
  (21 other events, 16.8 us)
where the time goes:
time: 221 us; the launch traced here: 220 us
  Pallas kernels  130 us (59%)
  starting transfers between devices  45.3 us (20%)
  waiting for transfers between devices  29.6 us (13%)
  local copies, waits for them, and re-layouts  10 us (5%)
  other arithmetic  4.91 us (2%)
    pallas_call x8, Pallas kernels, call_kernel(): pl.pallas_call(functools.partial(kernel, *statics), grid=(steps,), in_spe...  104 us
    ppermute x36, starting transfers between devices, permute(): lax.ppermute(array, ('dp', 'group'), [(rank, rank ^ mask) for rank in ran...  38 us
    ppermute x36, waiting for transfers between devices, permute(): lax.ppermute(array, ('dp', 'group'), [(rank, rank ^ mask) for rank in ran...  29.5 us
    unnamed x62, local copies, waits for them, and re-layouts  9.98 us
    all_to_all x2, starting transfers between devices, to_group(): lax.all_to_all(parts, 'group', split_axis=0, concat_axis=0, tiled=True)  7.29 us
    pallas_call x2, Pallas kernels, settle(): small(functools.partial(settle_kernel, spread), in_specs=[in_smem] + [in_...  5.55 us
  transfers between devices with their start and end apart: 38, of which 11 were waited for; matrix products, arithmetic and copies ran while one was open for 2% of the time, Pallas kernels for 35%

commit v1 on v0

--- a/solution.py
+++ b/solution.py
@@ -96,7 +96,7 @@
 
 
 PER_STEP = 4
-FF_PER_STEP = 2
+FF_PER_STEP = 4
 SLICE = 48
 FF_CHUNK = 256
 vmem_bytes = 60 * 1024 * 1024
@@ -245,12 +245,12 @@
         x = x_ref[pl.ds(pl.multiple_of(base + rows.start, SLICE), SLICE), :].astype(jnp.float32)
         unit, _ = normal_form(x)
         normed_ref[rows, :] = (unit * vectors_ref[0:1] + vectors_ref[1:2]).astype(jnp.bfloat16)
-    for part in range(3):
-        cols = slice(part * width, (part + 1) * width)
-        projected = dot(normed_ref[...], w_qkv_ref[:, cols])
-        if part != 1:
-            row = 2 if part == 0 else 3
-            projected = projected + vectors_ref[row : row + 1]
+    shift = jnp.concatenate(
+        [vectors_ref[2:3], jnp.zeros((1, width), jnp.float32), vectors_ref[3:4]], axis=1
+    )
+    for start in range(0, 3 * width, 512):
+        cols = slice(start, min(start + 512, 3 * width))
+        projected = dot(normed_ref[...], w_qkv_ref[:, cols]) + shift[:, cols]
         qkv_ref[:, cols] = projected.astype(jnp.bfloat16)
 
     pairs = width // (2 * HEAD_DIM)
@@ -701,6 +701,12 @@
             put(row, col, packed_ref[gathered_place((row * spread + col) ^ place, count)])
 
 
+def unpack_in_order(blocks_ref, put, dp_size, spread):
+    for row in range(dp_size):
+        for col in range(spread):
+            put(row, col, blocks_ref[row * spread + col])
+
+
 def pack(place_ref, take, keep_ref, leave_ref, dp_size, spread):
     place = place_ref[0]
     odd = (place & 1) == 1
@@ -1086,15 +1092,6 @@
 
 def after_kernel(*refs):
     pass
-
-
-def add_kernel(count, keep_ref, arrived_ref, *refs):
-    parts = refs[-count:]
-    size = parts[0].shape[0]
-    for at, part_ref in enumerate(parts):
-        rows = slice(at * size, (at + 1) * size)
-        total = keep_ref[rows].astype(jnp.float32) + arrived_ref[rows].astype(jnp.float32)
-        part_ref[...] = total.astype(part_ref.dtype)
 
 
 def gradient_kernel(count, *refs):
@@ -1278,9 +1275,12 @@
             out_shape=jax.ShapeDtypeStruct((count, *parts[0].shape[1:]), low),
         )(*parts, *awaited)
 
-    def gather_rest(held):
+    def gather_rest(held, awaited=None):
         arrived = permute(held, across_x)
-        return [held, arrived, permute(held, core_bits[0]), permute(arrived, core_bits[0])]
+        leaving = [held, arrived]
+        if awaited is not None:
+            leaving = [after(part, [awaited]) for part in leaving]
+        return leaving + [permute(part, core_bits[0]) for part in leaving]
 
     first_far = join(gather_far(first_pair))
     upstream = to_images(cotangent_cut)
@@ -1317,17 +1317,17 @@
         (place, inputs, *first_blocks, keep_mask, vectors),
         attention_flops,
     )
-    second_blocks = gather_rest(join(second_far, attention[:1]))
-    for first_step, count in ((1, steps - 2), (steps - 1, 1)):
-        attention = call_kernel(
-            next_attention_kernel, (first_step * PER_STEP,), count,
-            [block] + [None] * 4 + ["await"] * len(attention),
-            attention_outs, attention_scratches,
-            (x, keep_mask, w_qkv, w_proj, vectors, *attention),
-            attention_flops * count, first_step=first_step,
-            aliases={5 + at: at for at in range(len(attention))},
-        )
+    second_joined = join(second_far, attention[:1])
+    attention = call_kernel(
+        next_attention_kernel, (PER_STEP,), steps - 1,
+        [block] + [None] * 4 + ["await"] * len(attention),
+        attention_outs, attention_scratches,
+        (x, keep_mask, w_qkv, w_proj, vectors, *attention),
+        attention_flops * (steps - 1), first_step=1,
+        aliases={5 + at: at for at in range(len(attention))},
+    )
     qkv, probs, attended, middle = attention
+    second_blocks = gather_rest(second_joined, middle)
     piece = ((slots * images, width), low, None)
     ff_rows = FF_PER_STEP * length
     ff_block = (ff_rows, width)
@@ -1371,16 +1371,6 @@
     )
     d_middle, d_attended, ff_keep, ff_leave, proj_total, ff_sums, up_sums = results[spread:]
 
-    def add_parts(count, keep, arrived, awaited):
-        part = (keep.shape[0] // count, *keep.shape[1:])
-        return small(
-            functools.partial(add_kernel, count),
-            in_specs=[in_vmem] * 2 + [anywhere] * len(awaited),
-            out_specs=[in_vmem] * count,
-            out_shape=[jax.ShapeDtypeStruct(part, high)]
-            + [jax.ShapeDtypeStruct(part, low)] * (count - 1),
-        )(keep, arrived, *awaited)
-
     ff_first = permute(ff_leave, core_bits[0])
     ff_count = half // 2
     ff_next = add_wide(ff_keep[ff_count:], ff_first[ff_count:]).astype(low)
@@ -1396,7 +1386,7 @@
         (place, x, qkv, probs, d_attended, vectors, proj_total, ff_next),
         2 * total * width * 3 * width + 16 * total * length * width,
     )
-    qkv_arrived = permute(after(qkv_leave, output_parts[1:]), core_bits[0])
+    qkv_arrived = permute(after(qkv_leave, output_parts[1:] + [ff_arrived]), core_bits[0])
     input_flops = 2 * total * width * 3 * width
     input_ins = [block, wide_rows, block, None, None, None]
     input_outs = [((total, width), low, block), ((8, width), high, None)]
@@ -1409,7 +1399,11 @@
         ff_keep[ff_quarter:ff_count], ff_first[ff_quarter:ff_count], ff_arrived[ff_quarter:]
     ).astype(low)
     ff_last_arrived = permute(ff_last, across_y)
-    qkv_held, *leaving = add_parts(4, qkv_keep, qkv_arrived, [ff_last])
+    qkv_held = add_wide(qkv_keep, qkv_arrived)
+    leaving = [
+        qkv_held[at : at + ff_quarter].astype(low) for at in range(ff_quarter, half, ff_quarter)
+    ]
+    qkv_held = qkv_held[:ff_quarter]
     qkv_parts = [permute(part, mask) for part, mask in zip(leaving, direct_masks(near_bits))]
     d_input, att_sums = call_kernel(
         first_input_kernel, (length,), 1, input_ins + ["await"] * 2, input_outs, [scratch(step_rows, width)],

time: 221 us -> 213 us (0.964)
  Pallas kernels: 130 us -> 121 us
    pallas_call x8 -> x7, Pallas kernels: 104 us -> 98.1 us  [call_kernel(): pl.pallas_call(functools.partial(kernel, *statics), grid=(steps,), in_spe...]
    unnamed x62 -> x66, local copies, waits for them, and re-layouts: 9.98 us -> 9.73 us
  transfers between devices with their start and end apart: 38 -> 38, of which waited for: 11 -> 13; matrix products, arithmetic and copies ran while one was open for 2% -> 3% of each run, Pallas kernels for 35% -> 34%
where the time goes in v1:
time: 213 us; the launch traced here: 212 us
  Pallas kernels  121 us (57%)
  starting transfers between devices  44.9 us (21%)
  waiting for transfers between devices  28.8 us (14%)
  local copies, waits for them, and re-layouts  9.8 us (5%)
  other arithmetic  5.72 us (3%)
    pallas_call x7, Pallas kernels, call_kernel(): pl.pallas_call(functools.partial(kernel, *statics), grid=(steps,), in_spe...  98.1 us
    ppermute x36, starting transfers between devices, permute(): lax.ppermute(array, ('dp', 'group'), [(rank, rank ^ mask) for rank in ran...  37.6 us
    ppermute x36, waiting for transfers between devices, permute(): lax.ppermute(array, ('dp', 'group'), [(rank, rank ^ mask) for rank in ran...  28.7 us
    unnamed x66, local copies, waits for them, and re-layouts  9.73 us
    all_to_all x2, starting transfers between devices, to_group(): lax.all_to_all(parts, 'group', split_axis=0, concat_axis=0, tiled=True)  7.29 us
    pallas_call x2, Pallas kernels, settle(): small(functools.partial(settle_kernel, spread), in_specs=[in_smem] + [in_...  5.55 us
  transfers between devices with their start and end apart: 38, of which 13 were waited for; matrix products, arithmetic and copies ran while one was open for 3% of the time, Pallas kernels for 34%

profile of v1, /device:TPU:0, one launch (start us, length us, event | category | flops | bytes accessed | tf_op | source)
XLA Modules:
  0.0 211.7 jit_solution(13088347283891845408)
XLA Ops:
  0.7 1.7 shard_map.329.own_ref
  2.4 3.0 %collective-permute-start = (bf16[48,1152]{1,0:T(8,128)(2,1)}, bf16[48,1152]{1,0:T(8,128)(2,1)S(1)}, u32[]{:S(2)}, u32[]{:S(2)}) collective-permute-start(bf16[48,1152]{1,0:T(8,128)(2,1)} %shard_map.329.own_ref), channel_id=1, source_target_pairs={{0,2},{1,3},{2,0},{3,1},{4,6},{5,7},{6,4},{7,5},{8,10},{9,11},{10,... | collective-permute-start | bytes 331784 | tf_op jit(solution)/shard_map/ppermute | solution.py:643
  5.3 2.8 %shard_map.328._ = bf16[4,36,16,384]{3,2,1,0:T(8,128)(2,1)} custom-call(bf16[36,64,384]{2,1,0:T(8,128)(2,1)} %bitcast.16), custom_call_target="tpu_custom_call" | custom-call | tf_op jit(solution)/shard_map/pallas_call | solution.py:1255
  9.3 2.9 %shard_map.330 = (bf16[4,36,16,384]{3,2,1,0:T(8,128)(2,1)}, bf16[2,48,384]{2,1,0:T(8,128)(2,1)}, bf16[2,48,768]{2,1,0:T(8,128)(2,1)}) custom-call(bf16[36,64,384]{2,1,0:T(8,128)(2,1)} %bitcast.15, bf16[48,1152]{1,0:T(8,128)(2,1)} %shard_map.329.own_ref, bf16[48,1152]{1,0:T(8,128)(2,1)} %copy-done.18, bf16[4,36,16,384]{3,2,1,0:T(8,128)(2,1)} %shard_map.328._), custom_call_target="tpu_custom_call" | custom-call | tf_op jit(solution)/shard_map/pallas_call | solution.py:1256
  12.2 3.7 %all-to-all-start.1 = ((bf16[4,36,16,384]{3,2,1,0:T(8,128)(2,1)}), bf16[4,36,16,384]{3,2,1,0:T(8,128)(2,1)S(1)}, u32[]{:S(2)}, u32[]{:S(2)}) async-start(bf16[4,36,16,384]{3,2,1,0:T(8,128)(2,1)} %get-tuple-element.89), calls=%async_computation.1 | async-start | bytes 3538944 | tf_op jit(solution)/shard_map/all_to_all | solution.py:1229
  15.9 3.9 %collective-permute-start.6 = (bf16[2,48,384]{2,1,0:T(8,128)(2,1)S(1)}, bf16[2,48,384]{2,1,0:T(8,128)(2,1)S(1)}, u32[]{:S(2)}, u32[]{:S(2)}) collective-permute-start(bf16[2,48,384]{2,1,0:T(8,128)(2,1)S(1)} %copy-done.23), channel_id=1, source_target_pairs={{0,24},{1,25},{2,26},{3,27},{4,28},{5,29},{6,30},{7,31},{8,16},{9,... | collective-permute-start | bytes 221192 | tf_op jit(solution)/shard_map/ppermute | solution.py:643
  20.4 2.5 %collective-permute-done.6.refs_3_ = bf16[2,48,384]{2,1,0:T(8,128)(2,1)S(1)} collective-permute-done((bf16[2,48,384]{2,1,0:T(8,128)(2,1)S(1)}, bf16[2,48,384]{2,1,0:T(8,128)(2,1)S(1)}, u32[]{:S(2)}, u32[]{:S(2)}) %collective-permute-start.6) | collective-permute-done | bytes 73760 | tf_op jit(solution)/shard_map/ppermute | solution.py:643
  23.0 3.6 %collective-permute-done.5.refs_2_ = bf16[2,48,384]{2,1,0:T(8,128)(2,1)S(1)} collective-permute-done((bf16[2,48,384]{2,1,0:T(8,128)(2,1)S(1)}, bf16[2,48,384]{2,1,0:T(8,128)(2,1)S(1)}, u32[]{:S(2)}, u32[]{:S(2)}) %collective-permute-start.5) | collective-permute-done | bytes 73760 | tf_op jit(solution)/shard_map/ppermute | solution.py:643
  27.8 1.8 shard_map.331.refs_0_
  29.6 1.5 collective-permute-start.7
  31.1 7.4 %collective-permute-done.7.refs_1_ = bf16[8,48,384]{2,1,0:T(8,128)(2,1)} collective-permute-done((bf16[8,48,384]{2,1,0:T(8,128)(2,1)}, bf16[8,48,384]{2,1,0:T(8,128)(2,1)}, u32[]{:S(2)}, u32[]{:S(2)}) %collective-permute-start.7) | collective-permute-done | bytes 294944 | tf_op jit(solution)/shard_map/ppermute | solution.py:643
  38.4 2.5 %collective-permute-start.3 = (bf16[2,48,768]{2,1,0:T(8,128)(2,1)}, bf16[2,48,768]{2,1,0:T(8,128)(2,1)}, u32[]{:S(2)}, u32[]{:S(2)}) collective-permute-start(bf16[2,48,768]{2,1,0:T(8,128)(2,1)} %get-tuple-element.88.refs_0_), channel_id=1, source_target_pairs={{0,24},{1,25},{2,26},{3,27},{4,28},{5,29},{6,30},{7,31},{8,16},{9,... | collective-permute-start | bytes 442376 | tf_op jit(solution)/shard_map/ppermute | solution.py:643
  40.9 1.9 collective-permute-start.1
  42.8 1.2 copy-done.3
  44.0 3.6 %all-to-all-start = ((bf16[4,36,16,384]{3,2,1,0:T(8,128)(2,1)}), bf16[4,36,16,384]{3,2,1,0:T(8,128)(2,1)S(1)}, u32[]{:S(2)}, u32[]{:S(2)}) async-start(bf16[4,36,16,384]{3,2,1,0:T(8,128)(2,1)} %shard_map.328._), calls=%async_computation | async-start | bytes 3538944 | tf_op jit(solution)/shard_map/all_to_all | solution.py:1229
  47.7 10.5 %shard_map.332 = (bf16[2304,1152]{1,0:T(8,128)(2,1)}, bf16[16,3,144,288]{3,2,1,0:T(8,128)(2,1)}, bf16[2304,384]{1,0:T(8,128)(2,1)}, f32[2304,384]{1,0:T(8,128)},...) custom-call(s32[1]{0:T(128)} %bitcast.place_ref, ...), custom_call_target="tpu_custom_call" | custom-call | flops 7474249728 | bytes 21703684 | tf_op jit(solution)/shard_map/pallas_call | solution.py:535
  58.1 2.0 shard_map.333.refs_0_
  60.1 1.5 collective-permute-start.10
  61.6 12.3 %shard_map.334 = (bf16[2304,1152]{1,0:T(8,128)(2,1)}, bf16[16,3,144,288]{3,2,1,0:T(8,128)(2,1)}, bf16[2304,384]{1,0:T(8,128)(2,1)}, f32[2304,384]{1,0:T(8,128)}) custom-call(bf16[2304,384]{1,0:T(8,128)(2,1)} %get-tuple-element.92.x_ref, s32[16,144]{1,0:T(8,128)} %keep_ref.1, ...), custom_call_target="tpu_custom_call", output_to_operand_aliasing={{0}: (5, {}), {1}: (6, {}), {2}: (7, {}), {3}: (8, {})} | custom-call | flops 22422749184 | bytes 32173056 | tf_op jit(solution)/shard_map/pallas_call | solution.py:535
  73.9 2.1 %collective-permute-done.10.refs_0_ = bf16[8,48,768]{2,1,0:T(8,128)(2,1)S(1)} collective-permute-done((bf16[8,48,768]{2,1,0:T(8,128)(2,1)}, bf16[8,48,768]{2,1,0:T(8,128)(2,1)S(1)}, u32[]{:S(2)}, u32[]{:S(2)}) %collective-permute-start.10) | collective-permute-done | bytes 589856 | tf_op jit(solution)/shard_map/ppermute | solution.py:643
  77.9 1.1 collective-permute-done.12.refs_4_
  80.7 42.0 %shard_map.337 = (bf16[576,384]{1,0:T(8,128)(2,1)}, bf16[576,384]{1,0:T(8,128)(2,1)}, bf16[576,384]{1,0:T(8,128)(2,1)}, bf16[576,384]{1,0:T(8,128)(2,1)}, f32[23...) custom-call(s32[1]{0:T(128)} %bitcast.place_ref, ...), custom_call_target="tpu_custom_call" | custom-call | flops 141331267584 | bytes 19795972 | tf_op jit(solution)/shard_map/pallas_call | solution.py:535
  123.3 1.7 collective-permute-start.17
  125.8 1.6 add_convert_fusion._
  127.5 1.6 collective-permute-start.14
  129.0 16.9 %shard_map.338 = (bf16[2304,1152]{1,0:T(8,128)(2,1)}, bf16[16,48,384]{2,1,0:T(8,128)(2,1)}, bf16[16,48,384]{2,1,0:T(8,128)(2,1)}, f32[8,384]{1,0:T(8,128)}) custom-call(s32[1]{0:T(128)} %bitcast.place_ref, bf16[2304,384]{1,0:T(8,128)(2,1)} %get-tuple-element.92.x_ref, bf16[2304,1152]{1,0:T(8,128)(2,1)} %get-tuple-element.104.qkv_ref, ...), custom_call_target="tpu_custom_call" | custom-call | flops 32614907904 | bytes 20527108 | tf_op jit(solution)/shard_map/pallas_call | solution.py:535
  145.9 1.3 add_convert_fusion.1
  147.2 1.7 collective-permute-start.15
  150.0 4.0 %shard_map.340 = (bf16[2304,384]{1,0:T(8,128)(2,1)}, f32[8,384]{1,0:T(8,128)}) custom-call(bf16[2304,384]{1,0:T(8,128)(2,1)} %get-tuple-element.92.x_ref, bf16[2304,1152]{1,0:T(8,128)(2,1)} %get-tuple-element.113.d_projected_ref, f32[2304,384]{1,0:T(8,128)} %get-tuple-element.114.d_middle_ref, bf16[1152,384]{1,0:T(8,128)(2,1)} %get-tuple-element.115.qkv_t_ref, ...), custom_call_target="tpu_custom_call" | custom-call | flops 4076863488 | bytes 13314048 | tf_op jit(solution)/shard_map/pallas_call | solution.py:535
  154.0 2.0 collective-permute-done.15
  156.1 1.1 convert_add_fusion.1
  157.4 2.2 %collective-permute-start.22 = (bf16[4,48,384]{2,1,0:T(8,128)(2,1)S(1)}, bf16[4,48,384]{2,1,0:T(8,128)(2,1)S(1)}, u32[]{:S(2)}, u32[]{:S(2)}) collective-permute-start(bf16[4,48,384]{2,1,0:T(8,128)(2,1)S(1)} %get-tuple-element.158), channel_id=1, source_target_pairs={{0,6},{1,7},{2,4},{3,5},{4,2},{5,3},{6,0},{7,1},{8,14},{9,15},{10,... | collective-permute-start | bytes 442376 | tf_op jit(solution)/shard_map/ppermute | solution.py:643
  161.0 3.9 %shard_map.341 = (bf16[2304,384]{1,0:T(8,128)(2,1)}, f32[8,384]{1,0:T(8,128)}) custom-call(bf16[2304,384]{1,0:T(8,128)(2,1)} %get-tuple-element.92.x_ref, bf16[2304,1152]{1,0:T(8,128)(2,1)} %get-tuple-element.113.d_projected_ref, f32[2304,384]{1,0:T(8,128)} %get-tuple-element.114.d_middle_ref, ...), custom_call_target="tpu_custom_call", output_to_operand_aliasing={{0}: (6, {})} | custom-call | flops 4076863488 | bytes 15230976 | tf_op jit(solution)/shard_map/pallas_call | solution.py:535
  164.9 1.6 collective-permute-done.21
  166.6 2.5 %collective-permute-start.25 = (bf16[1,48,1152]{2,1,0:T(8,128)(2,1)S(1)}, bf16[1,48,1152]{2,1,0:T(8,128)(2,1)S(1)}, u32[]{:S(2)}, u32[]{:S(2)}) collective-permute-start(bf16[1,48,1152]{2,1,0:T(8,128)(2,1)S(1)} %get-tuple-element.160), channel_id=1, source_target_pairs={{0,24},{1,25},{2,26},{3,27},{4,28},{5,29},{6,30},{7,31},{8,16},{9,... | collective-permute-start | bytes 331784 | tf_op jit(solution)/shard_map/ppermute | solution.py:643
  169.2 1.9 collective-permute-start.23
  171.1 8.6 %shard_map.342 = (bf16[576,384]{1,0:T(8,128)(2,1)}, bf16[576,384]{1,0:T(8,128)(2,1)}, bf16[576,384]{1,0:T(8,128)(2,1)}, bf16[576,384]{1,0:T(8,128)(2,1)}, f32[8,384]{1,0:T(8,128)}) custom-call(s32[1]{0:T(128)} %bitcast.place_ref, bf16[2304,384]{1,0:T(8,128)(2,1)} %get-tuple-element.92.x_ref, bf16[2304,1152]{1,0:T(8,128)(2,1)} %get-tuple-element.113.d_projected_ref, ...), custom_call_target="tpu_custom_call" | custom-call | flops 8153726976 | bytes 15194116 | tf_op jit(solution)/shard_map/pallas_call | solution.py:535
  179.7 1.5 collective-permute-start.27
  182.6 2.6 %shard_map.343 = (f32[48,288]{1,0:T(8,128)}, f32[48,96]{1,0:T(8,128)}, f32[48,384]{1,0:T(8,128)}, f32[192,96]{1,0:T(8,128)}, f32[8,48]{1,0:T(8,128)}, /*index=5*/f32[24,384]{1,0:T(8,128)}) custom-call(f32[1,48,1152]{2,1,0:T(8,128)} %fusion.3.refs_0_, bf16[1,48,1152]{2,1,0:T(8,128)(2,1)} %copy-done.21, bf16[1,48,1152]{2,1,0:T(8,128)(2,1)} %copy-done.20, ...), custom_call_target="tpu_custom_call" | custom-call | tf_op jit(solution)/shard_map/pallas_call | solution.py:1438
  186.8 1.9 collective-permute-start.30
  188.7 2.3 %collective-permute-done.31 = f32[24,384]{1,0:T(8,128)S(1)} collective-permute-done((f32[24,384]{1,0:T(8,128)}, f32[24,384]{1,0:T(8,128)S(1)}, u32[]{:S(2)}, u32[]{:S(2)}) %collective-permute-start.31) | collective-permute-done | bytes 36896 | tf_op jit(solution)/shard_map/ppermute | solution.py:643
  190.9 1.3 collective-permute-start.29
  192.3 2.8 %collective-permute-done.29 = f32[24,384]{1,0:T(8,128)S(1)} collective-permute-done((f32[24,384]{1,0:T(8,128)}, f32[24,384]{1,0:T(8,128)S(1)}, u32[]{:S(2)}, u32[]{:S(2)}) %collective-permute-start.29) | collective-permute-done | bytes 36896 | tf_op jit(solution)/shard_map/ppermute | solution.py:643
  197.0 2.8 %shard_map.345 = (bf16[36,64,384]{2,1,0:T(8,128)(2,1)}, f32[8,128]{1,0:T(8,128)}) custom-call(s32[1]{0:T(128)} %bitcast.place_ref, bf16[36,16,384]{2,1,0:T(8,128)(2,1)} %bitcast.19, bf16[36,16,384]{2,1,0:T(8,128)(2,1)} %bitcast.20, bf16[36,16,384]{2,1,0:T(8,128)(2,1)} %bitcast.21, bf16[36,16,384]{2,1,0:T(8,128)(2,1)} %bitcast.22), custom_call_target="tpu_custom_call" | custom-call | tf_op jit(solution)/shard_map/pallas_call | solution.py:1239
  201.5 1.5 shard_map.348
  203.0 1.5 collective-permute-start.34
  205.8 2.8 %shard_map.347 = (bf16[36,64,384]{2,1,0:T(8,128)(2,1)}, f32[8,128]{1,0:T(8,128)}) custom-call(s32[1]{0:T(128)} %bitcast.place_ref, bf16[36,16,384]{2,1,0:T(8,128)(2,1)} %bitcast.23, bf16[36,16,384]{2,1,0:T(8,128)(2,1)} %bitcast.26, bf16[36,16,384]{2,1,0:T(8,128)(2,1)} %bitcast.24, bf16[36,16,384]{2,1,0:T(8,128)(2,1)} %bitcast.25), custom_call_target="tpu_custom_call" | custom-call | tf_op jit(solution)/shard_map/pallas_call | solution.py:1239
  209.2 2.3 %shard_map.349 = (f32[48,288]{1,0:T(8,128)}, f32[48,96]{1,0:T(8,128)}, f32[48,384]{1,0:T(8,128)}, f32[192,96]{1,0:T(8,128)}, f32[288]{0:T(512)}, /*index=5*/f32[...) custom-call(f32[64,128]{1,0:T(8,128)} %get-tuple-element.134.refs_0_, ...), custom_call_target="tpu_custom_call" | custom-call | tf_op jit(solution)/shard_map/pallas_call | solution.py:1460
  (126 shorter events, 19.3 us)
Async XLA Ops:
  2.4 6.2 %collective-permute-start = (bf16[48,1152]{1,0:T(8,128)(2,1)}, bf16[48,1152]{1,0:T(8,128)(2,1)S(1)}, u32[]{:S(2)}, u32[]{:S(2)}) collective-permute-start(bf16[48,1152]{1,0:T(8,128)(2,1)} %shard_map.329.own_ref), channel_id=1, source_target_pairs={{0,2},{1,3},{2,0},{3,1},{4,6},{5,7},{6,4},{7,5},{8,10},{9,11},{10,... | collective-permute-start | bytes 331784 | tf_op jit(solution)/shard_map/ppermute | solution.py:643
  12.2 3.7 %copy-start.23 = (bf16[2,48,384]{2,1,0:T(8,128)(2,1)S(1)}, bf16[2,48,384]{2,1,0:T(8,128)(2,1)}, u32[]{:S(2)}) copy-start(bf16[2,48,384]{2,1,0:T(8,128)(2,1)} %get-tuple-element.90.refs_0_) | copy-start | bytes 221188
  12.2 30.7 %all-to-all-start.1 = ((bf16[4,36,16,384]{3,2,1,0:T(8,128)(2,1)}), bf16[4,36,16,384]{3,2,1,0:T(8,128)(2,1)S(1)}, u32[]{:S(2)}, u32[]{:S(2)}) async-start(bf16[4,36,16,384]{3,2,1,0:T(8,128)(2,1)} %get-tuple-element.89), calls=%async_computation.1 | async-start | bytes 3538944 | tf_op jit(solution)/shard_map/all_to_all | solution.py:1229
  15.9 7.1 %collective-permute-start.6 = (bf16[2,48,384]{2,1,0:T(8,128)(2,1)S(1)}, bf16[2,48,384]{2,1,0:T(8,128)(2,1)S(1)}, u32[]{:S(2)}, u32[]{:S(2)}) collective-permute-start(bf16[2,48,384]{2,1,0:T(8,128)(2,1)S(1)} %copy-done.23), channel_id=1, source_target_pairs={{0,24},{1,25},{2,26},{3,27},{4,28},{5,29},{6,30},{7,31},{8,16},{9,... | collective-permute-start | bytes 221192 | tf_op jit(solution)/shard_map/ppermute | solution.py:643
  19.8 6.8 %collective-permute-start.5 = (bf16[2,48,384]{2,1,0:T(8,128)(2,1)S(1)}, bf16[2,48,384]{2,1,0:T(8,128)(2,1)S(1)}, u32[]{:S(2)}, u32[]{:S(2)}) collective-permute-start(bf16[2,48,384]{2,1,0:T(8,128)(2,1)S(1)} %copy-done.23), channel_id=1, source_target_pairs={{0,16},{1,17},{2,18},{3,19},{4,20},{5,21},{6,22},{7,23},{8,24},{9,... | collective-permute-start | bytes 221192 | tf_op jit(solution)/shard_map/ppermute | solution.py:643
  19.8 6.8 %collective-permute-start.4 = (bf16[2,48,384]{2,1,0:T(8,128)(2,1)S(1)}, bf16[2,48,384]{2,1,0:T(8,128)(2,1)S(1)}, u32[]{:S(2)}, u32[]{:S(2)}) collective-permute-start(bf16[2,48,384]{2,1,0:T(8,128)(2,1)S(1)} %copy-done.23), channel_id=1, source_target_pairs={{0,8},{1,9},{2,10},{3,11},{4,12},{5,13},{6,14},{7,15},{8,0},{9,1},... | collective-permute-start | bytes 221192 | tf_op jit(solution)/shard_map/ppermute | solution.py:643
  23.0 3.6 %copy-start.24 = (bf16[2,48,384]{2,1,0:T(8,128)(2,1)}, bf16[2,48,384]{2,1,0:T(8,128)(2,1)S(1)}, u32[]{:S(2)}) copy-start(bf16[2,48,384]{2,1,0:T(8,128)(2,1)S(1)} %collective-permute-done.6.refs_3_) | copy-start | bytes 221188
  29.6 8.9 %collective-permute-start.7 = (bf16[8,48,384]{2,1,0:T(8,128)(2,1)}, bf16[8,48,384]{2,1,0:T(8,128)(2,1)}, u32[]{:S(2)}, u32[]{:S(2)}) collective-permute-start(bf16[8,48,384]{2,1,0:T(8,128)(2,1)} %shard_map.331.refs_0_), channel_id=1, source_target_pairs={{0,4},{1,5},{2,6},{3,7},{4,0},{5,1},{6,2},{7,3},{8,12},{9,13},{10,... | collective-permute-start | bytes 884744 | tf_op jit(solution)/shard_map/ppermute | solution.py:643
  31.1 16.6 %collective-permute-start.8 = (bf16[8,48,384]{2,1,0:T(8,128)(2,1)}, bf16[8,48,384]{2,1,0:T(8,128)(2,1)}, u32[]{:S(2)}, u32[]{:S(2)}) collective-permute-start(bf16[8,48,384]{2,1,0:T(8,128)(2,1)} %shard_map.331.refs_0_), channel_id=1, source_target_pairs={{0,1},{1,0},{2,3},{3,2},{4,5},{5,4},{6,7},{7,6},{8,9},{9,8},{10,11... | collective-permute-start | bytes 884744 | tf_op jit(solution)/shard_map/ppermute | solution.py:643
  38.4 9.2 %collective-permute-start.9 = (bf16[8,48,384]{2,1,0:T(8,128)(2,1)}, bf16[8,48,384]{2,1,0:T(8,128)(2,1)}, u32[]{:S(2)}, u32[]{:S(2)}) collective-permute-start(bf16[8,48,384]{2,1,0:T(8,128)(2,1)} %collective-permute-done.7.refs_1_), channel_id=1, source_target_pairs={{0,1},{1,0},{2,3},{3,2},{4,5},{5,4},{6,7},{7,6},{8,9},{9,8},{10,11... | collective-permute-start | bytes 884744 | tf_op jit(solution)/shard_map/ppermute | solution.py:643
  38.4 19.7 %collective-permute-start.3 = (bf16[2,48,768]{2,1,0:T(8,128)(2,1)}, bf16[2,48,768]{2,1,0:T(8,128)(2,1)}, u32[]{:S(2)}, u32[]{:S(2)}) collective-permute-start(bf16[2,48,768]{2,1,0:T(8,128)(2,1)} %get-tuple-element.88.refs_0_), channel_id=1, source_target_pairs={{0,24},{1,25},{2,26},{3,27},{4,28},{5,29},{6,30},{7,31},{8,16},{9,... | collective-permute-start | bytes 442376 | tf_op jit(solution)/shard_map/ppermute | solution.py:643
  40.9 17.2 %collective-permute-start.2 = (bf16[2,48,768]{2,1,0:T(8,128)(2,1)}, bf16[2,48,768]{2,1,0:T(8,128)(2,1)}, u32[]{:S(2)}, u32[]{:S(2)}) collective-permute-start(bf16[2,48,768]{2,1,0:T(8,128)(2,1)} %get-tuple-element.88.refs_0_), channel_id=1, source_target_pairs={{0,16},{1,17},{2,18},{3,19},{4,20},{5,21},{6,22},{7,23},{8,24},{9,... | collective-permute-start | bytes 442376 | tf_op jit(solution)/shard_map/ppermute | solution.py:643
  40.9 17.2 %collective-permute-start.1 = (bf16[2,48,768]{2,1,0:T(8,128)(2,1)}, bf16[2,48,768]{2,1,0:T(8,128)(2,1)}, u32[]{:S(2)}, u32[]{:S(2)}) collective-permute-start(bf16[2,48,768]{2,1,0:T(8,128)(2,1)} %get-tuple-element.88.refs_0_), channel_id=1, source_target_pairs={{0,8},{1,9},{2,10},{3,11},{4,12},{5,13},{6,14},{7,15},{8,0},{9,1},... | collective-permute-start | bytes 442376 | tf_op jit(solution)/shard_map/ppermute | solution.py:643
  44.0 33.9 %all-to-all-start = ((bf16[4,36,16,384]{3,2,1,0:T(8,128)(2,1)}), bf16[4,36,16,384]{3,2,1,0:T(8,128)(2,1)S(1)}, u32[]{:S(2)}, u32[]{:S(2)}) async-start(bf16[4,36,16,384]{3,2,1,0:T(8,128)(2,1)} %shard_map.328._), calls=%async_computation | async-start | bytes 3538944 | tf_op jit(solution)/shard_map/all_to_all | solution.py:1229
  60.1 15.9 %collective-permute-start.10 = (bf16[8,48,768]{2,1,0:T(8,128)(2,1)}, bf16[8,48,768]{2,1,0:T(8,128)(2,1)S(1)}, u32[]{:S(2)}, u32[]{:S(2)}) collective-permute-start(bf16[8,48,768]{2,1,0:T(8,128)(2,1)} %shard_map.333.refs_0_), channel_id=1, source_target_pairs={{0,4},{1,5},{2,6},{3,7},{4,0},{5,1},{6,2},{7,3},{8,12},{9,13},{10,... | collective-permute-start | bytes 1769480 | tf_op jit(solution)/shard_map/ppermute | solution.py:643
  76.8 2.2 %collective-permute-start.12 = (bf16[8,48,768]{2,1,0:T(8,128)(2,1)}, bf16[8,48,768]{2,1,0:T(8,128)(2,1)S(1)}, u32[]{:S(2)}, u32[]{:S(2)}) collective-permute-start(bf16[8,48,768]{2,1,0:T(8,128)(2,1)} %shard_map.336.refs_2_), channel_id=1, source_target_pairs={{0,1},{1,0},{2,3},{3,2},{4,5},{5,4},{6,7},{7,6},{8,9},{9,8},{10,11... | collective-permute-start | bytes 1769480 | tf_op jit(solution)/shard_map/ppermute | solution.py:643
  77.9 2.0 collective-permute-start.11
  122.7 3.1 %collective-permute-start.13 = (bf16[16,48,768]{2,1,0:T(8,128)(2,1)}, bf16[16,48,768]{2,1,0:T(8,128)(2,1)S(1)}, u32[]{:S(2)}, u32[]{:S(2)}) collective-permute-start(bf16[16,48,768]{2,1,0:T(8,128)(2,1)} %get-tuple-element.103), channel_id=1, source_target_pairs={{0,1},{1,0},{2,3},{3,2},{4,5},{5,4},{6,7},{7,6},{8,9},{9,8},{10,11... | collective-permute-start | bytes 3538952 | tf_op jit(solution)/shard_map/ppermute | solution.py:643
  122.9 26.0 %collective-permute-start.16 = (bf16[576,384]{1,0:T(8,128)(2,1)}, bf16[576,384]{1,0:T(8,128)(2,1)S(1)}, u32[]{:S(2)}, u32[]{:S(2)}) collective-permute-start(bf16[576,384]{1,0:T(8,128)(2,1)} %get-tuple-element.110), channel_id=1, source_target_pairs={{0,1},{1,0},{2,3},{3,2},{4,5},{5,4},{6,7},{7,6},{8,9},{9,8},{10,11... | collective-permute-start | bytes 1327112 | tf_op jit(solution)/shard_map/ppermute | solution.py:643
  123.3 25.7 %collective-permute-start.17 = (bf16[576,384]{1,0:T(8,128)(2,1)}, bf16[576,384]{1,0:T(8,128)(2,1)S(1)}, u32[]{:S(2)}, u32[]{:S(2)}) collective-permute-start(bf16[576,384]{1,0:T(8,128)(2,1)} %get-tuple-element.111), channel_id=1, source_target_pairs={{0,2},{1,3},{2,0},{3,1},{4,6},{5,7},{6,4},{7,5},{8,10},{9,11},{10,... | collective-permute-start | bytes 1327112 | tf_op jit(solution)/shard_map/ppermute | solution.py:643
  124.9 24.0 %collective-permute-start.18 = (bf16[576,384]{1,0:T(8,128)(2,1)}, bf16[576,384]{1,0:T(8,128)(2,1)S(1)}, u32[]{:S(2)}, u32[]{:S(2)}) collective-permute-start(bf16[576,384]{1,0:T(8,128)(2,1)} %get-tuple-element.112), channel_id=1, source_target_pairs={{0,3},{1,2},{2,1},{3,0},{4,7},{5,6},{6,5},{7,4},{8,11},{9,10},{10,... | collective-permute-start | bytes 1327112 | tf_op jit(solution)/shard_map/ppermute | solution.py:643
  125.8 3.2 %copy-start.9 = (bf16[16,48,768]{2,1,0:T(8,128)(2,1)}, bf16[16,48,768]{2,1,0:T(8,128)(2,1)S(1)}, u32[]{:S(2)}) copy-start(bf16[16,48,768]{2,1,0:T(8,128)(2,1)S(1)} %collective-permute-done.13) | copy-start | bytes 3538948
  127.5 18.5 %collective-permute-start.14 = (bf16[8,48,768]{2,1,0:T(8,128)(2,1)S(1)}, bf16[8,48,768]{2,1,0:T(8,128)(2,1)S(1)}, u32[]{:S(2)}, u32[]{:S(2)}) collective-permute-start(bf16[8,48,768]{2,1,0:T(8,128)(2,1)S(1)} %add_convert_fusion._), channel_id=1, source_target_pairs={{0,4},{1,5},{2,6},{3,7},{4,0},{5,1},{6,2},{7,3},{8,12},{9,13},{10,... | collective-permute-start | bytes 1769480 | tf_op jit(solution)/shard_map/ppermute | solution.py:643
  129.0 16.9 %copy-start.8 = (bf16[16,48,768]{2,1,0:T(8,128)(2,1)S(1)}, bf16[16,48,768]{2,1,0:T(8,128)(2,1)}, u32[]{:S(2)}) copy-start(bf16[16,48,768]{2,1,0:T(8,128)(2,1)} %get-tuple-element.102) | copy-start | bytes 3538948
  145.9 3.1 %copy-start.1 = (bf16[8,48,768]{2,1,0:T(8,128)(2,1)}, bf16[8,48,768]{2,1,0:T(8,128)(2,1)S(1)}, u32[]{:S(2)}) copy-start(bf16[8,48,768]{2,1,0:T(8,128)(2,1)S(1)} %collective-permute-done.14.refs_4_) | copy-start | bytes 1769476
  147.2 8.8 %collective-permute-start.15 = (bf16[4,48,768]{2,1,0:T(8,128)(2,1)S(1)}, bf16[4,48,768]{2,1,0:T(8,128)(2,1)S(1)}, u32[]{:S(2)}, u32[]{:S(2)}) collective-permute-start(bf16[4,48,768]{2,1,0:T(8,128)(2,1)S(1)} %add_convert_fusion.1), channel_id=1, source_target_pairs={{0,2},{1,3},{2,0},{3,1},{4,6},{5,7},{6,4},{7,5},{8,10},{9,11},{10,... | collective-permute-start | bytes 884744 | tf_op jit(solution)/shard_map/ppermute | solution.py:643
  150.0 7.1 %collective-permute-start.19 = (bf16[16,48,384]{2,1,0:T(8,128)(2,1)}, bf16[16,48,384]{2,1,0:T(8,128)(2,1)S(1)}, u32[]{:S(2)}, u32[]{:S(2)}) collective-permute-start(bf16[16,48,384]{2,1,0:T(8,128)(2,1)} %shard_map.339), channel_id=1, source_target_pairs={{0,1},{1,0},{2,3},{3,2},{4,5},{5,4},{6,7},{7,6},{8,9},{9,8},{10,11... | collective-permute-start | bytes 1769480 | tf_op jit(solution)/shard_map/ppermute | solution.py:643
  150.0 6.0 %copy-start.2 = (bf16[8,48,768]{2,1,0:T(8,128)(2,1)S(1)}, bf16[8,48,768]{2,1,0:T(8,128)(2,1)}, u32[]{:S(2)}) copy-start(bf16[8,48,768]{2,1,0:T(8,128)(2,1)} %copy-done.1) | copy-start | bytes 1769476
  154.0 3.1 %copy-start.12 = (bf16[16,48,384]{2,1,0:T(8,128)(2,1)S(1)}, bf16[16,48,384]{2,1,0:T(8,128)(2,1)}, u32[]{:S(2)}) copy-start(bf16[16,48,384]{2,1,0:T(8,128)(2,1)} %get-tuple-element.108) | copy-start | bytes 1769476
  157.4 3.6 %copy-start.16 = (bf16[4,48,384]{2,1,0:T(8,128)(2,1)}, bf16[4,48,384]{2,1,0:T(8,128)(2,1)S(1)}, u32[]{:S(2)}) copy-start(bf16[4,48,384]{2,1,0:T(8,128)(2,1)S(1)} %get-tuple-element.157.refs_1_) | copy-start | bytes 442372
  157.4 7.5 %collective-permute-start.22 = (bf16[4,48,384]{2,1,0:T(8,128)(2,1)S(1)}, bf16[4,48,384]{2,1,0:T(8,128)(2,1)S(1)}, u32[]{:S(2)}, u32[]{:S(2)}) collective-permute-start(bf16[4,48,384]{2,1,0:T(8,128)(2,1)S(1)} %get-tuple-element.158), channel_id=1, source_target_pairs={{0,6},{1,7},{2,4},{3,5},{4,2},{5,3},{6,0},{7,1},{8,14},{9,15},{10,... | collective-permute-start | bytes 442376 | tf_op jit(solution)/shard_map/ppermute | solution.py:643
  159.6 6.9 %collective-permute-start.21 = (bf16[4,48,384]{2,1,0:T(8,128)(2,1)S(1)}, bf16[4,48,384]{2,1,0:T(8,128)(2,1)S(1)}, u32[]{:S(2)}, u32[]{:S(2)}) collective-permute-start(bf16[4,48,384]{2,1,0:T(8,128)(2,1)S(1)} %get-tuple-element.159), channel_id=1, source_target_pairs={{0,4},{1,5},{2,6},{3,7},{4,0},{5,1},{6,2},{7,3},{8,12},{9,13},{10,... | collective-permute-start | bytes 442376 | tf_op jit(solution)/shard_map/ppermute | solution.py:643
  160.6 5.9 %collective-permute-start.20 = (bf16[4,48,384]{2,1,0:T(8,128)(2,1)S(1)}, bf16[4,48,384]{2,1,0:T(8,128)(2,1)S(1)}, u32[]{:S(2)}, u32[]{:S(2)}) collective-permute-start(bf16[4,48,384]{2,1,0:T(8,128)(2,1)S(1)} %get-tuple-element.157.refs_1_), channel_id=1, source_target_pairs={{0,2},{1,3},{2,0},{3,1},{4,6},{5,7},{6,4},{7,5},{8,10},{9,11},{10,... | collective-permute-start | bytes 442376 | tf_op jit(solution)/shard_map/ppermute | solution.py:643
  166.6 4.5 %copy-start.22 = (bf16[1,48,1152]{2,1,0:T(8,128)(2,1)}, bf16[1,48,1152]{2,1,0:T(8,128)(2,1)S(1)}, u32[]{:S(2)}) copy-start(bf16[1,48,1152]{2,1,0:T(8,128)(2,1)S(1)} %get-tuple-element.162._) | copy-start | bytes 331780
  166.6 15.3 %collective-permute-start.25 = (bf16[1,48,1152]{2,1,0:T(8,128)(2,1)S(1)}, bf16[1,48,1152]{2,1,0:T(8,128)(2,1)S(1)}, u32[]{:S(2)}, u32[]{:S(2)}) collective-permute-start(bf16[1,48,1152]{2,1,0:T(8,128)(2,1)S(1)} %get-tuple-element.160), channel_id=1, source_target_pairs={{0,24},{1,25},{2,26},{3,27},{4,28},{5,29},{6,30},{7,31},{8,16},{9,... | collective-permute-start | bytes 331784 | tf_op jit(solution)/shard_map/ppermute | solution.py:643
  169.2 12.7 %collective-permute-start.24 = (bf16[1,48,1152]{2,1,0:T(8,128)(2,1)S(1)}, bf16[1,48,1152]{2,1,0:T(8,128)(2,1)S(1)}, u32[]{:S(2)}, u32[]{:S(2)}) collective-permute-start(bf16[1,48,1152]{2,1,0:T(8,128)(2,1)S(1)} %get-tuple-element.161), channel_id=1, source_target_pairs={{0,16},{1,17},{2,18},{3,19},{4,20},{5,21},{6,22},{7,23},{8,24},{9,... | collective-permute-start | bytes 331784 | tf_op jit(solution)/shard_map/ppermute | solution.py:643
  169.2 12.7 %collective-permute-start.23 = (bf16[1,48,1152]{2,1,0:T(8,128)(2,1)S(1)}, bf16[1,48,1152]{2,1,0:T(8,128)(2,1)S(1)}, u32[]{:S(2)}, u32[]{:S(2)}) collective-permute-start(bf16[1,48,1152]{2,1,0:T(8,128)(2,1)S(1)} %get-tuple-element.162._), channel_id=1, source_target_pairs={{0,8},{1,9},{2,10},{3,11},{4,12},{5,13},{6,14},{7,15},{8,0},{9,1},... | collective-permute-start | bytes 331784 | tf_op jit(solution)/shard_map/ppermute | solution.py:643
  179.7 24.7 %collective-permute-start.27 = (bf16[576,384]{1,0:T(8,128)(2,1)}, bf16[576,384]{1,0:T(8,128)(2,1)S(1)}, u32[]{:S(2)}, u32[]{:S(2)}) collective-permute-start(bf16[576,384]{1,0:T(8,128)(2,1)} %get-tuple-element.128), channel_id=1, source_target_pairs={{0,2},{1,3},{2,0},{3,1},{4,6},{5,7},{6,4},{7,5},{8,10},{9,11},{10,... | collective-permute-start | bytes 1327112 | tf_op jit(solution)/shard_map/ppermute | solution.py:643
  181.9 22.9 %collective-permute-start.28 = (bf16[576,384]{1,0:T(8,128)(2,1)}, bf16[576,384]{1,0:T(8,128)(2,1)S(1)}, u32[]{:S(2)}, u32[]{:S(2)}) collective-permute-start(bf16[576,384]{1,0:T(8,128)(2,1)} %get-tuple-element.129), channel_id=1, source_target_pairs={{0,3},{1,2},{2,1},{3,0},{4,7},{5,6},{6,5},{7,4},{8,11},{9,10},{10,... | collective-permute-start | bytes 1327112 | tf_op jit(solution)/shard_map/ppermute | solution.py:643
  185.2 19.6 %collective-permute-start.26 = (bf16[576,384]{1,0:T(8,128)(2,1)}, bf16[576,384]{1,0:T(8,128)(2,1)S(1)}, u32[]{:S(2)}, u32[]{:S(2)}) collective-permute-start(bf16[576,384]{1,0:T(8,128)(2,1)} %shard_map.346), channel_id=1, source_target_pairs={{0,1},{1,0},{2,3},{3,2},{4,5},{5,4},{6,7},{7,6},{8,9},{9,8},{10,11... | collective-permute-start | bytes 1327112 | tf_op jit(solution)/shard_map/ppermute | solution.py:643
  185.9 5.1 %collective-permute-start.31 = (f32[24,384]{1,0:T(8,128)}, f32[24,384]{1,0:T(8,128)S(1)}, u32[]{:S(2)}, u32[]{:S(2)}) collective-permute-start(f32[24,384]{1,0:T(8,128)} %get-tuple-element.132), channel_id=1, source_target_pairs={{0,12},{1,13},{2,14},{3,15},{4,8},{5,9},{6,10},{7,11},{8,4},{9,5},... | collective-permute-start | bytes 110600 | tf_op jit(solution)/shard_map/ppermute | solution.py:643
  186.8 5.5 %collective-permute-start.30 = (f32[24,384]{1,0:T(8,128)}, f32[24,384]{1,0:T(8,128)S(1)}, u32[]{:S(2)}, u32[]{:S(2)}) collective-permute-start(f32[24,384]{1,0:T(8,128)} %get-tuple-element.132), channel_id=1, source_target_pairs={{0,8},{1,9},{2,10},{3,11},{4,12},{5,13},{6,14},{7,15},{8,0},{9,1},... | collective-permute-start | bytes 110600 | tf_op jit(solution)/shard_map/ppermute | solution.py:643
  190.9 4.2 %collective-permute-start.29 = (f32[24,384]{1,0:T(8,128)}, f32[24,384]{1,0:T(8,128)S(1)}, u32[]{:S(2)}, u32[]{:S(2)}) collective-permute-start(f32[24,384]{1,0:T(8,128)} %get-tuple-element.132), channel_id=1, source_target_pairs={{0,4},{1,5},{2,6},{3,7},{4,0},{5,1},{6,2},{7,3},{8,12},{9,13},{10,... | collective-permute-start | bytes 110600 | tf_op jit(solution)/shard_map/ppermute | solution.py:643
  195.9 4.9 %copy-start.17 = (f32[24,384]{1,0:T(8,128)}, f32[24,384]{1,0:T(8,128)S(1)}, u32[]{:S(2)}) copy-start(f32[24,384]{1,0:T(8,128)S(1)} %add_add_fusion.refs_0_) | copy-start | bytes 110596
  195.9 4.9 %collective-permute-start.32 = (f32[24,384]{1,0:T(8,128)S(1)}, f32[24,384]{1,0:T(8,128)S(1)}, u32[]{:S(2)}, u32[]{:S(2)}) collective-permute-start(f32[24,384]{1,0:T(8,128)S(1)} %add_add_fusion.refs_0_), channel_id=1, source_target_pairs={{0,16},{1,17},{2,18},{3,19},{4,20},{5,21},{6,22},{7,23},{8,24},{9,... | collective-permute-start | bytes 110600 | tf_op jit(solution)/shard_map/ppermute | solution.py:643
  203.0 5.6 %collective-permute-start.35 = (f32[64,128]{1,0:T(8,128)}, f32[64,128]{1,0:T(8,128)S(1)}, u32[]{:S(2)}, u32[]{:S(2)}) collective-permute-start(f32[64,128]{1,0:T(8,128)} %get-tuple-element.134.refs_0_), channel_id=1, source_target_pairs={{0,3},{1,2},{2,1},{3,0},{4,7},{5,6},{6,5},{7,4},{8,11},{9,10},{10,... | collective-permute-start | bytes 98312 | tf_op jit(solution)/shard_map/ppermute | solution.py:643
  203.0 5.6 %collective-permute-start.34 = (f32[64,128]{1,0:T(8,128)}, f32[64,128]{1,0:T(8,128)S(1)}, u32[]{:S(2)}, u32[]{:S(2)}) collective-permute-start(f32[64,128]{1,0:T(8,128)} %get-tuple-element.134.refs_0_), channel_id=1, source_target_pairs={{0,2},{1,3},{2,0},{3,1},{4,6},{5,7},{6,4},{7,5},{8,10},{9,11},{10,... | collective-permute-start | bytes 98312 | tf_op jit(solution)/shard_map/ppermute | solution.py:643
  204.5 4.1 %collective-permute-start.33 = (f32[64,128]{1,0:T(8,128)}, f32[64,128]{1,0:T(8,128)S(1)}, u32[]{:S(2)}, u32[]{:S(2)}) collective-permute-start(f32[64,128]{1,0:T(8,128)} %get-tuple-element.134.refs_0_), channel_id=1, source_target_pairs={{0,1},{1,0},{2,3},{3,2},{4,5},{5,4},{6,7},{7,6},{8,9},{9,8},{10,11... | collective-permute-start | bytes 98312 | tf_op jit(solution)/shard_map/ppermute | solution.py:643
  (23 other events, 20.0 us)

commit v2 on v1

--- a/solution.py
+++ b/solution.py
@@ -99,7 +99,7 @@
 FF_PER_STEP = 4
 SLICE = 48
 FF_CHUNK = 256
-vmem_bytes = 60 * 1024 * 1024
+vmem_bytes = 64 * 1024 * 1024
 
 
 def dot(left, right, left_axis=1, right_axis=0):
@@ -430,7 +430,7 @@
 def attention_back_steps(
     x_ref, qkv_ref, probs_ref, d_attended_ref, vectors_ref, vector_sums_ref, normed_ref, d_projected_ref, qkv_total_ref
 ):
-    width = x_ref.shape[1]
+    width = d_attended_ref.shape[1]
     length = probs_ref.shape[2]
     per_step = probs_ref.shape[0]
 
@@ -475,11 +475,12 @@
             d_projected_ref[rows, cols[1]] = (dot(d_scores, queries) * scale).astype(jnp.bfloat16)
 
     query_sums = value_sums = jnp.zeros((8, width), jnp.float32)
-    for rows in slices_of(x_ref.shape[0]):
+    for rows in slices_of(d_attended_ref.shape[0]):
         query_sums += fold_rows(d_projected_ref[rows, :width].astype(jnp.float32))
         value_sums += fold_rows(d_projected_ref[rows, 2 * width :].astype(jnp.float32))
-        unit, _ = normal_form(x_ref[rows, :].astype(jnp.float32))
-        normed_ref[rows, :] = (unit * vectors_ref[0:1] + vectors_ref[1:2]).astype(jnp.bfloat16)
+        if x_ref is not None:
+            unit, _ = normal_form(x_ref[rows, :].astype(jnp.float32))
+            normed_ref[rows, :] = (unit * vectors_ref[0:1] + vectors_ref[1:2]).astype(jnp.bfloat16)
     vector_sums_ref[2:3] += column_sum(query_sums)
     vector_sums_ref[3:4] += column_sum(value_sums)
     qkv_total_ref[...] += dot(normed_ref[...], d_projected_ref[...], 0, 0)
@@ -862,8 +863,8 @@
 
 def first_attention_kernel(images, dp_size, spread, place_ref, tokens_ref, *refs):
     blocks, refs = refs[:4], refs[4:]
-    keep_ref, vectors_ref, *outs, x_ref, w_qkv_ref, w_proj_ref, qkv_t_ref, proj_t_ref = refs[:-4]
-    packed_ref, wide_ref, bias_ref, normed_ref = refs[-4:]
+    keep_ref, vectors_ref, *outs, x_ref, w_qkv_ref, w_proj_ref, qkv_t_ref, proj_t_ref = refs[:-3]
+    packed_ref, wide_ref, bias_ref = refs[-3:]
     rows = packed_ref.shape[1]
     qkv_cols, proj_cols = w_qkv_ref.shape[1] // spread, w_proj_ref.shape[1] // spread
 
@@ -881,7 +882,7 @@
         qkv_t_ref[...] = w_qkv_ref[...].T
         proj_t_ref[...] = w_proj_ref[...].T
 
-    attention_part(0, x_ref, keep_ref, w_qkv_ref, w_proj_ref, vectors_ref, *outs, bias_ref, normed_ref)
+    attention_part(0, x_ref, keep_ref, w_qkv_ref, w_proj_ref, vectors_ref, *outs, bias_ref)
 
 
 def next_attention_kernel(start, x_ref, keep_ref, w_qkv_ref, w_proj_ref, vectors_ref, *refs):
@@ -890,7 +891,7 @@
 
 def attention_part(
     start, x_ref, keep_ref, w_qkv_ref, w_proj_ref, vectors_ref,
-    qkv_ref, probs_ref, attended_ref, middle_ref, bias_ref, normed_ref,
+    qkv_ref, probs_ref, attended_ref, middle_ref, normed_ref, bias_ref,
 ):
     @pl.when(pl.program_id(0) == 0)
     def _():
@@ -961,8 +962,8 @@
 
 
 def attention_back_packed_kernel(
-    dp_size, spread, place_ref, x_ref, qkv_ref, probs_ref, d_attended_ref, vectors_ref, proj_total_ref, _,
-    d_projected_ref, keep_ref, leave_ref, vector_sums_ref, normed_ref, total_ref,
+    dp_size, spread, place_ref, normed_ref, qkv_ref, probs_ref, d_attended_ref, vectors_ref, proj_total_ref, _,
+    d_projected_ref, keep_ref, leave_ref, vector_sums_ref, total_ref,
 ):
     @pl.when(pl.program_id(0) == 0)
     def _():
@@ -970,7 +971,7 @@
         vector_sums_ref[...] = jnp.zeros_like(vector_sums_ref)
 
     attention_back_steps(
-        x_ref, qkv_ref, probs_ref, d_attended_ref, vectors_ref, vector_sums_ref, normed_ref, d_projected_ref, total_ref
+        None, qkv_ref, probs_ref, d_attended_ref, vectors_ref, vector_sums_ref, normed_ref, d_projected_ref, total_ref
     )
 
     @pl.when(pl.program_id(0) == pl.num_programs(0) - 1)
@@ -1299,9 +1300,10 @@
         ((images, *probs_block[1:]), low, probs_block),
         ((total, width), low, block),
         ((total, width), high, block),
+        ((total, width), low, block),
     ]
     attention_flops = (2 * total * width * 4 * width + 8 * total * length * width) // steps
-    attention_scratches = [scratch(length, images), scratch(step_rows, width, dtype=low)]
+    attention_scratches = [scratch(length, images)]
     *attention, x, w_qkv, w_proj, qkv_t, proj_t = call_kernel(
         first_attention_kernel, statics, 1,
         ["place"] + [None] * 7,
@@ -1326,7 +1328,7 @@
         attention_flops * (steps - 1), first_step=1,
         aliases={5 + at: at for at in range(len(attention))},
     )
-    qkv, probs, attended, middle = attention
+    qkv, probs, attended, middle, normed = attention
     second_blocks = gather_rest(second_joined, middle)
     piece = ((slots * images, width), low, None)
     ff_rows = FF_PER_STEP * length
@@ -1382,8 +1384,8 @@
         attention_back_packed_kernel, (dp_size, spread), steps,
         ["place", block, wide_rows, probs_block, block, None, None, "await"],
         [((total, 3 * width), low, wide_rows), pack_half, pack_half, ((8, width), high, None)],
-        [scratch(step_rows, width, dtype=low), scratch(width, 3 * width)],
-        (place, x, qkv, probs, d_attended, vectors, proj_total, ff_next),
+        [scratch(width, 3 * width)],
+        (place, normed, qkv, probs, d_attended, vectors, proj_total, ff_next),
         2 * total * width * 3 * width + 16 * total * length * width,
     )
     qkv_arrived = permute(after(qkv_leave, output_parts[1:] + [ff_arrived]), core_bits[0])

time: 213 us -> 220 us (1.033)
  other arithmetic: 5.72 us -> 13.9 us
  local copies, waits for them, and re-layouts: 9.8 us -> 5.3 us
  waiting for transfers between devices: 28.8 us -> 32.9 us
    unnamed x66 -> x18, local copies, waits for them, and re-layouts: 9.73 us -> 3.79 us
    ppermute x36, waiting for transfers between devices: 28.7 us -> 32.9 us  [permute(): lax.ppermute(array, ('dp', 'group'), [(rank, rank ^ mask) for rank in ran...]
    another operation x2, other arithmetic: 0.19 us -> 3.33 us
    add x2, other arithmetic: 1.16 us -> 3.45 us  [add_wide(): total = total + part.astype(jnp.float32)]
  transfers between devices with their start and end apart: 38 -> 38, of which waited for: 13 -> 14; matrix products, arithmetic and copies ran while one was open for 3% -> 4% of each run, Pallas kernels for 34% -> 33%
where the time goes in v2:
time: 220 us; the launch traced here: 219 us
  Pallas kernels  121 us (55%)
  starting transfers between devices  45.3 us (21%)
  waiting for transfers between devices  32.9 us (15%)
  other arithmetic  13.9 us (6%)
  local copies, waits for them, and re-layouts  5.3 us (2%)
    pallas_call x7, Pallas kernels, call_kernel(): pl.pallas_call(functools.partial(kernel, *statics), grid=(steps,), in_spe...  97.3 us
    ppermute x36, starting transfers between devices, permute(): lax.ppermute(array, ('dp', 'group'), [(rank, rank ^ mask) for rank in ran...  36.4 us
    ppermute x36, waiting for transfers between devices, permute(): lax.ppermute(array, ('dp', 'group'), [(rank, rank ^ mask) for rank in ran...  32.9 us
    all_to_all x2, starting transfers between devices, to_group(): lax.all_to_all(parts, 'group', split_axis=0, concat_axis=0, tiled=True)  8.91 us
    pallas_call x2, Pallas kernels, settle(): small(functools.partial(settle_kernel, spread), in_specs=[in_smem] + [in_...  5.55 us
  transfers between devices with their start and end apart: 38, of which 14 were waited for; matrix products, arithmetic and copies ran while one was open for 4% of the time, Pallas kernels for 33%

profile of v2, /device:TPU:0, one launch (start us, length us, event | category | flops | bytes accessed | tf_op | source)
XLA Modules:
  0.0 219.0 jit_solution(5359652372299497643)
XLA Ops:
  0.7 1.7 shard_map.329.own_ref
  2.4 3.0 %collective-permute-start = (bf16[48,1152]{1,0:T(8,128)(2,1)}, bf16[48,1152]{1,0:T(8,128)(2,1)}, u32[]{:S(2)}, u32[]{:S(2)}) collective-permute-start(bf16[48,1152]{1,0:T(8,128)(2,1)} %shard_map.329.own_ref), channel_id=1, source_target_pairs={{0,2},{1,3},{2,0},{3,1},{4,6},{5,7},{6,4},{7,5},{8,10},{9,11},{10,... | collective-permute-start | bytes 331784 | tf_op jit(solution)/shard_map/ppermute | solution.py:644
  5.3 2.8 %shard_map.328._ = bf16[4,36,16,384]{3,2,1,0:T(8,128)(2,1)} custom-call(bf16[36,64,384]{2,1,0:T(8,128)(2,1)} %bitcast.16), custom_call_target="tpu_custom_call" | custom-call | tf_op jit(solution)/shard_map/pallas_call | solution.py:1256
  8.7 2.9 %shard_map.330 = (bf16[4,36,16,384]{3,2,1,0:T(8,128)(2,1)}, bf16[2,48,384]{2,1,0:T(8,128)(2,1)}, bf16[2,48,768]{2,1,0:T(8,128)(2,1)}) custom-call(bf16[36,64,384]{2,1,0:T(8,128)(2,1)} %bitcast.15, bf16[48,1152]{1,0:T(8,128)(2,1)} %shard_map.329.own_ref, bf16[48,1152]{1,0:T(8,128)(2,1)} %collective-permute-done.arrived_ref, bf16[4,36,16,384]{3,2,1,0:T(8,128)(2,1)} %shard_map.328._), custom_call_target="tpu_custom_call" | custom-call | tf_op jit(solution)/shard_map/pallas_call | solution.py:1257
  11.6 4.5 %all-to-all-start.1 = ((bf16[4,36,16,384]{3,2,1,0:T(8,128)(2,1)}), bf16[4,36,16,384]{3,2,1,0:T(8,128)(2,1)}, u32[]{:S(2)}, u32[]{:S(2)}) async-start(bf16[4,36,16,384]{3,2,1,0:T(8,128)(2,1)} %get-tuple-element.91), calls=%async_computation.1 | async-start | bytes 3538944 | tf_op jit(solution)/shard_map/all_to_all | solution.py:1230
  16.2 3.9 %collective-permute-start.6 = (bf16[2,48,384]{2,1,0:T(8,128)(2,1)S(1)}, bf16[2,48,384]{2,1,0:T(8,128)(2,1)S(1)}, u32[]{:S(2)}, u32[]{:S(2)}) collective-permute-start(bf16[2,48,384]{2,1,0:T(8,128)(2,1)S(1)} %copy-done.3), channel_id=1, source_target_pairs={{0,24},{1,25},{2,26},{3,27},{4,28},{5,29},{6,30},{7,31},{8,16},{9,... | collective-permute-start | bytes 221192 | tf_op jit(solution)/shard_map/ppermute | solution.py:644
  20.7 2.6 %collective-permute-done.6.refs_3_ = bf16[2,48,384]{2,1,0:T(8,128)(2,1)S(1)} collective-permute-done((bf16[2,48,384]{2,1,0:T(8,128)(2,1)S(1)}, bf16[2,48,384]{2,1,0:T(8,128)(2,1)S(1)}, u32[]{:S(2)}, u32[]{:S(2)}) %collective-permute-start.6) | collective-permute-done | bytes 73760 | tf_op jit(solution)/shard_map/ppermute | solution.py:644
  23.3 3.5 %collective-permute-done.5.refs_2_ = bf16[2,48,384]{2,1,0:T(8,128)(2,1)S(1)} collective-permute-done((bf16[2,48,384]{2,1,0:T(8,128)(2,1)S(1)}, bf16[2,48,384]{2,1,0:T(8,128)(2,1)S(1)}, u32[]{:S(2)}, u32[]{:S(2)}) %collective-permute-start.5) | collective-permute-done | bytes 73760 | tf_op jit(solution)/shard_map/ppermute | solution.py:644
  27.4 1.8 shard_map.331.refs_0_
  29.2 1.5 collective-permute-start.7
  30.7 7.2 %collective-permute-done.7.refs_1_ = bf16[8,48,384]{2,1,0:T(8,128)(2,1)S(1)} collective-permute-done((bf16[8,48,384]{2,1,0:T(8,128)(2,1)}, bf16[8,48,384]{2,1,0:T(8,128)(2,1)S(1)}, u32[]{:S(2)}, u32[]{:S(2)}) %collective-permute-start.7) | collective-permute-done | bytes 294944 | tf_op jit(solution)/shard_map/ppermute | solution.py:644
  37.9 2.5 %collective-permute-start.3 = (bf16[2,48,768]{2,1,0:T(8,128)(2,1)}, bf16[2,48,768]{2,1,0:T(8,128)(2,1)}, u32[]{:S(2)}, u32[]{:S(2)}) collective-permute-start(bf16[2,48,768]{2,1,0:T(8,128)(2,1)} %get-tuple-element.90.refs_0_), channel_id=1, source_target_pairs={{0,24},{1,25},{2,26},{3,27},{4,28},{5,29},{6,30},{7,31},{8,16},{9,... | collective-permute-start | bytes 442376 | tf_op jit(solution)/shard_map/ppermute | solution.py:644
  40.3 1.9 collective-permute-start.1
  42.3 4.4 %all-to-all-start = ((bf16[4,36,16,384]{3,2,1,0:T(8,128)(2,1)}), bf16[4,36,16,384]{3,2,1,0:T(8,128)(2,1)}, u32[]{:S(2)}, u32[]{:S(2)}) async-start(bf16[4,36,16,384]{3,2,1,0:T(8,128)(2,1)} %shard_map.328._), calls=%async_computation | async-start | bytes 3538944 | tf_op jit(solution)/shard_map/all_to_all | solution.py:1230
  48.1 10.2 %shard_map.332 = (bf16[2304,1152]{1,0:T(8,128)(2,1)}, bf16[16,3,144,288]{3,2,1,0:T(8,128)(2,1)}, bf16[2304,384]{1,0:T(8,128)(2,1)}, f32[2304,384]{1,0:T(8,128)},...) custom-call(s32[1]{0:T(128)} %bitcast.place_ref, ...), custom_call_target="tpu_custom_call" | custom-call | flops 7474249728 | bytes 23473156 | tf_op jit(solution)/shard_map/pallas_call | solution.py:536
  58.3 2.0 shard_map.333.refs_0_
  60.3 1.5 collective-permute-start.10
  61.8 12.5 %shard_map.334 = (bf16[2304,1152]{1,0:T(8,128)(2,1)}, bf16[16,3,144,288]{3,2,1,0:T(8,128)(2,1)}, bf16[2304,384]{1,0:T(8,128)(2,1)}, f32[2304,384]{1,0:T(8,128)}, bf16[2304,384]{1,0:T(8,128)(2,1)}) custom-call(bf16[2304,384]{1,0:T(8,128)(2,1)} %get-tuple-element.94.x_ref, ...), custom_call_target="tpu_custom_call", output_to_operand_aliasing={{0}: (5, {}), {1}: (6, {}), {2}: (7, {}), {3}: (8, {}), {4}... | custom-call | flops 22422749184 | bytes 35712000 | tf_op jit(solution)/shard_map/pallas_call | solution.py:536
  74.3 2.0 collective-permute-done.10.refs_0_
  76.8 1.8 collective-permute-done.12.refs_4_
  79.5 42.0 %shard_map.337 = (bf16[576,384]{1,0:T(8,128)(2,1)}, bf16[576,384]{1,0:T(8,128)(2,1)}, bf16[576,384]{1,0:T(8,128)(2,1)}, bf16[576,384]{1,0:T(8,128)(2,1)}, f32[23...) custom-call(s32[1]{0:T(128)} %bitcast.place_ref, ...), custom_call_target="tpu_custom_call" | custom-call | flops 141331267584 | bytes 19795972 | tf_op jit(solution)/shard_map/pallas_call | solution.py:536
  122.0 1.7 collective-permute-start.17
  125.9 2.1 add_convert_fusion._
  128.0 1.6 collective-permute-start.14
  129.5 16.1 %shard_map.338 = (bf16[2304,1152]{1,0:T(8,128)(2,1)}, bf16[16,48,384]{2,1,0:T(8,128)(2,1)}, bf16[16,48,384]{2,1,0:T(8,128)(2,1)}, f32[8,384]{1,0:T(8,128)}) custom-call(s32[1]{0:T(128)} %bitcast.place_ref, bf16[2304,384]{1,0:T(8,128)(2,1)} %get-tuple-element.107.normed_ref, bf16[2304,1152]{1,0:T(8,128)(2,1)} %get-tuple-element.108.qkv_ref, ...), custom_call_target="tpu_custom_call" | custom-call | flops 32614907904 | bytes 20527108 | tf_op jit(solution)/shard_map/pallas_call | solution.py:536
  145.7 2.0 add_convert_fusion.1
  147.7 1.6 collective-permute-start.15
  149.3 3.9 %shard_map.340 = (bf16[2304,384]{1,0:T(8,128)(2,1)}, f32[8,384]{1,0:T(8,128)}) custom-call(bf16[2304,384]{1,0:T(8,128)(2,1)} %get-tuple-element.94.x_ref, bf16[2304,1152]{1,0:T(8,128)(2,1)} %get-tuple-element.117.d_projected_ref, f32[2304,384]{1,0:T(8,128)} %get-tuple-element.118.d_middle_ref, bf16[1152,384]{1,0:T(8,128)(2,1)} %get-tuple-element.119.qkv_t_ref, ...), custom_call_target="tpu_custom_call" | custom-call | flops 4076863488 | bytes 13314048 | tf_op jit(solution)/shard_map/pallas_call | solution.py:536
  153.3 3.5 %collective-permute-done.15 = bf16[4,48,768]{2,1,0:T(8,128)(2,1)} collective-permute-done((bf16[4,48,768]{2,1,0:T(8,128)(2,1)}, bf16[4,48,768]{2,1,0:T(8,128)(2,1)}, u32[]{:S(2)}, u32[]{:S(2)}) %collective-permute-start.15) | collective-permute-done | bytes 294944 | tf_op jit(solution)/shard_map/ppermute | solution.py:644
  156.7 2.2 %convert_add_fusion.1 = f32[4,48,768]{2,1,0:T(8,128)} fusion(bf16[4,48,768]{2,1,0:T(8,128)(2,1)} %collective-permute-done.15, bf16[8,48,768]{2,1,0:T(8,128)(2,1)} %collective-permute-done.14.refs_4_, bf16[16,48,768]{2,1,0:T(8,128)(2,1)} %copy-done.1, bf16[16,48,768]{2,1,0:T(8,128)(2,1)} %get-tuple-element.105), kind=kLoop, calls=%fused_computation.6 | loop fusion | flops 1032192 | bytes 1769472 | tf_op jit(solution)/shard_map/add | solution.py:678
  159.0 2.2 %fusion.4 = (bf16[16,48,384]{2,1,0:T(8,128)(2,1)S(1)}, f32[16,48,384]{2,1,0:T(8,128)}) fusion(bf16[16,48,384]{2,1,0:T(8,128)(2,1)} %collective-permute-done.19, bf16[16,48,384]{2,1,0:T(8,128)(2,1)S(1)} %copy-done.2), kind=kLoop, calls=%fused_computation.13 | loop fusion | flops 1179648 | bytes 2949120 | tf_op jit(solution)/shard_map/convert.5
  162.0 1.6 collective-permute-start.22
  163.5 1.5 collective-permute-start.21
  165.5 3.9 %shard_map.341 = (bf16[2304,384]{1,0:T(8,128)(2,1)}, f32[8,384]{1,0:T(8,128)}) custom-call(bf16[2304,384]{1,0:T(8,128)(2,1)} %get-tuple-element.94.x_ref, bf16[2304,1152]{1,0:T(8,128)(2,1)} %get-tuple-element.117.d_projected_ref, f32[2304,384]{1,0:T(8,128)} %get-tuple-element.118.d_middle_ref, ...), custom_call_target="tpu_custom_call", output_to_operand_aliasing={{0}: (6, {})} | custom-call | flops 4076863488 | bytes 15230976 | tf_op jit(solution)/shard_map/pallas_call | solution.py:536
  169.6 1.6 collective-permute-done.21
  175.0 2.5 %collective-permute-start.25 = (bf16[1,48,1152]{2,1,0:T(8,128)(2,1)}, bf16[1,48,1152]{2,1,0:T(8,128)(2,1)}, u32[]{:S(2)}, u32[]{:S(2)}) collective-permute-start(bf16[1,48,1152]{2,1,0:T(8,128)(2,1)} %get-tuple-element.164), channel_id=1, source_target_pairs={{0,24},{1,25},{2,26},{3,27},{4,28},{5,29},{6,30},{7,31},{8,16},{9,... | collective-permute-start | bytes 331784 | tf_op jit(solution)/shard_map/ppermute | solution.py:644
  177.5 1.9 collective-permute-start.23
  179.4 8.7 %shard_map.342 = (bf16[576,384]{1,0:T(8,128)(2,1)}, bf16[576,384]{1,0:T(8,128)(2,1)}, bf16[576,384]{1,0:T(8,128)(2,1)}, bf16[576,384]{1,0:T(8,128)(2,1)}, f32[8,384]{1,0:T(8,128)}) custom-call(s32[1]{0:T(128)} %bitcast.place_ref, bf16[2304,384]{1,0:T(8,128)(2,1)} %get-tuple-element.94.x_ref, bf16[2304,1152]{1,0:T(8,128)(2,1)} %get-tuple-element.117.d_projected_ref, ...), custom_call_target="tpu_custom_call" | custom-call | flops 8153726976 | bytes 15194116 | tf_op jit(solution)/shard_map/pallas_call | solution.py:536
  189.5 1.7 fusion.3.refs_0_
  191.2 2.6 %shard_map.343 = (f32[48,288]{1,0:T(8,128)}, f32[48,96]{1,0:T(8,128)}, f32[48,384]{1,0:T(8,128)}, f32[192,96]{1,0:T(8,128)}, f32[8,48]{1,0:T(8,128)}, /*index=5*/f32[24,384]{1,0:T(8,128)}) custom-call(f32[1,48,1152]{2,1,0:T(8,128)} %fusion.3.refs_0_, bf16[1,48,1152]{2,1,0:T(8,128)(2,1)} %collective-permute-done.23.refs_1_, ...), custom_call_target="tpu_custom_call" | custom-call | tf_op jit(solution)/shard_map/pallas_call | solution.py:1440
  194.6 1.9 collective-permute-start.30
  196.5 3.0 %collective-permute-done.31 = f32[24,384]{1,0:T(8,128)S(1)} collective-permute-done((f32[24,384]{1,0:T(8,128)}, f32[24,384]{1,0:T(8,128)S(1)}, u32[]{:S(2)}, u32[]{:S(2)}) %collective-permute-start.31) | collective-permute-done | bytes 36896 | tf_op jit(solution)/shard_map/ppermute | solution.py:644
  200.1 3.6 %collective-permute-done.29 = f32[24,384]{1,0:T(8,128)S(1)} collective-permute-done((f32[24,384]{1,0:T(8,128)}, f32[24,384]{1,0:T(8,128)S(1)}, u32[]{:S(2)}, u32[]{:S(2)}) %collective-permute-start.29) | collective-permute-done | bytes 36896 | tf_op jit(solution)/shard_map/ppermute | solution.py:644
  206.1 2.8 %shard_map.345 = (bf16[36,64,384]{2,1,0:T(8,128)(2,1)}, f32[8,128]{1,0:T(8,128)}) custom-call(s32[1]{0:T(128)} %bitcast.place_ref, bf16[36,16,384]{2,1,0:T(8,128)(2,1)} %bitcast.17, bf16[36,16,384]{2,1,0:T(8,128)(2,1)} %bitcast.6.refs_1_, bf16[36,16,384]{2,1,0:T(8,128)(2,1)} %bitcast.7.refs_2_, bf16[36,16,384]{2,1,0:T(8,128)(2,1)} %bitcast.8.refs_3_), custom_call_target="tpu_custom_call" | custom-call | tf_op jit(solution)/shard_map/pallas_call | solution.py:1240
  210.3 1.5 shard_map.348
  211.8 1.5 collective-permute-start.34
  213.7 2.8 %shard_map.347 = (bf16[36,64,384]{2,1,0:T(8,128)(2,1)}, f32[8,128]{1,0:T(8,128)}) custom-call(s32[1]{0:T(128)} %bitcast.place_ref, bf16[36,16,384]{2,1,0:T(8,128)(2,1)} %bitcast.18, bf16[36,16,384]{2,1,0:T(8,128)(2,1)} %bitcast.11.refs_1_, bf16[36,16,384]{2,1,0:T(8,128)(2,1)} %bitcast.12.refs_2_, bf16[36,16,384]{2,1,0:T(8,128)(2,1)} %bitcast.13.refs_3_), custom_call_target="tpu_custom_call" | custom-call | tf_op jit(solution)/shard_map/pallas_call | solution.py:1240
  216.5 2.4 %shard_map.349 = (f32[48,288]{1,0:T(8,128)}, f32[48,96]{1,0:T(8,128)}, f32[48,384]{1,0:T(8,128)}, f32[192,96]{1,0:T(8,128)}, f32[288]{0:T(512)}, /*index=5*/f32[...) custom-call(f32[64,128]{1,0:T(8,128)} %get-tuple-element.138.refs_0_, ...), custom_call_target="tpu_custom_call" | custom-call | tf_op jit(solution)/shard_map/pallas_call | solution.py:1462
  (78 shorter events, 19.6 us)
Async XLA Ops:
  2.4 6.3 %collective-permute-start = (bf16[48,1152]{1,0:T(8,128)(2,1)}, bf16[48,1152]{1,0:T(8,128)(2,1)}, u32[]{:S(2)}, u32[]{:S(2)}) collective-permute-start(bf16[48,1152]{1,0:T(8,128)(2,1)} %shard_map.329.own_ref), channel_id=1, source_target_pairs={{0,2},{1,3},{2,0},{3,1},{4,6},{5,7},{6,4},{7,5},{8,10},{9,11},{10,... | collective-permute-start | bytes 331784 | tf_op jit(solution)/shard_map/ppermute | solution.py:644
  11.6 4.5 %copy-start.3 = (bf16[2,48,384]{2,1,0:T(8,128)(2,1)S(1)}, bf16[2,48,384]{2,1,0:T(8,128)(2,1)}, u32[]{:S(2)}) copy-start(bf16[2,48,384]{2,1,0:T(8,128)(2,1)} %get-tuple-element.92.refs_0_) | copy-start | bytes 221188
  11.6 30.6 %all-to-all-start.1 = ((bf16[4,36,16,384]{3,2,1,0:T(8,128)(2,1)}), bf16[4,36,16,384]{3,2,1,0:T(8,128)(2,1)}, u32[]{:S(2)}, u32[]{:S(2)}) async-start(bf16[4,36,16,384]{3,2,1,0:T(8,128)(2,1)} %get-tuple-element.91), calls=%async_computation.1 | async-start | bytes 3538944 | tf_op jit(solution)/shard_map/all_to_all | solution.py:1230
  16.2 7.1 %collective-permute-start.6 = (bf16[2,48,384]{2,1,0:T(8,128)(2,1)S(1)}, bf16[2,48,384]{2,1,0:T(8,128)(2,1)S(1)}, u32[]{:S(2)}, u32[]{:S(2)}) collective-permute-start(bf16[2,48,384]{2,1,0:T(8,128)(2,1)S(1)} %copy-done.3), channel_id=1, source_target_pairs={{0,24},{1,25},{2,26},{3,27},{4,28},{5,29},{6,30},{7,31},{8,16},{9,... | collective-permute-start | bytes 221192 | tf_op jit(solution)/shard_map/ppermute | solution.py:644
  20.1 6.7 %collective-permute-start.5 = (bf16[2,48,384]{2,1,0:T(8,128)(2,1)S(1)}, bf16[2,48,384]{2,1,0:T(8,128)(2,1)S(1)}, u32[]{:S(2)}, u32[]{:S(2)}) collective-permute-start(bf16[2,48,384]{2,1,0:T(8,128)(2,1)S(1)} %copy-done.3), channel_id=1, source_target_pairs={{0,16},{1,17},{2,18},{3,19},{4,20},{5,21},{6,22},{7,23},{8,24},{9,... | collective-permute-start | bytes 221192 | tf_op jit(solution)/shard_map/ppermute | solution.py:644
  20.1 7.3 %collective-permute-start.4 = (bf16[2,48,384]{2,1,0:T(8,128)(2,1)S(1)}, bf16[2,48,384]{2,1,0:T(8,128)(2,1)}, u32[]{:S(2)}, u32[]{:S(2)}) collective-permute-start(bf16[2,48,384]{2,1,0:T(8,128)(2,1)S(1)} %copy-done.3), channel_id=1, source_target_pairs={{0,8},{1,9},{2,10},{3,11},{4,12},{5,13},{6,14},{7,15},{8,0},{9,1},... | collective-permute-start | bytes 221192 | tf_op jit(solution)/shard_map/ppermute | solution.py:644
  23.3 3.5 %copy-start.4 = (bf16[2,48,384]{2,1,0:T(8,128)(2,1)}, bf16[2,48,384]{2,1,0:T(8,128)(2,1)S(1)}, u32[]{:S(2)}) copy-start(bf16[2,48,384]{2,1,0:T(8,128)(2,1)S(1)} %collective-permute-done.6.refs_3_) | copy-start | bytes 221188
  26.8 0.6 copy-start.5
  29.2 8.7 %collective-permute-start.7 = (bf16[8,48,384]{2,1,0:T(8,128)(2,1)}, bf16[8,48,384]{2,1,0:T(8,128)(2,1)S(1)}, u32[]{:S(2)}, u32[]{:S(2)}) collective-permute-start(bf16[8,48,384]{2,1,0:T(8,128)(2,1)} %shard_map.331.refs_0_), channel_id=1, source_target_pairs={{0,4},{1,5},{2,6},{3,7},{4,0},{5,1},{6,2},{7,3},{8,12},{9,13},{10,... | collective-permute-start | bytes 884744 | tf_op jit(solution)/shard_map/ppermute | solution.py:644
  30.7 16.0 %collective-permute-start.8 = (bf16[8,48,384]{2,1,0:T(8,128)(2,1)}, bf16[8,48,384]{2,1,0:T(8,128)(2,1)S(1)}, u32[]{:S(2)}, u32[]{:S(2)}) collective-permute-start(bf16[8,48,384]{2,1,0:T(8,128)(2,1)} %shard_map.331.refs_0_), channel_id=1, source_target_pairs={{0,1},{1,0},{2,3},{3,2},{4,5},{5,4},{6,7},{7,6},{8,9},{9,8},{10,11... | collective-permute-start | bytes 884744 | tf_op jit(solution)/shard_map/ppermute | solution.py:644
  37.9 4.4 %copy-start.6 = (bf16[8,48,384]{2,1,0:T(8,128)(2,1)}, bf16[8,48,384]{2,1,0:T(8,128)(2,1)S(1)}, u32[]{:S(2)}) copy-start(bf16[8,48,384]{2,1,0:T(8,128)(2,1)S(1)} %collective-permute-done.7.refs_1_) | copy-start | bytes 884740
  37.9 8.8 %collective-permute-start.9 = (bf16[8,48,384]{2,1,0:T(8,128)(2,1)S(1)}, bf16[8,48,384]{2,1,0:T(8,128)(2,1)S(1)}, u32[]{:S(2)}, u32[]{:S(2)}) collective-permute-start(bf16[8,48,384]{2,1,0:T(8,128)(2,1)S(1)} %collective-permute-done.7.refs_1_), channel_id=1, source_target_pairs={{0,1},{1,0},{2,3},{3,2},{4,5},{5,4},{6,7},{7,6},{8,9},{9,8},{10,11... | collective-permute-start | bytes 884744 | tf_op jit(solution)/shard_map/ppermute | solution.py:644
  37.9 20.4 %collective-permute-start.3 = (bf16[2,48,768]{2,1,0:T(8,128)(2,1)}, bf16[2,48,768]{2,1,0:T(8,128)(2,1)}, u32[]{:S(2)}, u32[]{:S(2)}) collective-permute-start(bf16[2,48,768]{2,1,0:T(8,128)(2,1)} %get-tuple-element.90.refs_0_), channel_id=1, source_target_pairs={{0,24},{1,25},{2,26},{3,27},{4,28},{5,29},{6,30},{7,31},{8,16},{9,... | collective-permute-start | bytes 442376 | tf_op jit(solution)/shard_map/ppermute | solution.py:644
  40.3 17.9 %collective-permute-start.2 = (bf16[2,48,768]{2,1,0:T(8,128)(2,1)}, bf16[2,48,768]{2,1,0:T(8,128)(2,1)}, u32[]{:S(2)}, u32[]{:S(2)}) collective-permute-start(bf16[2,48,768]{2,1,0:T(8,128)(2,1)} %get-tuple-element.90.refs_0_), channel_id=1, source_target_pairs={{0,16},{1,17},{2,18},{3,19},{4,20},{5,21},{6,22},{7,23},{8,24},{9,... | collective-permute-start | bytes 442376 | tf_op jit(solution)/shard_map/ppermute | solution.py:644
  40.3 17.9 %collective-permute-start.1 = (bf16[2,48,768]{2,1,0:T(8,128)(2,1)}, bf16[2,48,768]{2,1,0:T(8,128)(2,1)}, u32[]{:S(2)}, u32[]{:S(2)}) collective-permute-start(bf16[2,48,768]{2,1,0:T(8,128)(2,1)} %get-tuple-element.90.refs_0_), channel_id=1, source_target_pairs={{0,8},{1,9},{2,10},{3,11},{4,12},{5,13},{6,14},{7,15},{8,0},{9,1},... | collective-permute-start | bytes 442376 | tf_op jit(solution)/shard_map/ppermute | solution.py:644
  42.3 34.5 %all-to-all-start = ((bf16[4,36,16,384]{3,2,1,0:T(8,128)(2,1)}), bf16[4,36,16,384]{3,2,1,0:T(8,128)(2,1)}, u32[]{:S(2)}, u32[]{:S(2)}) async-start(bf16[4,36,16,384]{3,2,1,0:T(8,128)(2,1)} %shard_map.328._), calls=%async_computation | async-start | bytes 3538944 | tf_op jit(solution)/shard_map/all_to_all | solution.py:1230
  46.7 0.7 copy-start.7
  47.4 0.7 copy-start.8
  60.3 16.0 %collective-permute-start.10 = (bf16[8,48,768]{2,1,0:T(8,128)(2,1)}, bf16[8,48,768]{2,1,0:T(8,128)(2,1)}, u32[]{:S(2)}, u32[]{:S(2)}) collective-permute-start(bf16[8,48,768]{2,1,0:T(8,128)(2,1)} %shard_map.333.refs_0_), channel_id=1, source_target_pairs={{0,4},{1,5},{2,6},{3,7},{4,0},{5,1},{6,2},{7,3},{8,12},{9,13},{10,... | collective-permute-start | bytes 1769480 | tf_op jit(solution)/shard_map/ppermute | solution.py:644
  76.3 2.3 %collective-permute-start.12 = (bf16[8,48,768]{2,1,0:T(8,128)(2,1)}, bf16[8,48,768]{2,1,0:T(8,128)(2,1)}, u32[]{:S(2)}, u32[]{:S(2)}) collective-permute-start(bf16[8,48,768]{2,1,0:T(8,128)(2,1)} %shard_map.336.refs_2_), channel_id=1, source_target_pairs={{0,1},{1,0},{2,3},{3,2},{4,5},{5,4},{6,7},{7,6},{8,9},{9,8},{10,11... | collective-permute-start | bytes 1769480 | tf_op jit(solution)/shard_map/ppermute | solution.py:644
  76.3 3.2 %collective-permute-start.11 = (bf16[8,48,768]{2,1,0:T(8,128)(2,1)}, bf16[8,48,768]{2,1,0:T(8,128)(2,1)}, u32[]{:S(2)}, u32[]{:S(2)}) collective-permute-start(bf16[8,48,768]{2,1,0:T(8,128)(2,1)} %shard_map.335.refs_1_), channel_id=1, source_target_pairs={{0,1},{1,0},{2,3},{3,2},{4,5},{5,4},{6,7},{7,6},{8,9},{9,8},{10,11... | collective-permute-start | bytes 1769480 | tf_op jit(solution)/shard_map/ppermute | solution.py:644
  121.5 3.4 %collective-permute-start.13 = (bf16[16,48,768]{2,1,0:T(8,128)(2,1)}, bf16[16,48,768]{2,1,0:T(8,128)(2,1)S(1)}, u32[]{:S(2)}, u32[]{:S(2)}) collective-permute-start(bf16[16,48,768]{2,1,0:T(8,128)(2,1)} %get-tuple-element.106), channel_id=1, source_target_pairs={{0,1},{1,0},{2,3},{3,2},{4,5},{5,4},{6,7},{7,6},{8,9},{9,8},{10,11... | collective-permute-start | bytes 3538952 | tf_op jit(solution)/shard_map/ppermute | solution.py:644
  121.7 27.6 %collective-permute-start.16 = (bf16[576,384]{1,0:T(8,128)(2,1)}, bf16[576,384]{1,0:T(8,128)(2,1)}, u32[]{:S(2)}, u32[]{:S(2)}) collective-permute-start(bf16[576,384]{1,0:T(8,128)(2,1)} %get-tuple-element.114), channel_id=1, source_target_pairs={{0,1},{1,0},{2,3},{3,2},{4,5},{5,4},{6,7},{7,6},{8,9},{9,8},{10,11... | collective-permute-start | bytes 1327112 | tf_op jit(solution)/shard_map/ppermute | solution.py:644
  122.0 27.2 %collective-permute-start.17 = (bf16[576,384]{1,0:T(8,128)(2,1)}, bf16[576,384]{1,0:T(8,128)(2,1)}, u32[]{:S(2)}, u32[]{:S(2)}) collective-permute-start(bf16[576,384]{1,0:T(8,128)(2,1)} %get-tuple-element.115), channel_id=1, source_target_pairs={{0,2},{1,3},{2,0},{3,1},{4,6},{5,7},{6,4},{7,5},{8,10},{9,11},{10,... | collective-permute-start | bytes 1327112 | tf_op jit(solution)/shard_map/ppermute | solution.py:644
  123.7 25.5 %collective-permute-start.18 = (bf16[576,384]{1,0:T(8,128)(2,1)}, bf16[576,384]{1,0:T(8,128)(2,1)}, u32[]{:S(2)}, u32[]{:S(2)}) collective-permute-start(bf16[576,384]{1,0:T(8,128)(2,1)} %get-tuple-element.116), channel_id=1, source_target_pairs={{0,3},{1,2},{2,1},{3,0},{4,7},{5,6},{6,5},{7,4},{8,11},{9,10},{10,... | collective-permute-start | bytes 1327112 | tf_op jit(solution)/shard_map/ppermute | solution.py:644
  124.9 1.0 copy-start.1
  128.0 17.7 %collective-permute-start.14 = (bf16[8,48,768]{2,1,0:T(8,128)(2,1)}, bf16[8,48,768]{2,1,0:T(8,128)(2,1)}, u32[]{:S(2)}, u32[]{:S(2)}) collective-permute-start(bf16[8,48,768]{2,1,0:T(8,128)(2,1)} %add_convert_fusion._), channel_id=1, source_target_pairs={{0,4},{1,5},{2,6},{3,7},{4,0},{5,1},{6,2},{7,3},{8,12},{9,13},{10,... | collective-permute-start | bytes 1769480 | tf_op jit(solution)/shard_map/ppermute | solution.py:644
  147.7 9.1 %collective-permute-start.15 = (bf16[4,48,768]{2,1,0:T(8,128)(2,1)}, bf16[4,48,768]{2,1,0:T(8,128)(2,1)}, u32[]{:S(2)}, u32[]{:S(2)}) collective-permute-start(bf16[4,48,768]{2,1,0:T(8,128)(2,1)} %add_convert_fusion.1), channel_id=1, source_target_pairs={{0,2},{1,3},{2,0},{3,1},{4,6},{5,7},{6,4},{7,5},{8,10},{9,11},{10,... | collective-permute-start | bytes 884744 | tf_op jit(solution)/shard_map/ppermute | solution.py:644
  149.3 9.7 %collective-permute-start.19 = (bf16[16,48,384]{2,1,0:T(8,128)(2,1)}, bf16[16,48,384]{2,1,0:T(8,128)(2,1)}, u32[]{:S(2)}, u32[]{:S(2)}) collective-permute-start(bf16[16,48,384]{2,1,0:T(8,128)(2,1)} %shard_map.339), channel_id=1, source_target_pairs={{0,1},{1,0},{2,3},{3,2},{4,5},{5,4},{6,7},{7,6},{8,9},{9,8},{10,11... | collective-permute-start | bytes 1769480 | tf_op jit(solution)/shard_map/ppermute | solution.py:644
  153.3 5.7 %copy-start.2 = (bf16[16,48,384]{2,1,0:T(8,128)(2,1)S(1)}, bf16[16,48,384]{2,1,0:T(8,128)(2,1)}, u32[]{:S(2)}) copy-start(bf16[16,48,384]{2,1,0:T(8,128)(2,1)} %get-tuple-element.112) | copy-start | bytes 1769476
  162.0 7.6 %collective-permute-start.22 = (bf16[4,48,384]{2,1,0:T(8,128)(2,1)}, bf16[4,48,384]{2,1,0:T(8,128)(2,1)}, u32[]{:S(2)}, u32[]{:S(2)}) collective-permute-start(bf16[4,48,384]{2,1,0:T(8,128)(2,1)} %get-tuple-element.162), channel_id=1, source_target_pairs={{0,6},{1,7},{2,4},{3,5},{4,2},{5,3},{6,0},{7,1},{8,14},{9,15},{10,... | collective-permute-start | bytes 442376 | tf_op jit(solution)/shard_map/ppermute | solution.py:644
  163.5 7.7 %collective-permute-start.21 = (bf16[4,48,384]{2,1,0:T(8,128)(2,1)}, bf16[4,48,384]{2,1,0:T(8,128)(2,1)}, u32[]{:S(2)}, u32[]{:S(2)}) collective-permute-start(bf16[4,48,384]{2,1,0:T(8,128)(2,1)} %get-tuple-element.163), channel_id=1, source_target_pairs={{0,4},{1,5},{2,6},{3,7},{4,0},{5,1},{6,2},{7,3},{8,12},{9,13},{10,... | collective-permute-start | bytes 442376 | tf_op jit(solution)/shard_map/ppermute | solution.py:644
  165.0 6.2 %collective-permute-start.20 = (bf16[4,48,384]{2,1,0:T(8,128)(2,1)}, bf16[4,48,384]{2,1,0:T(8,128)(2,1)}, u32[]{:S(2)}, u32[]{:S(2)}) collective-permute-start(bf16[4,48,384]{2,1,0:T(8,128)(2,1)} %get-tuple-element.161.refs_1_), channel_id=1, source_target_pairs={{0,2},{1,3},{2,0},{3,1},{4,6},{5,7},{6,4},{7,5},{8,10},{9,11},{10,... | collective-permute-start | bytes 442376 | tf_op jit(solution)/shard_map/ppermute | solution.py:644
  172.4 0.7 copy-start
  175.0 16.2 %collective-permute-start.25 = (bf16[1,48,1152]{2,1,0:T(8,128)(2,1)}, bf16[1,48,1152]{2,1,0:T(8,128)(2,1)}, u32[]{:S(2)}, u32[]{:S(2)}) collective-permute-start(bf16[1,48,1152]{2,1,0:T(8,128)(2,1)} %get-tuple-element.164), channel_id=1, source_target_pairs={{0,24},{1,25},{2,26},{3,27},{4,28},{5,29},{6,30},{7,31},{8,16},{9,... | collective-permute-start | bytes 331784 | tf_op jit(solution)/shard_map/ppermute | solution.py:644
  177.5 13.7 %collective-permute-start.24 = (bf16[1,48,1152]{2,1,0:T(8,128)(2,1)}, bf16[1,48,1152]{2,1,0:T(8,128)(2,1)}, u32[]{:S(2)}, u32[]{:S(2)}) collective-permute-start(bf16[1,48,1152]{2,1,0:T(8,128)(2,1)} %get-tuple-element.165), channel_id=1, source_target_pairs={{0,16},{1,17},{2,18},{3,19},{4,20},{5,21},{6,22},{7,23},{8,24},{9,... | collective-permute-start | bytes 331784 | tf_op jit(solution)/shard_map/ppermute | solution.py:644
  177.5 13.7 %collective-permute-start.23 = (bf16[1,48,1152]{2,1,0:T(8,128)(2,1)}, bf16[1,48,1152]{2,1,0:T(8,128)(2,1)}, u32[]{:S(2)}, u32[]{:S(2)}) collective-permute-start(bf16[1,48,1152]{2,1,0:T(8,128)(2,1)} %get-tuple-element.166._), channel_id=1, source_target_pairs={{0,8},{1,9},{2,10},{3,11},{4,12},{5,13},{6,14},{7,15},{8,0},{9,1},... | collective-permute-start | bytes 331784 | tf_op jit(solution)/shard_map/ppermute | solution.py:644
  188.1 25.2 %collective-permute-start.27 = (bf16[576,384]{1,0:T(8,128)(2,1)}, bf16[576,384]{1,0:T(8,128)(2,1)}, u32[]{:S(2)}, u32[]{:S(2)}) collective-permute-start(bf16[576,384]{1,0:T(8,128)(2,1)} %get-tuple-element.132), channel_id=1, source_target_pairs={{0,2},{1,3},{2,0},{3,1},{4,6},{5,7},{6,4},{7,5},{8,10},{9,11},{10,... | collective-permute-start | bytes 1327112 | tf_op jit(solution)/shard_map/ppermute | solution.py:644
  191.2 22.5 %collective-permute-start.28 = (bf16[576,384]{1,0:T(8,128)(2,1)}, bf16[576,384]{1,0:T(8,128)(2,1)}, u32[]{:S(2)}, u32[]{:S(2)}) collective-permute-start(bf16[576,384]{1,0:T(8,128)(2,1)} %get-tuple-element.133), channel_id=1, source_target_pairs={{0,3},{1,2},{2,1},{3,0},{4,7},{5,6},{6,5},{7,4},{8,11},{9,10},{10,... | collective-permute-start | bytes 1327112 | tf_op jit(solution)/shard_map/ppermute | solution.py:644
  193.8 19.9 %collective-permute-start.26 = (bf16[576,384]{1,0:T(8,128)(2,1)}, bf16[576,384]{1,0:T(8,128)(2,1)}, u32[]{:S(2)}, u32[]{:S(2)}) collective-permute-start(bf16[576,384]{1,0:T(8,128)(2,1)} %shard_map.346), channel_id=1, source_target_pairs={{0,1},{1,0},{2,3},{3,2},{4,5},{5,4},{6,7},{7,6},{8,9},{9,8},{10,11... | collective-permute-start | bytes 1327112 | tf_op jit(solution)/shard_map/ppermute | solution.py:644
  194.5 5.1 %collective-permute-start.31 = (f32[24,384]{1,0:T(8,128)}, f32[24,384]{1,0:T(8,128)S(1)}, u32[]{:S(2)}, u32[]{:S(2)}) collective-permute-start(f32[24,384]{1,0:T(8,128)} %get-tuple-element.136), channel_id=1, source_target_pairs={{0,12},{1,13},{2,14},{3,15},{4,8},{5,9},{6,10},{7,11},{8,4},{9,5},... | collective-permute-start | bytes 110600 | tf_op jit(solution)/shard_map/ppermute | solution.py:644
  194.6 5.5 %collective-permute-start.30 = (f32[24,384]{1,0:T(8,128)}, f32[24,384]{1,0:T(8,128)S(1)}, u32[]{:S(2)}, u32[]{:S(2)}) collective-permute-start(f32[24,384]{1,0:T(8,128)} %get-tuple-element.136), channel_id=1, source_target_pairs={{0,8},{1,9},{2,10},{3,11},{4,12},{5,13},{6,14},{7,15},{8,0},{9,1},... | collective-permute-start | bytes 110600 | tf_op jit(solution)/shard_map/ppermute | solution.py:644
  199.5 4.2 %collective-permute-start.29 = (f32[24,384]{1,0:T(8,128)}, f32[24,384]{1,0:T(8,128)S(1)}, u32[]{:S(2)}, u32[]{:S(2)}) collective-permute-start(f32[24,384]{1,0:T(8,128)} %get-tuple-element.136), channel_id=1, source_target_pairs={{0,4},{1,5},{2,6},{3,7},{4,0},{5,1},{6,2},{7,3},{8,12},{9,13},{10,... | collective-permute-start | bytes 110600 | tf_op jit(solution)/shard_map/ppermute | solution.py:644
  205.1 5.2 %collective-permute-start.32 = (f32[24,384]{1,0:T(8,128)}, f32[24,384]{1,0:T(8,128)}, u32[]{:S(2)}, u32[]{:S(2)}) collective-permute-start(f32[24,384]{1,0:T(8,128)} %add_add_fusion.refs_0_), channel_id=1, source_target_pairs={{0,16},{1,17},{2,18},{3,19},{4,20},{5,21},{6,22},{7,23},{8,24},{9,... | collective-permute-start | bytes 110600 | tf_op jit(solution)/shard_map/ppermute | solution.py:644
  211.8 4.7 %collective-permute-start.35 = (f32[64,128]{1,0:T(8,128)}, f32[64,128]{1,0:T(8,128)}, u32[]{:S(2)}, u32[]{:S(2)}) collective-permute-start(f32[64,128]{1,0:T(8,128)} %get-tuple-element.138.refs_0_), channel_id=1, source_target_pairs={{0,3},{1,2},{2,1},{3,0},{4,7},{5,6},{6,5},{7,4},{8,11},{9,10},{10,... | collective-permute-start | bytes 98312 | tf_op jit(solution)/shard_map/ppermute | solution.py:644
  211.8 4.7 %collective-permute-start.34 = (f32[64,128]{1,0:T(8,128)}, f32[64,128]{1,0:T(8,128)}, u32[]{:S(2)}, u32[]{:S(2)}) collective-permute-start(f32[64,128]{1,0:T(8,128)} %get-tuple-element.138.refs_0_), channel_id=1, source_target_pairs={{0,2},{1,3},{2,0},{3,1},{4,6},{5,7},{6,4},{7,5},{8,10},{9,11},{10,... | collective-permute-start | bytes 98312 | tf_op jit(solution)/shard_map/ppermute | solution.py:644
  213.3 3.2 %collective-permute-start.33 = (f32[64,128]{1,0:T(8,128)}, f32[64,128]{1,0:T(8,128)}, u32[]{:S(2)}, u32[]{:S(2)}) collective-permute-start(f32[64,128]{1,0:T(8,128)} %get-tuple-element.138.refs_0_), channel_id=1, source_target_pairs={{0,1},{1,0},{2,3},{3,2},{4,5},{5,4},{6,7},{7,6},{8,9},{9,8},{10,11... | collective-permute-start | bytes 98312 | tf_op jit(solution)/shard_map/ppermute | solution.py:644

commit v3 on v2

--- a/solution.py
+++ b/solution.py
@@ -99,7 +99,7 @@
 FF_PER_STEP = 4
 SLICE = 48
 FF_CHUNK = 256
-vmem_bytes = 64 * 1024 * 1024
+vmem_bytes = 60 * 1024 * 1024
 
 
 def dot(left, right, left_axis=1, right_axis=0):
@@ -913,8 +913,8 @@
     middle_ref, attended_ref, proj_t_ref, vectors_ref = refs[:4]
     outputs, refs = refs[4 : 4 + spread], refs[4 + spread :]
     d_middle_ref, d_attended_ref, keep_ref, leave_ref, proj_total_ref, vector_sums_ref, up_sums_ref = refs[:7]
-    w_up_ref, w_down_ref, down_low_ref, packed_ref, bias_up_ref, wide_ref = refs[7:13]
-    scratches = refs[13:]
+    w_up_ref, w_down_ref, packed_ref, bias_up_ref, wide_ref = refs[7:12]
+    scratches = refs[12:]
     width = w_up_ref.shape[0]
     up_total_ref, down_total_ref = scratches[-2:]
     rows = packed_ref.shape[1]
@@ -947,15 +947,13 @@
     @pl.when(pl.program_id(0) == pl.num_programs(0) - 1)
     def _():
         narrow_pieces(place_ref, wide_ref, outputs, spread)
-        down_low_ref[...] = down_total_ref[...].T.astype(jnp.bfloat16)
 
         def take(row, col):
             across = slice(row * rows, (row + 1) * rows)
-            cols = slice(col * out_cols, (col + 1) * out_cols)
             parts = [up_total_ref[across, col * up_cols : (col + 1) * up_cols].astype(jnp.bfloat16)]
-            for fold in range(folds):
-                down = (row * folds + fold) * rows
-                parts.append(down_low_ref[down : down + rows, cols])
+            lanes = slice(row * folds * rows, (row + 1) * folds * rows)
+            for start in range(col * out_cols, (col + 1) * out_cols, rows):
+                parts.append(down_total_ref[start : start + rows, lanes].astype(jnp.bfloat16))
             return jnp.concatenate(parts, axis=1)
 
         pack(place_ref, take, keep_ref, leave_ref, dp_size, spread)
@@ -1104,7 +1102,12 @@
     qkv_cols, out_cols = grads[0].shape[1], grads[1].shape[1]
     folds = grads[3].shape[0] // rows
     up = blocks[:, :up_cols]
-    downs = [blocks[:, up_cols + fold * out_cols :][:, :out_cols] for fold in range(folds)]
+    turned = [
+        blocks[:, up_cols + part * folds * rows : up_cols + (part + 1) * folds * rows]
+        for part in range(out_cols // rows)
+    ]
+    down = jnp.concatenate(turned, axis=0).T
+    downs = [down[fold * rows : (fold + 1) * rows] for fold in range(folds)]
     start = up_cols + folds * out_cols
     qkv = blocks[:, start : start + qkv_cols]
     proj = blocks[:, start + qkv_cols :]
@@ -1349,7 +1352,6 @@
         [
             scratch(width, hidden, dtype=low),
             scratch(hidden, width, dtype=low),
-            scratch(hidden, width, dtype=low),
             scratch(dp_size * spread, rows, second_cols, dtype=low),
             scratch(1, hidden),
             wide,
@@ -1480,7 +1482,7 @@
     powers = all(size & (size - 1) == 0 for size in (spread, dp_size))
     fits = powers and spread == 4 and dp_size > 2
     fits = fits and arrays[5].shape[1] <= width and folds <= 5
-    fits = fits and rows % 16 == 0 and images % FF_PER_STEP == 0 and images > 2 * PER_STEP and images % 16 == 0 and slots % 4 == 0
+    fits = fits and arrays[6].shape[1] % rows == 0 and rows % 16 == 0 and images % FF_PER_STEP == 0 and images > 2 * PER_STEP and images % 16 == 0 and slots % 4 == 0
     return packed_body(*arrays) if fits else general_body(*arrays)
 
 

time: 220 us -> 211 us (0.959)
  other arithmetic: 13.9 us -> 5.72 us
  local copies, waits for them, and re-layouts: 5.3 us -> 9.86 us
  waiting for transfers between devices: 32.9 us -> 28.4 us
    unnamed x18 -> x66, local copies, waits for them, and re-layouts: 3.79 us -> 9.79 us
    ppermute x36, waiting for transfers between devices: 32.9 us -> 28.4 us  [permute(): lax.ppermute(array, ('dp', 'group'), [(rank, rank ^ mask) for rank in ran...]
    another operation x2, other arithmetic: 3.33 us -> 0.19 us
    add x2, other arithmetic: 3.45 us -> 1.16 us  [add_wide(): total = total + part.astype(jnp.float32)]
  transfers between devices with their start and end apart: 38 -> 38, of which waited for: 14 -> 13; matrix products, arithmetic and copies ran while one was open for 4% -> 3% of each run, Pallas kernels for 33% -> 34%
where the time goes in v3:
time: 211 us; the launch traced here: 210 us
  Pallas kernels  120 us (57%)
  starting transfers between devices  45 us (21%)
  waiting for transfers between devices  28.4 us (13%)
  local copies, waits for them, and re-layouts  9.86 us (5%)
  other arithmetic  5.72 us (3%)
    pallas_call x7, Pallas kernels, call_kernel(): pl.pallas_call(functools.partial(kernel, *statics), grid=(steps,), in_spe...  97.3 us
    ppermute x36, starting transfers between devices, permute(): lax.ppermute(array, ('dp', 'group'), [(rank, rank ^ mask) for rank in ran...  37.7 us
    ppermute x36, waiting for transfers between devices, permute(): lax.ppermute(array, ('dp', 'group'), [(rank, rank ^ mask) for rank in ran...  28.4 us
    unnamed x66, local copies, waits for them, and re-layouts  9.79 us
    all_to_all x2, starting transfers between devices, to_group(): lax.all_to_all(parts, 'group', split_axis=0, concat_axis=0, tiled=True)  7.29 us
    pallas_call x2, Pallas kernels, settle(): small(functools.partial(settle_kernel, spread), in_specs=[in_smem] + [in_...  5.55 us
  transfers between devices with their start and end apart: 38, of which 13 were waited for; matrix products, arithmetic and copies ran while one was open for 3% of the time, Pallas kernels for 34%

profile of v3, /device:TPU:0, one launch (start us, length us, event | category | flops | bytes accessed | tf_op | source)
XLA Modules:
  0.0 210.4 jit_solution(7115931570658868655)
XLA Ops:
  0.7 1.7 shard_map.329.own_ref
  2.4 3.0 %collective-permute-start = (bf16[48,1152]{1,0:T(8,128)(2,1)}, bf16[48,1152]{1,0:T(8,128)(2,1)S(1)}, u32[]{:S(2)}, u32[]{:S(2)}) collective-permute-start(bf16[48,1152]{1,0:T(8,128)(2,1)} %shard_map.329.own_ref), channel_id=1, source_target_pairs={{0,2},{1,3},{2,0},{3,1},{4,6},{5,7},{6,4},{7,5},{8,10},{9,11},{10,... | collective-permute-start | bytes 331784 | tf_op jit(solution)/shard_map/ppermute | solution.py:644
  5.3 2.8 %shard_map.328._ = bf16[4,36,16,384]{3,2,1,0:T(8,128)(2,1)} custom-call(bf16[36,64,384]{2,1,0:T(8,128)(2,1)} %bitcast.16), custom_call_target="tpu_custom_call" | custom-call | tf_op jit(solution)/shard_map/pallas_call | solution.py:1259
  9.3 2.9 %shard_map.330 = (bf16[4,36,16,384]{3,2,1,0:T(8,128)(2,1)}, bf16[2,48,384]{2,1,0:T(8,128)(2,1)}, bf16[2,48,768]{2,1,0:T(8,128)(2,1)}) custom-call(bf16[36,64,384]{2,1,0:T(8,128)(2,1)} %bitcast.15, bf16[48,1152]{1,0:T(8,128)(2,1)} %shard_map.329.own_ref, bf16[48,1152]{1,0:T(8,128)(2,1)} %copy-done.18, bf16[4,36,16,384]{3,2,1,0:T(8,128)(2,1)} %shard_map.328._), custom_call_target="tpu_custom_call" | custom-call | tf_op jit(solution)/shard_map/pallas_call | solution.py:1260
  12.2 3.7 %all-to-all-start.1 = ((bf16[4,36,16,384]{3,2,1,0:T(8,128)(2,1)}), bf16[4,36,16,384]{3,2,1,0:T(8,128)(2,1)S(1)}, u32[]{:S(2)}, u32[]{:S(2)}) async-start(bf16[4,36,16,384]{3,2,1,0:T(8,128)(2,1)} %get-tuple-element.91), calls=%async_computation.1 | async-start | bytes 3538944 | tf_op jit(solution)/shard_map/all_to_all | solution.py:1233
  15.9 3.9 %collective-permute-start.6 = (bf16[2,48,384]{2,1,0:T(8,128)(2,1)S(1)}, bf16[2,48,384]{2,1,0:T(8,128)(2,1)S(1)}, u32[]{:S(2)}, u32[]{:S(2)}) collective-permute-start(bf16[2,48,384]{2,1,0:T(8,128)(2,1)S(1)} %copy-done.23), channel_id=1, source_target_pairs={{0,24},{1,25},{2,26},{3,27},{4,28},{5,29},{6,30},{7,31},{8,16},{9,... | collective-permute-start | bytes 221192 | tf_op jit(solution)/shard_map/ppermute | solution.py:644
  20.4 2.5 %collective-permute-done.6.refs_3_ = bf16[2,48,384]{2,1,0:T(8,128)(2,1)S(1)} collective-permute-done((bf16[2,48,384]{2,1,0:T(8,128)(2,1)S(1)}, bf16[2,48,384]{2,1,0:T(8,128)(2,1)S(1)}, u32[]{:S(2)}, u32[]{:S(2)}) %collective-permute-start.6) | collective-permute-done | bytes 73760 | tf_op jit(solution)/shard_map/ppermute | solution.py:644
  23.0 3.6 %collective-permute-done.5.refs_2_ = bf16[2,48,384]{2,1,0:T(8,128)(2,1)S(1)} collective-permute-done((bf16[2,48,384]{2,1,0:T(8,128)(2,1)S(1)}, bf16[2,48,384]{2,1,0:T(8,128)(2,1)S(1)}, u32[]{:S(2)}, u32[]{:S(2)}) %collective-permute-start.5) | collective-permute-done | bytes 73760 | tf_op jit(solution)/shard_map/ppermute | solution.py:644
  27.8 1.8 shard_map.331.refs_0_
  29.6 1.5 collective-permute-start.7
  31.1 7.4 %collective-permute-done.7.refs_1_ = bf16[8,48,384]{2,1,0:T(8,128)(2,1)} collective-permute-done((bf16[8,48,384]{2,1,0:T(8,128)(2,1)}, bf16[8,48,384]{2,1,0:T(8,128)(2,1)}, u32[]{:S(2)}, u32[]{:S(2)}) %collective-permute-start.7) | collective-permute-done | bytes 294944 | tf_op jit(solution)/shard_map/ppermute | solution.py:644
  38.5 2.5 %collective-permute-start.3 = (bf16[2,48,768]{2,1,0:T(8,128)(2,1)}, bf16[2,48,768]{2,1,0:T(8,128)(2,1)}, u32[]{:S(2)}, u32[]{:S(2)}) collective-permute-start(bf16[2,48,768]{2,1,0:T(8,128)(2,1)} %get-tuple-element.90.refs_0_), channel_id=1, source_target_pairs={{0,24},{1,25},{2,26},{3,27},{4,28},{5,29},{6,30},{7,31},{8,16},{9,... | collective-permute-start | bytes 442376 | tf_op jit(solution)/shard_map/ppermute | solution.py:644
  40.9 1.9 collective-permute-start.1
  42.9 1.2 copy-done.3
  44.1 3.6 %all-to-all-start = ((bf16[4,36,16,384]{3,2,1,0:T(8,128)(2,1)}), bf16[4,36,16,384]{3,2,1,0:T(8,128)(2,1)S(1)}, u32[]{:S(2)}, u32[]{:S(2)}) async-start(bf16[4,36,16,384]{3,2,1,0:T(8,128)(2,1)} %shard_map.328._), calls=%async_computation | async-start | bytes 3538944 | tf_op jit(solution)/shard_map/all_to_all | solution.py:1233
  47.7 10.3 %shard_map.332 = (bf16[2304,1152]{1,0:T(8,128)(2,1)}, bf16[16,3,144,288]{3,2,1,0:T(8,128)(2,1)}, bf16[2304,384]{1,0:T(8,128)(2,1)}, f32[2304,384]{1,0:T(8,128)},...) custom-call(s32[1]{0:T(128)} %bitcast.place_ref, ...), custom_call_target="tpu_custom_call" | custom-call | flops 7474249728 | bytes 23473156 | tf_op jit(solution)/shard_map/pallas_call | solution.py:536
  58.0 2.0 shard_map.333.refs_0_
  60.0 1.5 collective-permute-start.10
  61.4 12.5 %shard_map.334 = (bf16[2304,1152]{1,0:T(8,128)(2,1)}, bf16[16,3,144,288]{3,2,1,0:T(8,128)(2,1)}, bf16[2304,384]{1,0:T(8,128)(2,1)}, f32[2304,384]{1,0:T(8,128)}, bf16[2304,384]{1,0:T(8,128)(2,1)}) custom-call(bf16[2304,384]{1,0:T(8,128)(2,1)} %get-tuple-element.94.x_ref, ...), custom_call_target="tpu_custom_call", output_to_operand_aliasing={{0}: (5, {}), {1}: (6, {}), {2}: (7, {}), {3}: (8, {}), {4}... | custom-call | flops 22422749184 | bytes 35712000 | tf_op jit(solution)/shard_map/pallas_call | solution.py:536
  73.9 1.9 collective-permute-done.10.refs_0_
  77.8 1.1 collective-permute-done.12.refs_4_
  80.6 41.5 %shard_map.337 = (bf16[576,384]{1,0:T(8,128)(2,1)}, bf16[576,384]{1,0:T(8,128)(2,1)}, bf16[576,384]{1,0:T(8,128)(2,1)}, bf16[576,384]{1,0:T(8,128)(2,1)}, f32[23...) custom-call(s32[1]{0:T(128)} %bitcast.place_ref, ...), custom_call_target="tpu_custom_call" | custom-call | flops 141331267584 | bytes 19795972 | tf_op jit(solution)/shard_map/pallas_call | solution.py:536
  122.7 1.7 collective-permute-start.17
  125.2 1.6 add_convert_fusion._
  126.8 1.6 collective-permute-start.14
  128.4 16.4 %shard_map.338 = (bf16[2304,1152]{1,0:T(8,128)(2,1)}, bf16[16,48,384]{2,1,0:T(8,128)(2,1)}, bf16[16,48,384]{2,1,0:T(8,128)(2,1)}, f32[8,384]{1,0:T(8,128)}) custom-call(s32[1]{0:T(128)} %bitcast.place_ref, bf16[2304,384]{1,0:T(8,128)(2,1)} %get-tuple-element.107.normed_ref, bf16[2304,1152]{1,0:T(8,128)(2,1)} %get-tuple-element.108.qkv_ref, ...), custom_call_target="tpu_custom_call" | custom-call | flops 32614907904 | bytes 20527108 | tf_op jit(solution)/shard_map/pallas_call | solution.py:536
  144.8 1.3 add_convert_fusion.1
  146.1 1.7 collective-permute-start.15
  149.0 4.0 %shard_map.340 = (bf16[2304,384]{1,0:T(8,128)(2,1)}, f32[8,384]{1,0:T(8,128)}) custom-call(bf16[2304,384]{1,0:T(8,128)(2,1)} %get-tuple-element.94.x_ref, bf16[2304,1152]{1,0:T(8,128)(2,1)} %get-tuple-element.117.d_projected_ref, f32[2304,384]{1,0:T(8,128)} %get-tuple-element.118.d_middle_ref, bf16[1152,384]{1,0:T(8,128)(2,1)} %get-tuple-element.119.qkv_t_ref, ...), custom_call_target="tpu_custom_call" | custom-call | flops 4076863488 | bytes 13314048 | tf_op jit(solution)/shard_map/pallas_call | solution.py:536
  153.0 2.0 collective-permute-done.15
  155.0 1.1 convert_add_fusion.1
  156.3 2.2 %collective-permute-start.22 = (bf16[4,48,384]{2,1,0:T(8,128)(2,1)S(1)}, bf16[4,48,384]{2,1,0:T(8,128)(2,1)S(1)}, u32[]{:S(2)}, u32[]{:S(2)}) collective-permute-start(bf16[4,48,384]{2,1,0:T(8,128)(2,1)S(1)} %get-tuple-element.162), channel_id=1, source_target_pairs={{0,6},{1,7},{2,4},{3,5},{4,2},{5,3},{6,0},{7,1},{8,14},{9,15},{10,... | collective-permute-start | bytes 442376 | tf_op jit(solution)/shard_map/ppermute | solution.py:644
  159.9 3.9 %shard_map.341 = (bf16[2304,384]{1,0:T(8,128)(2,1)}, f32[8,384]{1,0:T(8,128)}) custom-call(bf16[2304,384]{1,0:T(8,128)(2,1)} %get-tuple-element.94.x_ref, bf16[2304,1152]{1,0:T(8,128)(2,1)} %get-tuple-element.117.d_projected_ref, f32[2304,384]{1,0:T(8,128)} %get-tuple-element.118.d_middle_ref, ...), custom_call_target="tpu_custom_call", output_to_operand_aliasing={{0}: (6, {})} | custom-call | flops 4076863488 | bytes 15230976 | tf_op jit(solution)/shard_map/pallas_call | solution.py:536
  163.8 1.6 collective-permute-done.21
  165.5 2.6 %collective-permute-start.25 = (bf16[1,48,1152]{2,1,0:T(8,128)(2,1)S(1)}, bf16[1,48,1152]{2,1,0:T(8,128)(2,1)S(1)}, u32[]{:S(2)}, u32[]{:S(2)}) collective-permute-start(bf16[1,48,1152]{2,1,0:T(8,128)(2,1)S(1)} %get-tuple-element.164), channel_id=1, source_target_pairs={{0,24},{1,25},{2,26},{3,27},{4,28},{5,29},{6,30},{7,31},{8,16},{9,... | collective-permute-start | bytes 331784 | tf_op jit(solution)/shard_map/ppermute | solution.py:644
  168.1 1.9 collective-permute-start.23
  170.0 8.7 %shard_map.342 = (bf16[576,384]{1,0:T(8,128)(2,1)}, bf16[576,384]{1,0:T(8,128)(2,1)}, bf16[576,384]{1,0:T(8,128)(2,1)}, bf16[576,384]{1,0:T(8,128)(2,1)}, f32[8,384]{1,0:T(8,128)}) custom-call(s32[1]{0:T(128)} %bitcast.place_ref, bf16[2304,384]{1,0:T(8,128)(2,1)} %get-tuple-element.94.x_ref, bf16[2304,1152]{1,0:T(8,128)(2,1)} %get-tuple-element.117.d_projected_ref, ...), custom_call_target="tpu_custom_call" | custom-call | flops 8153726976 | bytes 15194116 | tf_op jit(solution)/shard_map/pallas_call | solution.py:536
  178.7 1.5 collective-permute-start.27
  181.6 2.3 %shard_map.343 = (f32[48,288]{1,0:T(8,128)}, f32[48,96]{1,0:T(8,128)}, f32[48,384]{1,0:T(8,128)}, f32[192,96]{1,0:T(8,128)}, f32[8,48]{1,0:T(8,128)}, /*index=5*/f32[24,384]{1,0:T(8,128)}) custom-call(f32[1,48,1152]{2,1,0:T(8,128)} %fusion.3.refs_0_, bf16[1,48,1152]{2,1,0:T(8,128)(2,1)} %copy-done.21, bf16[1,48,1152]{2,1,0:T(8,128)(2,1)} %copy-done.20, ...), custom_call_target="tpu_custom_call" | custom-call | tf_op jit(solution)/shard_map/pallas_call | solution.py:1442
  185.5 1.9 collective-permute-start.30
  187.4 2.3 %collective-permute-done.31 = f32[24,384]{1,0:T(8,128)S(1)} collective-permute-done((f32[24,384]{1,0:T(8,128)}, f32[24,384]{1,0:T(8,128)S(1)}, u32[]{:S(2)}, u32[]{:S(2)}) %collective-permute-start.31) | collective-permute-done | bytes 36896 | tf_op jit(solution)/shard_map/ppermute | solution.py:644
  189.7 1.3 collective-permute-start.29
  191.0 2.8 %collective-permute-done.29 = f32[24,384]{1,0:T(8,128)S(1)} collective-permute-done((f32[24,384]{1,0:T(8,128)}, f32[24,384]{1,0:T(8,128)S(1)}, u32[]{:S(2)}, u32[]{:S(2)}) %collective-permute-start.29) | collective-permute-done | bytes 36896 | tf_op jit(solution)/shard_map/ppermute | solution.py:644
  195.7 2.8 %shard_map.345 = (bf16[36,64,384]{2,1,0:T(8,128)(2,1)}, f32[8,128]{1,0:T(8,128)}) custom-call(s32[1]{0:T(128)} %bitcast.place_ref, bf16[36,16,384]{2,1,0:T(8,128)(2,1)} %bitcast.19, bf16[36,16,384]{2,1,0:T(8,128)(2,1)} %bitcast.20, bf16[36,16,384]{2,1,0:T(8,128)(2,1)} %bitcast.21, bf16[36,16,384]{2,1,0:T(8,128)(2,1)} %bitcast.22), custom_call_target="tpu_custom_call" | custom-call | tf_op jit(solution)/shard_map/pallas_call | solution.py:1243
  200.2 1.5 shard_map.348
  201.7 1.5 collective-permute-start.34
  204.5 2.8 %shard_map.347 = (bf16[36,64,384]{2,1,0:T(8,128)(2,1)}, f32[8,128]{1,0:T(8,128)}) custom-call(s32[1]{0:T(128)} %bitcast.place_ref, bf16[36,16,384]{2,1,0:T(8,128)(2,1)} %bitcast.23, bf16[36,16,384]{2,1,0:T(8,128)(2,1)} %bitcast.26, bf16[36,16,384]{2,1,0:T(8,128)(2,1)} %bitcast.24, bf16[36,16,384]{2,1,0:T(8,128)(2,1)} %bitcast.25), custom_call_target="tpu_custom_call" | custom-call | tf_op jit(solution)/shard_map/pallas_call | solution.py:1243
  207.9 2.3 %shard_map.349 = (f32[48,288]{1,0:T(8,128)}, f32[48,96]{1,0:T(8,128)}, f32[48,384]{1,0:T(8,128)}, f32[192,96]{1,0:T(8,128)}, f32[288]{0:T(512)}, /*index=5*/f32[...) custom-call(f32[64,128]{1,0:T(8,128)} %get-tuple-element.138.refs_0_, ...), custom_call_target="tpu_custom_call" | custom-call | tf_op jit(solution)/shard_map/pallas_call | solution.py:1464
  (126 shorter events, 19.3 us)
Async XLA Ops:
  2.4 6.2 %collective-permute-start = (bf16[48,1152]{1,0:T(8,128)(2,1)}, bf16[48,1152]{1,0:T(8,128)(2,1)S(1)}, u32[]{:S(2)}, u32[]{:S(2)}) collective-permute-start(bf16[48,1152]{1,0:T(8,128)(2,1)} %shard_map.329.own_ref), channel_id=1, source_target_pairs={{0,2},{1,3},{2,0},{3,1},{4,6},{5,7},{6,4},{7,5},{8,10},{9,11},{10,... | collective-permute-start | bytes 331784 | tf_op jit(solution)/shard_map/ppermute | solution.py:644
  12.2 3.7 %copy-start.23 = (bf16[2,48,384]{2,1,0:T(8,128)(2,1)S(1)}, bf16[2,48,384]{2,1,0:T(8,128)(2,1)}, u32[]{:S(2)}) copy-start(bf16[2,48,384]{2,1,0:T(8,128)(2,1)} %get-tuple-element.92.refs_0_) | copy-start | bytes 221188
  12.2 30.7 %all-to-all-start.1 = ((bf16[4,36,16,384]{3,2,1,0:T(8,128)(2,1)}), bf16[4,36,16,384]{3,2,1,0:T(8,128)(2,1)S(1)}, u32[]{:S(2)}, u32[]{:S(2)}) async-start(bf16[4,36,16,384]{3,2,1,0:T(8,128)(2,1)} %get-tuple-element.91), calls=%async_computation.1 | async-start | bytes 3538944 | tf_op jit(solution)/shard_map/all_to_all | solution.py:1233
  15.9 7.1 %collective-permute-start.6 = (bf16[2,48,384]{2,1,0:T(8,128)(2,1)S(1)}, bf16[2,48,384]{2,1,0:T(8,128)(2,1)S(1)}, u32[]{:S(2)}, u32[]{:S(2)}) collective-permute-start(bf16[2,48,384]{2,1,0:T(8,128)(2,1)S(1)} %copy-done.23), channel_id=1, source_target_pairs={{0,24},{1,25},{2,26},{3,27},{4,28},{5,29},{6,30},{7,31},{8,16},{9,... | collective-permute-start | bytes 221192 | tf_op jit(solution)/shard_map/ppermute | solution.py:644
  19.8 6.8 %collective-permute-start.5 = (bf16[2,48,384]{2,1,0:T(8,128)(2,1)S(1)}, bf16[2,48,384]{2,1,0:T(8,128)(2,1)S(1)}, u32[]{:S(2)}, u32[]{:S(2)}) collective-permute-start(bf16[2,48,384]{2,1,0:T(8,128)(2,1)S(1)} %copy-done.23), channel_id=1, source_target_pairs={{0,16},{1,17},{2,18},{3,19},{4,20},{5,21},{6,22},{7,23},{8,24},{9,... | collective-permute-start | bytes 221192 | tf_op jit(solution)/shard_map/ppermute | solution.py:644
  19.8 6.8 %collective-permute-start.4 = (bf16[2,48,384]{2,1,0:T(8,128)(2,1)S(1)}, bf16[2,48,384]{2,1,0:T(8,128)(2,1)S(1)}, u32[]{:S(2)}, u32[]{:S(2)}) collective-permute-start(bf16[2,48,384]{2,1,0:T(8,128)(2,1)S(1)} %copy-done.23), channel_id=1, source_target_pairs={{0,8},{1,9},{2,10},{3,11},{4,12},{5,13},{6,14},{7,15},{8,0},{9,1},... | collective-permute-start | bytes 221192 | tf_op jit(solution)/shard_map/ppermute | solution.py:644
  23.0 3.6 %copy-start.24 = (bf16[2,48,384]{2,1,0:T(8,128)(2,1)}, bf16[2,48,384]{2,1,0:T(8,128)(2,1)S(1)}, u32[]{:S(2)}) copy-start(bf16[2,48,384]{2,1,0:T(8,128)(2,1)S(1)} %collective-permute-done.6.refs_3_) | copy-start | bytes 221188
  29.6 8.9 %collective-permute-start.7 = (bf16[8,48,384]{2,1,0:T(8,128)(2,1)}, bf16[8,48,384]{2,1,0:T(8,128)(2,1)}, u32[]{:S(2)}, u32[]{:S(2)}) collective-permute-start(bf16[8,48,384]{2,1,0:T(8,128)(2,1)} %shard_map.331.refs_0_), channel_id=1, source_target_pairs={{0,4},{1,5},{2,6},{3,7},{4,0},{5,1},{6,2},{7,3},{8,12},{9,13},{10,... | collective-permute-start | bytes 884744 | tf_op jit(solution)/shard_map/ppermute | solution.py:644
  31.1 16.6 %collective-permute-start.8 = (bf16[8,48,384]{2,1,0:T(8,128)(2,1)}, bf16[8,48,384]{2,1,0:T(8,128)(2,1)}, u32[]{:S(2)}, u32[]{:S(2)}) collective-permute-start(bf16[8,48,384]{2,1,0:T(8,128)(2,1)} %shard_map.331.refs_0_), channel_id=1, source_target_pairs={{0,1},{1,0},{2,3},{3,2},{4,5},{5,4},{6,7},{7,6},{8,9},{9,8},{10,11... | collective-permute-start | bytes 884744 | tf_op jit(solution)/shard_map/ppermute | solution.py:644
  38.5 9.2 %collective-permute-start.9 = (bf16[8,48,384]{2,1,0:T(8,128)(2,1)}, bf16[8,48,384]{2,1,0:T(8,128)(2,1)}, u32[]{:S(2)}, u32[]{:S(2)}) collective-permute-start(bf16[8,48,384]{2,1,0:T(8,128)(2,1)} %collective-permute-done.7.refs_1_), channel_id=1, source_target_pairs={{0,1},{1,0},{2,3},{3,2},{4,5},{5,4},{6,7},{7,6},{8,9},{9,8},{10,11... | collective-permute-start | bytes 884744 | tf_op jit(solution)/shard_map/ppermute | solution.py:644
  38.5 19.5 %collective-permute-start.3 = (bf16[2,48,768]{2,1,0:T(8,128)(2,1)}, bf16[2,48,768]{2,1,0:T(8,128)(2,1)}, u32[]{:S(2)}, u32[]{:S(2)}) collective-permute-start(bf16[2,48,768]{2,1,0:T(8,128)(2,1)} %get-tuple-element.90.refs_0_), channel_id=1, source_target_pairs={{0,24},{1,25},{2,26},{3,27},{4,28},{5,29},{6,30},{7,31},{8,16},{9,... | collective-permute-start | bytes 442376 | tf_op jit(solution)/shard_map/ppermute | solution.py:644
  40.9 17.0 %collective-permute-start.2 = (bf16[2,48,768]{2,1,0:T(8,128)(2,1)}, bf16[2,48,768]{2,1,0:T(8,128)(2,1)}, u32[]{:S(2)}, u32[]{:S(2)}) collective-permute-start(bf16[2,48,768]{2,1,0:T(8,128)(2,1)} %get-tuple-element.90.refs_0_), channel_id=1, source_target_pairs={{0,16},{1,17},{2,18},{3,19},{4,20},{5,21},{6,22},{7,23},{8,24},{9,... | collective-permute-start | bytes 442376 | tf_op jit(solution)/shard_map/ppermute | solution.py:644
  40.9 17.0 %collective-permute-start.1 = (bf16[2,48,768]{2,1,0:T(8,128)(2,1)}, bf16[2,48,768]{2,1,0:T(8,128)(2,1)}, u32[]{:S(2)}, u32[]{:S(2)}) collective-permute-start(bf16[2,48,768]{2,1,0:T(8,128)(2,1)} %get-tuple-element.90.refs_0_), channel_id=1, source_target_pairs={{0,8},{1,9},{2,10},{3,11},{4,12},{5,13},{6,14},{7,15},{8,0},{9,1},... | collective-permute-start | bytes 442376 | tf_op jit(solution)/shard_map/ppermute | solution.py:644
  44.1 33.7 %all-to-all-start = ((bf16[4,36,16,384]{3,2,1,0:T(8,128)(2,1)}), bf16[4,36,16,384]{3,2,1,0:T(8,128)(2,1)S(1)}, u32[]{:S(2)}, u32[]{:S(2)}) async-start(bf16[4,36,16,384]{3,2,1,0:T(8,128)(2,1)} %shard_map.328._), calls=%async_computation | async-start | bytes 3538944 | tf_op jit(solution)/shard_map/all_to_all | solution.py:1233
  60.0 15.9 %collective-permute-start.10 = (bf16[8,48,768]{2,1,0:T(8,128)(2,1)}, bf16[8,48,768]{2,1,0:T(8,128)(2,1)S(1)}, u32[]{:S(2)}, u32[]{:S(2)}) collective-permute-start(bf16[8,48,768]{2,1,0:T(8,128)(2,1)} %shard_map.333.refs_0_), channel_id=1, source_target_pairs={{0,4},{1,5},{2,6},{3,7},{4,0},{5,1},{6,2},{7,3},{8,12},{9,13},{10,... | collective-permute-start | bytes 1769480 | tf_op jit(solution)/shard_map/ppermute | solution.py:644
  76.7 2.2 %collective-permute-start.12 = (bf16[8,48,768]{2,1,0:T(8,128)(2,1)}, bf16[8,48,768]{2,1,0:T(8,128)(2,1)S(1)}, u32[]{:S(2)}, u32[]{:S(2)}) collective-permute-start(bf16[8,48,768]{2,1,0:T(8,128)(2,1)} %shard_map.336.refs_2_), channel_id=1, source_target_pairs={{0,1},{1,0},{2,3},{3,2},{4,5},{5,4},{6,7},{7,6},{8,9},{9,8},{10,11... | collective-permute-start | bytes 1769480 | tf_op jit(solution)/shard_map/ppermute | solution.py:644
  77.7 2.0 collective-permute-start.11
  122.1 3.1 %collective-permute-start.13 = (bf16[16,48,768]{2,1,0:T(8,128)(2,1)}, bf16[16,48,768]{2,1,0:T(8,128)(2,1)S(1)}, u32[]{:S(2)}, u32[]{:S(2)}) collective-permute-start(bf16[16,48,768]{2,1,0:T(8,128)(2,1)} %get-tuple-element.106), channel_id=1, source_target_pairs={{0,1},{1,0},{2,3},{3,2},{4,5},{5,4},{6,7},{7,6},{8,9},{9,8},{10,11... | collective-permute-start | bytes 3538952 | tf_op jit(solution)/shard_map/ppermute | solution.py:644
  122.3 25.6 %collective-permute-start.16 = (bf16[576,384]{1,0:T(8,128)(2,1)}, bf16[576,384]{1,0:T(8,128)(2,1)S(1)}, u32[]{:S(2)}, u32[]{:S(2)}) collective-permute-start(bf16[576,384]{1,0:T(8,128)(2,1)} %get-tuple-element.114), channel_id=1, source_target_pairs={{0,1},{1,0},{2,3},{3,2},{4,5},{5,4},{6,7},{7,6},{8,9},{9,8},{10,11... | collective-permute-start | bytes 1327112 | tf_op jit(solution)/shard_map/ppermute | solution.py:644
  122.7 25.2 %collective-permute-start.17 = (bf16[576,384]{1,0:T(8,128)(2,1)}, bf16[576,384]{1,0:T(8,128)(2,1)S(1)}, u32[]{:S(2)}, u32[]{:S(2)}) collective-permute-start(bf16[576,384]{1,0:T(8,128)(2,1)} %get-tuple-element.115), channel_id=1, source_target_pairs={{0,2},{1,3},{2,0},{3,1},{4,6},{5,7},{6,4},{7,5},{8,10},{9,11},{10,... | collective-permute-start | bytes 1327112 | tf_op jit(solution)/shard_map/ppermute | solution.py:644
  124.3 23.5 %collective-permute-start.18 = (bf16[576,384]{1,0:T(8,128)(2,1)}, bf16[576,384]{1,0:T(8,128)(2,1)S(1)}, u32[]{:S(2)}, u32[]{:S(2)}) collective-permute-start(bf16[576,384]{1,0:T(8,128)(2,1)} %get-tuple-element.116), channel_id=1, source_target_pairs={{0,3},{1,2},{2,1},{3,0},{4,7},{5,6},{6,5},{7,4},{8,11},{9,10},{10,... | collective-permute-start | bytes 1327112 | tf_op jit(solution)/shard_map/ppermute | solution.py:644
  125.2 3.2 %copy-start.9 = (bf16[16,48,768]{2,1,0:T(8,128)(2,1)}, bf16[16,48,768]{2,1,0:T(8,128)(2,1)S(1)}, u32[]{:S(2)}) copy-start(bf16[16,48,768]{2,1,0:T(8,128)(2,1)S(1)} %collective-permute-done.13) | copy-start | bytes 3538948
  126.8 18.0 %collective-permute-start.14 = (bf16[8,48,768]{2,1,0:T(8,128)(2,1)S(1)}, bf16[8,48,768]{2,1,0:T(8,128)(2,1)S(1)}, u32[]{:S(2)}, u32[]{:S(2)}) collective-permute-start(bf16[8,48,768]{2,1,0:T(8,128)(2,1)S(1)} %add_convert_fusion._), channel_id=1, source_target_pairs={{0,4},{1,5},{2,6},{3,7},{4,0},{5,1},{6,2},{7,3},{8,12},{9,13},{10,... | collective-permute-start | bytes 1769480 | tf_op jit(solution)/shard_map/ppermute | solution.py:644
  128.4 16.4 %copy-start.8 = (bf16[16,48,768]{2,1,0:T(8,128)(2,1)S(1)}, bf16[16,48,768]{2,1,0:T(8,128)(2,1)}, u32[]{:S(2)}) copy-start(bf16[16,48,768]{2,1,0:T(8,128)(2,1)} %get-tuple-element.105) | copy-start | bytes 3538948
  144.8 3.1 %copy-start.1 = (bf16[8,48,768]{2,1,0:T(8,128)(2,1)}, bf16[8,48,768]{2,1,0:T(8,128)(2,1)S(1)}, u32[]{:S(2)}) copy-start(bf16[8,48,768]{2,1,0:T(8,128)(2,1)S(1)} %collective-permute-done.14.refs_4_) | copy-start | bytes 1769476
  146.1 8.8 %collective-permute-start.15 = (bf16[4,48,768]{2,1,0:T(8,128)(2,1)S(1)}, bf16[4,48,768]{2,1,0:T(8,128)(2,1)S(1)}, u32[]{:S(2)}, u32[]{:S(2)}) collective-permute-start(bf16[4,48,768]{2,1,0:T(8,128)(2,1)S(1)} %add_convert_fusion.1), channel_id=1, source_target_pairs={{0,2},{1,3},{2,0},{3,1},{4,6},{5,7},{6,4},{7,5},{8,10},{9,11},{10,... | collective-permute-start | bytes 884744 | tf_op jit(solution)/shard_map/ppermute | solution.py:644
  149.0 7.1 %collective-permute-start.19 = (bf16[16,48,384]{2,1,0:T(8,128)(2,1)}, bf16[16,48,384]{2,1,0:T(8,128)(2,1)S(1)}, u32[]{:S(2)}, u32[]{:S(2)}) collective-permute-start(bf16[16,48,384]{2,1,0:T(8,128)(2,1)} %shard_map.339), channel_id=1, source_target_pairs={{0,1},{1,0},{2,3},{3,2},{4,5},{5,4},{6,7},{7,6},{8,9},{9,8},{10,11... | collective-permute-start | bytes 1769480 | tf_op jit(solution)/shard_map/ppermute | solution.py:644
  149.0 6.0 %copy-start.2 = (bf16[8,48,768]{2,1,0:T(8,128)(2,1)S(1)}, bf16[8,48,768]{2,1,0:T(8,128)(2,1)}, u32[]{:S(2)}) copy-start(bf16[8,48,768]{2,1,0:T(8,128)(2,1)} %copy-done.1) | copy-start | bytes 1769476
  153.0 3.1 %copy-start.12 = (bf16[16,48,384]{2,1,0:T(8,128)(2,1)S(1)}, bf16[16,48,384]{2,1,0:T(8,128)(2,1)}, u32[]{:S(2)}) copy-start(bf16[16,48,384]{2,1,0:T(8,128)(2,1)} %get-tuple-element.112) | copy-start | bytes 1769476
  156.3 3.6 %copy-start.16 = (bf16[4,48,384]{2,1,0:T(8,128)(2,1)}, bf16[4,48,384]{2,1,0:T(8,128)(2,1)S(1)}, u32[]{:S(2)}) copy-start(bf16[4,48,384]{2,1,0:T(8,128)(2,1)S(1)} %get-tuple-element.161.refs_1_) | copy-start | bytes 442372
  156.3 7.5 %collective-permute-start.22 = (bf16[4,48,384]{2,1,0:T(8,128)(2,1)S(1)}, bf16[4,48,384]{2,1,0:T(8,128)(2,1)S(1)}, u32[]{:S(2)}, u32[]{:S(2)}) collective-permute-start(bf16[4,48,384]{2,1,0:T(8,128)(2,1)S(1)} %get-tuple-element.162), channel_id=1, source_target_pairs={{0,6},{1,7},{2,4},{3,5},{4,2},{5,3},{6,0},{7,1},{8,14},{9,15},{10,... | collective-permute-start | bytes 442376 | tf_op jit(solution)/shard_map/ppermute | solution.py:644
  158.5 6.9 %collective-permute-start.21 = (bf16[4,48,384]{2,1,0:T(8,128)(2,1)S(1)}, bf16[4,48,384]{2,1,0:T(8,128)(2,1)S(1)}, u32[]{:S(2)}, u32[]{:S(2)}) collective-permute-start(bf16[4,48,384]{2,1,0:T(8,128)(2,1)S(1)} %get-tuple-element.163), channel_id=1, source_target_pairs={{0,4},{1,5},{2,6},{3,7},{4,0},{5,1},{6,2},{7,3},{8,12},{9,13},{10,... | collective-permute-start | bytes 442376 | tf_op jit(solution)/shard_map/ppermute | solution.py:644
  159.5 5.9 %collective-permute-start.20 = (bf16[4,48,384]{2,1,0:T(8,128)(2,1)S(1)}, bf16[4,48,384]{2,1,0:T(8,128)(2,1)S(1)}, u32[]{:S(2)}, u32[]{:S(2)}) collective-permute-start(bf16[4,48,384]{2,1,0:T(8,128)(2,1)S(1)} %get-tuple-element.161.refs_1_), channel_id=1, source_target_pairs={{0,2},{1,3},{2,0},{3,1},{4,6},{5,7},{6,4},{7,5},{8,10},{9,11},{10,... | collective-permute-start | bytes 442376 | tf_op jit(solution)/shard_map/ppermute | solution.py:644
  165.5 4.5 %copy-start.22 = (bf16[1,48,1152]{2,1,0:T(8,128)(2,1)}, bf16[1,48,1152]{2,1,0:T(8,128)(2,1)S(1)}, u32[]{:S(2)}) copy-start(bf16[1,48,1152]{2,1,0:T(8,128)(2,1)S(1)} %get-tuple-element.166._) | copy-start | bytes 331780
  165.5 15.3 %collective-permute-start.25 = (bf16[1,48,1152]{2,1,0:T(8,128)(2,1)S(1)}, bf16[1,48,1152]{2,1,0:T(8,128)(2,1)S(1)}, u32[]{:S(2)}, u32[]{:S(2)}) collective-permute-start(bf16[1,48,1152]{2,1,0:T(8,128)(2,1)S(1)} %get-tuple-element.164), channel_id=1, source_target_pairs={{0,24},{1,25},{2,26},{3,27},{4,28},{5,29},{6,30},{7,31},{8,16},{9,... | collective-permute-start | bytes 331784 | tf_op jit(solution)/shard_map/ppermute | solution.py:644
  168.1 12.7 %collective-permute-start.24 = (bf16[1,48,1152]{2,1,0:T(8,128)(2,1)S(1)}, bf16[1,48,1152]{2,1,0:T(8,128)(2,1)S(1)}, u32[]{:S(2)}, u32[]{:S(2)}) collective-permute-start(bf16[1,48,1152]{2,1,0:T(8,128)(2,1)S(1)} %get-tuple-element.165), channel_id=1, source_target_pairs={{0,16},{1,17},{2,18},{3,19},{4,20},{5,21},{6,22},{7,23},{8,24},{9,... | collective-permute-start | bytes 331784 | tf_op jit(solution)/shard_map/ppermute | solution.py:644
  168.1 12.8 %collective-permute-start.23 = (bf16[1,48,1152]{2,1,0:T(8,128)(2,1)S(1)}, bf16[1,48,1152]{2,1,0:T(8,128)(2,1)S(1)}, u32[]{:S(2)}, u32[]{:S(2)}) collective-permute-start(bf16[1,48,1152]{2,1,0:T(8,128)(2,1)S(1)} %get-tuple-element.166._), channel_id=1, source_target_pairs={{0,8},{1,9},{2,10},{3,11},{4,12},{5,13},{6,14},{7,15},{8,0},{9,1},... | collective-permute-start | bytes 331784 | tf_op jit(solution)/shard_map/ppermute | solution.py:644
  178.7 24.5 %collective-permute-start.27 = (bf16[576,384]{1,0:T(8,128)(2,1)}, bf16[576,384]{1,0:T(8,128)(2,1)S(1)}, u32[]{:S(2)}, u32[]{:S(2)}) collective-permute-start(bf16[576,384]{1,0:T(8,128)(2,1)} %get-tuple-element.132), channel_id=1, source_target_pairs={{0,2},{1,3},{2,0},{3,1},{4,6},{5,7},{6,4},{7,5},{8,10},{9,11},{10,... | collective-permute-start | bytes 1327112 | tf_op jit(solution)/shard_map/ppermute | solution.py:644
  180.8 22.7 %collective-permute-start.28 = (bf16[576,384]{1,0:T(8,128)(2,1)}, bf16[576,384]{1,0:T(8,128)(2,1)S(1)}, u32[]{:S(2)}, u32[]{:S(2)}) collective-permute-start(bf16[576,384]{1,0:T(8,128)(2,1)} %get-tuple-element.133), channel_id=1, source_target_pairs={{0,3},{1,2},{2,1},{3,0},{4,7},{5,6},{6,5},{7,4},{8,11},{9,10},{10,... | collective-permute-start | bytes 1327112 | tf_op jit(solution)/shard_map/ppermute | solution.py:644
  183.9 19.7 %collective-permute-start.26 = (bf16[576,384]{1,0:T(8,128)(2,1)}, bf16[576,384]{1,0:T(8,128)(2,1)S(1)}, u32[]{:S(2)}, u32[]{:S(2)}) collective-permute-start(bf16[576,384]{1,0:T(8,128)(2,1)} %shard_map.346), channel_id=1, source_target_pairs={{0,1},{1,0},{2,3},{3,2},{4,5},{5,4},{6,7},{7,6},{8,9},{9,8},{10,11... | collective-permute-start | bytes 1327112 | tf_op jit(solution)/shard_map/ppermute | solution.py:644
  184.6 5.1 %collective-permute-start.31 = (f32[24,384]{1,0:T(8,128)}, f32[24,384]{1,0:T(8,128)S(1)}, u32[]{:S(2)}, u32[]{:S(2)}) collective-permute-start(f32[24,384]{1,0:T(8,128)} %get-tuple-element.136), channel_id=1, source_target_pairs={{0,12},{1,13},{2,14},{3,15},{4,8},{5,9},{6,10},{7,11},{8,4},{9,5},... | collective-permute-start | bytes 110600 | tf_op jit(solution)/shard_map/ppermute | solution.py:644
  185.5 5.5 %collective-permute-start.30 = (f32[24,384]{1,0:T(8,128)}, f32[24,384]{1,0:T(8,128)S(1)}, u32[]{:S(2)}, u32[]{:S(2)}) collective-permute-start(f32[24,384]{1,0:T(8,128)} %get-tuple-element.136), channel_id=1, source_target_pairs={{0,8},{1,9},{2,10},{3,11},{4,12},{5,13},{6,14},{7,15},{8,0},{9,1},... | collective-permute-start | bytes 110600 | tf_op jit(solution)/shard_map/ppermute | solution.py:644
  189.7 4.2 %collective-permute-start.29 = (f32[24,384]{1,0:T(8,128)}, f32[24,384]{1,0:T(8,128)S(1)}, u32[]{:S(2)}, u32[]{:S(2)}) collective-permute-start(f32[24,384]{1,0:T(8,128)} %get-tuple-element.136), channel_id=1, source_target_pairs={{0,4},{1,5},{2,6},{3,7},{4,0},{5,1},{6,2},{7,3},{8,12},{9,13},{10,... | collective-permute-start | bytes 110600 | tf_op jit(solution)/shard_map/ppermute | solution.py:644
  194.6 4.9 %copy-start.17 = (f32[24,384]{1,0:T(8,128)}, f32[24,384]{1,0:T(8,128)S(1)}, u32[]{:S(2)}) copy-start(f32[24,384]{1,0:T(8,128)S(1)} %add_add_fusion.refs_0_) | copy-start | bytes 110596
  194.6 4.9 %collective-permute-start.32 = (f32[24,384]{1,0:T(8,128)S(1)}, f32[24,384]{1,0:T(8,128)S(1)}, u32[]{:S(2)}, u32[]{:S(2)}) collective-permute-start(f32[24,384]{1,0:T(8,128)S(1)} %add_add_fusion.refs_0_), channel_id=1, source_target_pairs={{0,16},{1,17},{2,18},{3,19},{4,20},{5,21},{6,22},{7,23},{8,24},{9,... | collective-permute-start | bytes 110600 | tf_op jit(solution)/shard_map/ppermute | solution.py:644
  201.7 5.6 %collective-permute-start.35 = (f32[64,128]{1,0:T(8,128)}, f32[64,128]{1,0:T(8,128)S(1)}, u32[]{:S(2)}, u32[]{:S(2)}) collective-permute-start(f32[64,128]{1,0:T(8,128)} %get-tuple-element.138.refs_0_), channel_id=1, source_target_pairs={{0,3},{1,2},{2,1},{3,0},{4,7},{5,6},{6,5},{7,4},{8,11},{9,10},{10,... | collective-permute-start | bytes 98312 | tf_op jit(solution)/shard_map/ppermute | solution.py:644
  201.7 5.6 %collective-permute-start.34 = (f32[64,128]{1,0:T(8,128)}, f32[64,128]{1,0:T(8,128)S(1)}, u32[]{:S(2)}, u32[]{:S(2)}) collective-permute-start(f32[64,128]{1,0:T(8,128)} %get-tuple-element.138.refs_0_), channel_id=1, source_target_pairs={{0,2},{1,3},{2,0},{3,1},{4,6},{5,7},{6,4},{7,5},{8,10},{9,11},{10,... | collective-permute-start | bytes 98312 | tf_op jit(solution)/shard_map/ppermute | solution.py:644
  203.2 4.1 %collective-permute-start.33 = (f32[64,128]{1,0:T(8,128)}, f32[64,128]{1,0:T(8,128)S(1)}, u32[]{:S(2)}, u32[]{:S(2)}) collective-permute-start(f32[64,128]{1,0:T(8,128)} %get-tuple-element.138.refs_0_), channel_id=1, source_target_pairs={{0,1},{1,0},{2,3},{3,2},{4,5},{5,4},{6,7},{7,6},{8,9},{9,8},{10,11... | collective-permute-start | bytes 98312 | tf_op jit(solution)/shard_map/ppermute | solution.py:644
  (23 other events, 20.1 us)

commit v4 on v3

--- a/solution.py
+++ b/solution.py
@@ -100,6 +100,7 @@
 SLICE = 48
 FF_CHUNK = 256
 vmem_bytes = 60 * 1024 * 1024
+all_vmem_bytes = 64 * 1024 * 1024
 
 
 def dot(left, right, left_axis=1, right_axis=0):
@@ -1257,7 +1258,10 @@
     across_y, across_x = near_bits
     pack_arrived = permute(pack_own, across_y)
     cotangent_cut = small(cut, out_shape=parted)(cotangent.transpose(1, 0, 2))
-    token_cut, first_pair, second_pair = small(
+    roomy = functools.partial(
+        pl.pallas_call, compiler_params=pltpu.CompilerParams(vmem_limit_bytes=all_vmem_bytes)
+    )
+    token_cut, first_pair, second_pair = roomy(
         token_kernel,
         in_specs=[in_vmem] * 3 + [anywhere],
         out_shape=[
@@ -1273,7 +1277,7 @@
 
     def join(parts, awaited=()):
         count = len(parts) * parts[0].shape[0]
-        return small(
+        return roomy(
             functools.partial(join_kernel, len(parts)),
             in_specs=[in_vmem] * len(parts) + [anywhere] * len(awaited),
             out_shape=jax.ShapeDtypeStruct((count, *parts[0].shape[1:]), low),

time: 211 us -> 211 us (level)
    unnamed x66 -> x62, local copies, waits for them, and re-layouts: 9.79 us -> 8.06 us
where the time goes in v4:
time: 211 us; the launch traced here: 210 us
  Pallas kernels  120 us (57%)
  starting transfers between devices  45.9 us (22%)
  waiting for transfers between devices  29 us (14%)
  local copies, waits for them, and re-layouts  8.13 us (4%)
  other arithmetic  5.81 us (3%)
    pallas_call x7, Pallas kernels, call_kernel(): pl.pallas_call(functools.partial(kernel, *statics), grid=(steps,), in_spe...  97 us
    ppermute x36, starting transfers between devices, permute(): lax.ppermute(array, ('dp', 'group'), [(rank, rank ^ mask) for rank in ran...  37 us
    ppermute x36, waiting for transfers between devices, permute(): lax.ppermute(array, ('dp', 'group'), [(rank, rank ^ mask) for rank in ran...  29 us
    all_to_all x2, starting transfers between devices, to_group(): lax.all_to_all(parts, 'group', split_axis=0, concat_axis=0, tiled=True)  8.89 us
    unnamed x62, local copies, waits for them, and re-layouts  8.06 us
    pallas_call x2, Pallas kernels, settle(): small(functools.partial(settle_kernel, spread), in_specs=[in_smem] + [in_...  5.55 us
  transfers between devices with their start and end apart: 38, of which 13 were waited for; matrix products, arithmetic and copies ran while one was open for 3% of the time, Pallas kernels for 34%

profile of v4, /device:TPU:0, one launch (start us, length us, event | category | flops | bytes accessed | tf_op | source)
XLA Modules:
  0.0 210.0 jit_solution(2062187445766969398)
XLA Ops:
  0.7 1.7 shard_map.329.own_ref
  2.4 3.0 %collective-permute-start = (bf16[48,1152]{1,0:T(8,128)(2,1)}, bf16[48,1152]{1,0:T(8,128)(2,1)}, u32[]{:S(2)}, u32[]{:S(2)}) collective-permute-start(bf16[48,1152]{1,0:T(8,128)(2,1)} %shard_map.329.own_ref), channel_id=1, source_target_pairs={{0,2},{1,3},{2,0},{3,1},{4,6},{5,7},{6,4},{7,5},{8,10},{9,11},{10,... | collective-permute-start | bytes 331784 | tf_op jit(solution)/shard_map/ppermute | solution.py:645
  5.3 2.8 %shard_map.328._ = bf16[4,36,16,384]{3,2,1,0:T(8,128)(2,1)} custom-call(bf16[36,64,384]{2,1,0:T(8,128)(2,1)} %bitcast.16), custom_call_target="tpu_custom_call" | custom-call | tf_op jit(solution)/shard_map/pallas_call | solution.py:1260
  8.7 2.9 %shard_map.330 = (bf16[4,36,16,384]{3,2,1,0:T(8,128)(2,1)}, bf16[2,48,384]{2,1,0:T(8,128)(2,1)}, bf16[2,48,768]{2,1,0:T(8,128)(2,1)}) custom-call(bf16[36,64,384]{2,1,0:T(8,128)(2,1)} %bitcast.15, bf16[48,1152]{1,0:T(8,128)(2,1)} %shard_map.329.own_ref, bf16[48,1152]{1,0:T(8,128)(2,1)} %collective-permute-done.arrived_ref, bf16[4,36,16,384]{3,2,1,0:T(8,128)(2,1)} %shard_map.328._), custom_call_target="tpu_custom_call" | custom-call | tf_op jit(solution)/shard_map/pallas_call | solution.py:1264
  11.6 4.5 %all-to-all-start.1 = ((bf16[4,36,16,384]{3,2,1,0:T(8,128)(2,1)}), bf16[4,36,16,384]{3,2,1,0:T(8,128)(2,1)}, u32[]{:S(2)}, u32[]{:S(2)}) async-start(bf16[4,36,16,384]{3,2,1,0:T(8,128)(2,1)} %get-tuple-element.91), calls=%async_computation.1 | async-start | bytes 3538944 | tf_op jit(solution)/shard_map/all_to_all | solution.py:1234
  16.2 3.9 %collective-permute-start.6 = (bf16[2,48,384]{2,1,0:T(8,128)(2,1)S(1)}, bf16[2,48,384]{2,1,0:T(8,128)(2,1)S(1)}, u32[]{:S(2)}, u32[]{:S(2)}) collective-permute-start(bf16[2,48,384]{2,1,0:T(8,128)(2,1)S(1)} %copy-done.19), channel_id=1, source_target_pairs={{0,24},{1,25},{2,26},{3,27},{4,28},{5,29},{6,30},{7,31},{8,16},{9,... | collective-permute-start | bytes 221192 | tf_op jit(solution)/shard_map/ppermute | solution.py:645
  20.7 2.6 %collective-permute-done.6.refs_3_ = bf16[2,48,384]{2,1,0:T(8,128)(2,1)S(1)} collective-permute-done((bf16[2,48,384]{2,1,0:T(8,128)(2,1)S(1)}, bf16[2,48,384]{2,1,0:T(8,128)(2,1)S(1)}, u32[]{:S(2)}, u32[]{:S(2)}) %collective-permute-start.6) | collective-permute-done | bytes 73760 | tf_op jit(solution)/shard_map/ppermute | solution.py:645
  23.3 3.5 %collective-permute-done.5.refs_2_ = bf16[2,48,384]{2,1,0:T(8,128)(2,1)S(1)} collective-permute-done((bf16[2,48,384]{2,1,0:T(8,128)(2,1)S(1)}, bf16[2,48,384]{2,1,0:T(8,128)(2,1)S(1)}, u32[]{:S(2)}, u32[]{:S(2)}) %collective-permute-start.5) | collective-permute-done | bytes 73760 | tf_op jit(solution)/shard_map/ppermute | solution.py:645
  27.4 1.7 shard_map.331.refs_0_
  29.1 1.5 collective-permute-start.7
  30.6 7.2 %collective-permute-done.7.refs_1_ = bf16[8,48,384]{2,1,0:T(8,128)(2,1)S(1)} collective-permute-done((bf16[8,48,384]{2,1,0:T(8,128)(2,1)}, bf16[8,48,384]{2,1,0:T(8,128)(2,1)S(1)}, u32[]{:S(2)}, u32[]{:S(2)}) %collective-permute-start.7) | collective-permute-done | bytes 294944 | tf_op jit(solution)/shard_map/ppermute | solution.py:645
  37.8 2.5 %collective-permute-start.3 = (bf16[2,48,768]{2,1,0:T(8,128)(2,1)}, bf16[2,48,768]{2,1,0:T(8,128)(2,1)}, u32[]{:S(2)}, u32[]{:S(2)}) collective-permute-start(bf16[2,48,768]{2,1,0:T(8,128)(2,1)} %get-tuple-element.90.refs_0_), channel_id=1, source_target_pairs={{0,24},{1,25},{2,26},{3,27},{4,28},{5,29},{6,30},{7,31},{8,16},{9,... | collective-permute-start | bytes 442376 | tf_op jit(solution)/shard_map/ppermute | solution.py:645
  40.3 1.9 collective-permute-start.1
  42.2 4.4 %all-to-all-start = ((bf16[4,36,16,384]{3,2,1,0:T(8,128)(2,1)}), bf16[4,36,16,384]{3,2,1,0:T(8,128)(2,1)}, u32[]{:S(2)}, u32[]{:S(2)}) async-start(bf16[4,36,16,384]{3,2,1,0:T(8,128)(2,1)} %shard_map.328._), calls=%async_computation | async-start | bytes 3538944 | tf_op jit(solution)/shard_map/all_to_all | solution.py:1234
  47.4 10.2 %shard_map.332 = (bf16[2304,1152]{1,0:T(8,128)(2,1)}, bf16[16,3,144,288]{3,2,1,0:T(8,128)(2,1)}, bf16[2304,384]{1,0:T(8,128)(2,1)}, f32[2304,384]{1,0:T(8,128)},...) custom-call(s32[1]{0:T(128)} %bitcast.place_ref, ...), custom_call_target="tpu_custom_call" | custom-call | flops 7474249728 | bytes 23473156 | tf_op jit(solution)/shard_map/pallas_call | solution.py:537
  57.6 2.0 shard_map.333.refs_0_
  59.6 1.5 collective-permute-start.10
  61.1 12.4 %shard_map.334 = (bf16[2304,1152]{1,0:T(8,128)(2,1)}, bf16[16,3,144,288]{3,2,1,0:T(8,128)(2,1)}, bf16[2304,384]{1,0:T(8,128)(2,1)}, f32[2304,384]{1,0:T(8,128)}, bf16[2304,384]{1,0:T(8,128)(2,1)}) custom-call(bf16[2304,384]{1,0:T(8,128)(2,1)} %get-tuple-element.94.x_ref, ...), custom_call_target="tpu_custom_call", output_to_operand_aliasing={{0}: (5, {}), {1}: (6, {}), {2}: (7, {}), {3}: (8, {}), {4}... | custom-call | flops 22422749184 | bytes 35712000 | tf_op jit(solution)/shard_map/pallas_call | solution.py:537
  73.6 2.0 collective-permute-done.10.refs_0_
  77.4 1.1 collective-permute-done.12.refs_4_
  80.3 41.5 %shard_map.337 = (bf16[576,384]{1,0:T(8,128)(2,1)}, bf16[576,384]{1,0:T(8,128)(2,1)}, bf16[576,384]{1,0:T(8,128)(2,1)}, bf16[576,384]{1,0:T(8,128)(2,1)}, f32[23...) custom-call(s32[1]{0:T(128)} %bitcast.place_ref, ...), custom_call_target="tpu_custom_call" | custom-call | flops 141331267584 | bytes 19795972 | tf_op jit(solution)/shard_map/pallas_call | solution.py:537
  122.3 1.7 collective-permute-start.17
  124.9 1.6 add_convert_fusion._
  126.5 1.6 collective-permute-start.14
  128.1 16.3 %shard_map.338 = (bf16[2304,1152]{1,0:T(8,128)(2,1)}, bf16[16,48,384]{2,1,0:T(8,128)(2,1)}, bf16[16,48,384]{2,1,0:T(8,128)(2,1)}, f32[8,384]{1,0:T(8,128)}) custom-call(s32[1]{0:T(128)} %bitcast.place_ref, bf16[2304,384]{1,0:T(8,128)(2,1)} %get-tuple-element.107.normed_ref, bf16[2304,1152]{1,0:T(8,128)(2,1)} %get-tuple-element.108.qkv_ref, ...), custom_call_target="tpu_custom_call" | custom-call | flops 32614907904 | bytes 20527108 | tf_op jit(solution)/shard_map/pallas_call | solution.py:537
  144.4 1.3 add_convert_fusion.1
  145.7 1.7 collective-permute-start.15
  148.6 4.0 %shard_map.340 = (bf16[2304,384]{1,0:T(8,128)(2,1)}, f32[8,384]{1,0:T(8,128)}) custom-call(bf16[2304,384]{1,0:T(8,128)(2,1)} %get-tuple-element.94.x_ref, bf16[2304,1152]{1,0:T(8,128)(2,1)} %get-tuple-element.117.d_projected_ref, f32[2304,384]{1,0:T(8,128)} %get-tuple-element.118.d_middle_ref, bf16[1152,384]{1,0:T(8,128)(2,1)} %get-tuple-element.119.qkv_t_ref, ...), custom_call_target="tpu_custom_call" | custom-call | flops 4076863488 | bytes 13314048 | tf_op jit(solution)/shard_map/pallas_call | solution.py:537
  152.6 2.0 collective-permute-done.15
  154.6 1.2 convert_add_fusion.1
  156.0 1.9 collective-permute-start.22
  157.9 1.2 collective-permute-start.21
  159.5 3.9 %shard_map.341 = (bf16[2304,384]{1,0:T(8,128)(2,1)}, f32[8,384]{1,0:T(8,128)}) custom-call(bf16[2304,384]{1,0:T(8,128)(2,1)} %get-tuple-element.94.x_ref, bf16[2304,1152]{1,0:T(8,128)(2,1)} %get-tuple-element.117.d_projected_ref, f32[2304,384]{1,0:T(8,128)} %get-tuple-element.118.d_middle_ref, ...), custom_call_target="tpu_custom_call", output_to_operand_aliasing={{0}: (6, {})} | custom-call | flops 4076863488 | bytes 15230976 | tf_op jit(solution)/shard_map/pallas_call | solution.py:537
  163.5 1.6 collective-permute-done.21
  165.2 2.5 %collective-permute-start.25 = (bf16[1,48,1152]{2,1,0:T(8,128)(2,1)S(1)}, bf16[1,48,1152]{2,1,0:T(8,128)(2,1)S(1)}, u32[]{:S(2)}, u32[]{:S(2)}) collective-permute-start(bf16[1,48,1152]{2,1,0:T(8,128)(2,1)S(1)} %get-tuple-element.164), channel_id=1, source_target_pairs={{0,24},{1,25},{2,26},{3,27},{4,28},{5,29},{6,30},{7,31},{8,16},{9,... | collective-permute-start | bytes 331784 | tf_op jit(solution)/shard_map/ppermute | solution.py:645
  167.8 1.9 collective-permute-start.23
  169.7 8.6 %shard_map.342 = (bf16[576,384]{1,0:T(8,128)(2,1)}, bf16[576,384]{1,0:T(8,128)(2,1)}, bf16[576,384]{1,0:T(8,128)(2,1)}, bf16[576,384]{1,0:T(8,128)(2,1)}, f32[8,384]{1,0:T(8,128)}) custom-call(s32[1]{0:T(128)} %bitcast.place_ref, bf16[2304,384]{1,0:T(8,128)(2,1)} %get-tuple-element.94.x_ref, bf16[2304,1152]{1,0:T(8,128)(2,1)} %get-tuple-element.117.d_projected_ref, ...), custom_call_target="tpu_custom_call" | custom-call | flops 8153726976 | bytes 15194116 | tf_op jit(solution)/shard_map/pallas_call | solution.py:537
  178.3 1.5 collective-permute-start.27
  181.2 2.3 %shard_map.343 = (f32[48,288]{1,0:T(8,128)}, f32[48,96]{1,0:T(8,128)}, f32[48,384]{1,0:T(8,128)}, f32[192,96]{1,0:T(8,128)}, f32[8,48]{1,0:T(8,128)}, /*index=5*/f32[24,384]{1,0:T(8,128)}) custom-call(f32[1,48,1152]{2,1,0:T(8,128)} %fusion.3.refs_0_, bf16[1,48,1152]{2,1,0:T(8,128)(2,1)} %copy-done.17, bf16[1,48,1152]{2,1,0:T(8,128)(2,1)} %copy-done.16, ...), custom_call_target="tpu_custom_call" | custom-call | tf_op jit(solution)/shard_map/pallas_call | solution.py:1446
  184.8 1.9 collective-permute-start.30
  186.7 2.6 %collective-permute-done.31 = f32[24,384]{1,0:T(8,128)S(1)} collective-permute-done((f32[24,384]{1,0:T(8,128)}, f32[24,384]{1,0:T(8,128)S(1)}, u32[]{:S(2)}, u32[]{:S(2)}) %collective-permute-start.31) | collective-permute-done | bytes 36896 | tf_op jit(solution)/shard_map/ppermute | solution.py:645
  190.3 3.1 %collective-permute-done.29 = f32[24,384]{1,0:T(8,128)S(1)} collective-permute-done((f32[24,384]{1,0:T(8,128)}, f32[24,384]{1,0:T(8,128)S(1)}, u32[]{:S(2)}, u32[]{:S(2)}) %collective-permute-start.29) | collective-permute-done | bytes 36896 | tf_op jit(solution)/shard_map/ppermute | solution.py:645
  194.3 1.1 collective-permute-start.32
  195.4 2.8 %shard_map.345 = (bf16[36,64,384]{2,1,0:T(8,128)(2,1)}, f32[8,128]{1,0:T(8,128)}) custom-call(s32[1]{0:T(128)} %bitcast.place_ref, bf16[36,16,384]{2,1,0:T(8,128)(2,1)} %bitcast.17, bf16[36,16,384]{2,1,0:T(8,128)(2,1)} %bitcast.18, bf16[36,16,384]{2,1,0:T(8,128)(2,1)} %bitcast.19, bf16[36,16,384]{2,1,0:T(8,128)(2,1)} %bitcast.20), custom_call_target="tpu_custom_call" | custom-call | tf_op jit(solution)/shard_map/pallas_call | solution.py:1244
  199.8 1.5 shard_map.348
  201.3 1.5 collective-permute-start.34
  204.1 2.8 %shard_map.347 = (bf16[36,64,384]{2,1,0:T(8,128)(2,1)}, f32[8,128]{1,0:T(8,128)}) custom-call(s32[1]{0:T(128)} %bitcast.place_ref, bf16[36,16,384]{2,1,0:T(8,128)(2,1)} %bitcast.21, bf16[36,16,384]{2,1,0:T(8,128)(2,1)} %bitcast.24, bf16[36,16,384]{2,1,0:T(8,128)(2,1)} %bitcast.22, bf16[36,16,384]{2,1,0:T(8,128)(2,1)} %bitcast.23), custom_call_target="tpu_custom_call" | custom-call | tf_op jit(solution)/shard_map/pallas_call | solution.py:1244
  207.5 2.3 %shard_map.349 = (f32[48,288]{1,0:T(8,128)}, f32[48,96]{1,0:T(8,128)}, f32[48,384]{1,0:T(8,128)}, f32[192,96]{1,0:T(8,128)}, f32[288]{0:T(512)}, /*index=5*/f32[...) custom-call(f32[64,128]{1,0:T(8,128)} %get-tuple-element.138.refs_0_, ...), custom_call_target="tpu_custom_call" | custom-call | tf_op jit(solution)/shard_map/pallas_call | solution.py:1468
  (122 shorter events, 17.5 us)
Async XLA Ops:
  2.4 6.3 %collective-permute-start = (bf16[48,1152]{1,0:T(8,128)(2,1)}, bf16[48,1152]{1,0:T(8,128)(2,1)}, u32[]{:S(2)}, u32[]{:S(2)}) collective-permute-start(bf16[48,1152]{1,0:T(8,128)(2,1)} %shard_map.329.own_ref), channel_id=1, source_target_pairs={{0,2},{1,3},{2,0},{3,1},{4,6},{5,7},{6,4},{7,5},{8,10},{9,11},{10,... | collective-permute-start | bytes 331784 | tf_op jit(solution)/shard_map/ppermute | solution.py:645
  11.6 4.5 %copy-start.19 = (bf16[2,48,384]{2,1,0:T(8,128)(2,1)S(1)}, bf16[2,48,384]{2,1,0:T(8,128)(2,1)}, u32[]{:S(2)}) copy-start(bf16[2,48,384]{2,1,0:T(8,128)(2,1)} %get-tuple-element.92.refs_0_) | copy-start | bytes 221188
  11.6 30.6 %all-to-all-start.1 = ((bf16[4,36,16,384]{3,2,1,0:T(8,128)(2,1)}), bf16[4,36,16,384]{3,2,1,0:T(8,128)(2,1)}, u32[]{:S(2)}, u32[]{:S(2)}) async-start(bf16[4,36,16,384]{3,2,1,0:T(8,128)(2,1)} %get-tuple-element.91), calls=%async_computation.1 | async-start | bytes 3538944 | tf_op jit(solution)/shard_map/all_to_all | solution.py:1234
  16.2 7.1 %collective-permute-start.6 = (bf16[2,48,384]{2,1,0:T(8,128)(2,1)S(1)}, bf16[2,48,384]{2,1,0:T(8,128)(2,1)S(1)}, u32[]{:S(2)}, u32[]{:S(2)}) collective-permute-start(bf16[2,48,384]{2,1,0:T(8,128)(2,1)S(1)} %copy-done.19), channel_id=1, source_target_pairs={{0,24},{1,25},{2,26},{3,27},{4,28},{5,29},{6,30},{7,31},{8,16},{9,... | collective-permute-start | bytes 221192 | tf_op jit(solution)/shard_map/ppermute | solution.py:645
  20.1 6.7 %collective-permute-start.5 = (bf16[2,48,384]{2,1,0:T(8,128)(2,1)S(1)}, bf16[2,48,384]{2,1,0:T(8,128)(2,1)S(1)}, u32[]{:S(2)}, u32[]{:S(2)}) collective-permute-start(bf16[2,48,384]{2,1,0:T(8,128)(2,1)S(1)} %copy-done.19), channel_id=1, source_target_pairs={{0,16},{1,17},{2,18},{3,19},{4,20},{5,21},{6,22},{7,23},{8,24},{9,... | collective-permute-start | bytes 221192 | tf_op jit(solution)/shard_map/ppermute | solution.py:645
  20.1 7.3 %collective-permute-start.4 = (bf16[2,48,384]{2,1,0:T(8,128)(2,1)S(1)}, bf16[2,48,384]{2,1,0:T(8,128)(2,1)}, u32[]{:S(2)}, u32[]{:S(2)}) collective-permute-start(bf16[2,48,384]{2,1,0:T(8,128)(2,1)S(1)} %copy-done.19), channel_id=1, source_target_pairs={{0,8},{1,9},{2,10},{3,11},{4,12},{5,13},{6,14},{7,15},{8,0},{9,1},... | collective-permute-start | bytes 221192 | tf_op jit(solution)/shard_map/ppermute | solution.py:645
  23.3 3.5 %copy-start.20 = (bf16[2,48,384]{2,1,0:T(8,128)(2,1)}, bf16[2,48,384]{2,1,0:T(8,128)(2,1)S(1)}, u32[]{:S(2)}) copy-start(bf16[2,48,384]{2,1,0:T(8,128)(2,1)S(1)} %collective-permute-done.6.refs_3_) | copy-start | bytes 221188
  29.1 8.7 %collective-permute-start.7 = (bf16[8,48,384]{2,1,0:T(8,128)(2,1)}, bf16[8,48,384]{2,1,0:T(8,128)(2,1)S(1)}, u32[]{:S(2)}, u32[]{:S(2)}) collective-permute-start(bf16[8,48,384]{2,1,0:T(8,128)(2,1)} %shard_map.331.refs_0_), channel_id=1, source_target_pairs={{0,4},{1,5},{2,6},{3,7},{4,0},{5,1},{6,2},{7,3},{8,12},{9,13},{10,... | collective-permute-start | bytes 884744 | tf_op jit(solution)/shard_map/ppermute | solution.py:645
  30.6 16.0 %collective-permute-start.8 = (bf16[8,48,384]{2,1,0:T(8,128)(2,1)}, bf16[8,48,384]{2,1,0:T(8,128)(2,1)S(1)}, u32[]{:S(2)}, u32[]{:S(2)}) collective-permute-start(bf16[8,48,384]{2,1,0:T(8,128)(2,1)} %shard_map.331.refs_0_), channel_id=1, source_target_pairs={{0,1},{1,0},{2,3},{3,2},{4,5},{5,4},{6,7},{7,6},{8,9},{9,8},{10,11... | collective-permute-start | bytes 884744 | tf_op jit(solution)/shard_map/ppermute | solution.py:645
  37.8 4.4 %copy-start.28 = (bf16[8,48,384]{2,1,0:T(8,128)(2,1)}, bf16[8,48,384]{2,1,0:T(8,128)(2,1)S(1)}, u32[]{:S(2)}) copy-start(bf16[8,48,384]{2,1,0:T(8,128)(2,1)S(1)} %collective-permute-done.7.refs_1_) | copy-start | bytes 884740
  37.8 8.8 %collective-permute-start.9 = (bf16[8,48,384]{2,1,0:T(8,128)(2,1)S(1)}, bf16[8,48,384]{2,1,0:T(8,128)(2,1)S(1)}, u32[]{:S(2)}, u32[]{:S(2)}) collective-permute-start(bf16[8,48,384]{2,1,0:T(8,128)(2,1)S(1)} %collective-permute-done.7.refs_1_), channel_id=1, source_target_pairs={{0,1},{1,0},{2,3},{3,2},{4,5},{5,4},{6,7},{7,6},{8,9},{9,8},{10,11... | collective-permute-start | bytes 884744 | tf_op jit(solution)/shard_map/ppermute | solution.py:645
  37.8 19.8 %collective-permute-start.3 = (bf16[2,48,768]{2,1,0:T(8,128)(2,1)}, bf16[2,48,768]{2,1,0:T(8,128)(2,1)}, u32[]{:S(2)}, u32[]{:S(2)}) collective-permute-start(bf16[2,48,768]{2,1,0:T(8,128)(2,1)} %get-tuple-element.90.refs_0_), channel_id=1, source_target_pairs={{0,24},{1,25},{2,26},{3,27},{4,28},{5,29},{6,30},{7,31},{8,16},{9,... | collective-permute-start | bytes 442376 | tf_op jit(solution)/shard_map/ppermute | solution.py:645
  40.3 17.3 %collective-permute-start.2 = (bf16[2,48,768]{2,1,0:T(8,128)(2,1)}, bf16[2,48,768]{2,1,0:T(8,128)(2,1)}, u32[]{:S(2)}, u32[]{:S(2)}) collective-permute-start(bf16[2,48,768]{2,1,0:T(8,128)(2,1)} %get-tuple-element.90.refs_0_), channel_id=1, source_target_pairs={{0,16},{1,17},{2,18},{3,19},{4,20},{5,21},{6,22},{7,23},{8,24},{9,... | collective-permute-start | bytes 442376 | tf_op jit(solution)/shard_map/ppermute | solution.py:645
  40.3 17.3 %collective-permute-start.1 = (bf16[2,48,768]{2,1,0:T(8,128)(2,1)}, bf16[2,48,768]{2,1,0:T(8,128)(2,1)}, u32[]{:S(2)}, u32[]{:S(2)}) collective-permute-start(bf16[2,48,768]{2,1,0:T(8,128)(2,1)} %get-tuple-element.90.refs_0_), channel_id=1, source_target_pairs={{0,8},{1,9},{2,10},{3,11},{4,12},{5,13},{6,14},{7,15},{8,0},{9,1},... | collective-permute-start | bytes 442376 | tf_op jit(solution)/shard_map/ppermute | solution.py:645
  42.2 35.2 %all-to-all-start = ((bf16[4,36,16,384]{3,2,1,0:T(8,128)(2,1)}), bf16[4,36,16,384]{3,2,1,0:T(8,128)(2,1)}, u32[]{:S(2)}, u32[]{:S(2)}) async-start(bf16[4,36,16,384]{3,2,1,0:T(8,128)(2,1)} %shard_map.328._), calls=%async_computation | async-start | bytes 3538944 | tf_op jit(solution)/shard_map/all_to_all | solution.py:1234
  59.6 15.9 %collective-permute-start.10 = (bf16[8,48,768]{2,1,0:T(8,128)(2,1)}, bf16[8,48,768]{2,1,0:T(8,128)(2,1)S(1)}, u32[]{:S(2)}, u32[]{:S(2)}) collective-permute-start(bf16[8,48,768]{2,1,0:T(8,128)(2,1)} %shard_map.333.refs_0_), channel_id=1, source_target_pairs={{0,4},{1,5},{2,6},{3,7},{4,0},{5,1},{6,2},{7,3},{8,12},{9,13},{10,... | collective-permute-start | bytes 1769480 | tf_op jit(solution)/shard_map/ppermute | solution.py:645
  76.4 2.2 %collective-permute-start.12 = (bf16[8,48,768]{2,1,0:T(8,128)(2,1)}, bf16[8,48,768]{2,1,0:T(8,128)(2,1)S(1)}, u32[]{:S(2)}, u32[]{:S(2)}) collective-permute-start(bf16[8,48,768]{2,1,0:T(8,128)(2,1)} %shard_map.336.refs_2_), channel_id=1, source_target_pairs={{0,1},{1,0},{2,3},{3,2},{4,5},{5,4},{6,7},{7,6},{8,9},{9,8},{10,11... | collective-permute-start | bytes 1769480 | tf_op jit(solution)/shard_map/ppermute | solution.py:645
  77.4 2.0 collective-permute-start.11
  121.8 3.1 %collective-permute-start.13 = (bf16[16,48,768]{2,1,0:T(8,128)(2,1)}, bf16[16,48,768]{2,1,0:T(8,128)(2,1)S(1)}, u32[]{:S(2)}, u32[]{:S(2)}) collective-permute-start(bf16[16,48,768]{2,1,0:T(8,128)(2,1)} %get-tuple-element.106), channel_id=1, source_target_pairs={{0,1},{1,0},{2,3},{3,2},{4,5},{5,4},{6,7},{7,6},{8,9},{9,8},{10,11... | collective-permute-start | bytes 3538952 | tf_op jit(solution)/shard_map/ppermute | solution.py:645
  122.0 25.5 %collective-permute-start.16 = (bf16[576,384]{1,0:T(8,128)(2,1)}, bf16[576,384]{1,0:T(8,128)(2,1)S(1)}, u32[]{:S(2)}, u32[]{:S(2)}) collective-permute-start(bf16[576,384]{1,0:T(8,128)(2,1)} %get-tuple-element.114), channel_id=1, source_target_pairs={{0,1},{1,0},{2,3},{3,2},{4,5},{5,4},{6,7},{7,6},{8,9},{9,8},{10,11... | collective-permute-start | bytes 1327112 | tf_op jit(solution)/shard_map/ppermute | solution.py:645
  122.3 25.1 %collective-permute-start.17 = (bf16[576,384]{1,0:T(8,128)(2,1)}, bf16[576,384]{1,0:T(8,128)(2,1)S(1)}, u32[]{:S(2)}, u32[]{:S(2)}) collective-permute-start(bf16[576,384]{1,0:T(8,128)(2,1)} %get-tuple-element.115), channel_id=1, source_target_pairs={{0,2},{1,3},{2,0},{3,1},{4,6},{5,7},{6,4},{7,5},{8,10},{9,11},{10,... | collective-permute-start | bytes 1327112 | tf_op jit(solution)/shard_map/ppermute | solution.py:645
  124.0 23.5 %collective-permute-start.18 = (bf16[576,384]{1,0:T(8,128)(2,1)}, bf16[576,384]{1,0:T(8,128)(2,1)S(1)}, u32[]{:S(2)}, u32[]{:S(2)}) collective-permute-start(bf16[576,384]{1,0:T(8,128)(2,1)} %get-tuple-element.116), channel_id=1, source_target_pairs={{0,3},{1,2},{2,1},{3,0},{4,7},{5,6},{6,5},{7,4},{8,11},{9,10},{10,... | collective-permute-start | bytes 1327112 | tf_op jit(solution)/shard_map/ppermute | solution.py:645
  124.9 19.5 %copy-start.6 = (bf16[16,48,768]{2,1,0:T(8,128)(2,1)}, bf16[16,48,768]{2,1,0:T(8,128)(2,1)S(1)}, u32[]{:S(2)}) copy-start(bf16[16,48,768]{2,1,0:T(8,128)(2,1)S(1)} %collective-permute-done.13) | copy-start | bytes 3538948
  126.5 17.9 %collective-permute-start.14 = (bf16[8,48,768]{2,1,0:T(8,128)(2,1)S(1)}, bf16[8,48,768]{2,1,0:T(8,128)(2,1)S(1)}, u32[]{:S(2)}, u32[]{:S(2)}) collective-permute-start(bf16[8,48,768]{2,1,0:T(8,128)(2,1)S(1)} %add_convert_fusion._), channel_id=1, source_target_pairs={{0,4},{1,5},{2,6},{3,7},{4,0},{5,1},{6,2},{7,3},{8,12},{9,13},{10,... | collective-permute-start | bytes 1769480 | tf_op jit(solution)/shard_map/ppermute | solution.py:645
  144.4 3.1 %copy-start.1 = (bf16[8,48,768]{2,1,0:T(8,128)(2,1)}, bf16[8,48,768]{2,1,0:T(8,128)(2,1)S(1)}, u32[]{:S(2)}) copy-start(bf16[8,48,768]{2,1,0:T(8,128)(2,1)S(1)} %collective-permute-done.14.refs_4_) | copy-start | bytes 1769476
  145.7 8.8 %collective-permute-start.15 = (bf16[4,48,768]{2,1,0:T(8,128)(2,1)S(1)}, bf16[4,48,768]{2,1,0:T(8,128)(2,1)S(1)}, u32[]{:S(2)}, u32[]{:S(2)}) collective-permute-start(bf16[4,48,768]{2,1,0:T(8,128)(2,1)S(1)} %add_convert_fusion.1), channel_id=1, source_target_pairs={{0,2},{1,3},{2,0},{3,1},{4,6},{5,7},{6,4},{7,5},{8,10},{9,11},{10,... | collective-permute-start | bytes 884744 | tf_op jit(solution)/shard_map/ppermute | solution.py:645
  148.5 7.2 %collective-permute-start.19 = (bf16[16,48,384]{2,1,0:T(8,128)(2,1)}, bf16[16,48,384]{2,1,0:T(8,128)(2,1)S(1)}, u32[]{:S(2)}, u32[]{:S(2)}) collective-permute-start(bf16[16,48,384]{2,1,0:T(8,128)(2,1)} %shard_map.339), channel_id=1, source_target_pairs={{0,1},{1,0},{2,3},{3,2},{4,5},{5,4},{6,7},{7,6},{8,9},{9,8},{10,11... | collective-permute-start | bytes 1769480 | tf_op jit(solution)/shard_map/ppermute | solution.py:645
  148.6 6.0 %copy-start.2 = (bf16[8,48,768]{2,1,0:T(8,128)(2,1)S(1)}, bf16[8,48,768]{2,1,0:T(8,128)(2,1)}, u32[]{:S(2)}) copy-start(bf16[8,48,768]{2,1,0:T(8,128)(2,1)} %copy-done.1) | copy-start | bytes 1769476
  152.6 3.2 %copy-start.9 = (bf16[16,48,384]{2,1,0:T(8,128)(2,1)S(1)}, bf16[16,48,384]{2,1,0:T(8,128)(2,1)}, u32[]{:S(2)}) copy-start(bf16[16,48,384]{2,1,0:T(8,128)(2,1)} %get-tuple-element.112) | copy-start | bytes 1769476
  156.0 3.6 %copy-start.13 = (bf16[4,48,384]{2,1,0:T(8,128)(2,1)}, bf16[4,48,384]{2,1,0:T(8,128)(2,1)S(1)}, u32[]{:S(2)}) copy-start(bf16[4,48,384]{2,1,0:T(8,128)(2,1)S(1)} %get-tuple-element.161.refs_1_) | copy-start | bytes 442372
  156.0 7.5 %collective-permute-start.22 = (bf16[4,48,384]{2,1,0:T(8,128)(2,1)S(1)}, bf16[4,48,384]{2,1,0:T(8,128)(2,1)S(1)}, u32[]{:S(2)}, u32[]{:S(2)}) collective-permute-start(bf16[4,48,384]{2,1,0:T(8,128)(2,1)S(1)} %get-tuple-element.162), channel_id=1, source_target_pairs={{0,6},{1,7},{2,4},{3,5},{4,2},{5,3},{6,0},{7,1},{8,14},{9,15},{10,... | collective-permute-start | bytes 442376 | tf_op jit(solution)/shard_map/ppermute | solution.py:645
  157.9 7.1 %collective-permute-start.21 = (bf16[4,48,384]{2,1,0:T(8,128)(2,1)S(1)}, bf16[4,48,384]{2,1,0:T(8,128)(2,1)S(1)}, u32[]{:S(2)}, u32[]{:S(2)}) collective-permute-start(bf16[4,48,384]{2,1,0:T(8,128)(2,1)S(1)} %get-tuple-element.163), channel_id=1, source_target_pairs={{0,4},{1,5},{2,6},{3,7},{4,0},{5,1},{6,2},{7,3},{8,12},{9,13},{10,... | collective-permute-start | bytes 442376 | tf_op jit(solution)/shard_map/ppermute | solution.py:645
  159.2 5.9 %collective-permute-start.20 = (bf16[4,48,384]{2,1,0:T(8,128)(2,1)S(1)}, bf16[4,48,384]{2,1,0:T(8,128)(2,1)S(1)}, u32[]{:S(2)}, u32[]{:S(2)}) collective-permute-start(bf16[4,48,384]{2,1,0:T(8,128)(2,1)S(1)} %get-tuple-element.161.refs_1_), channel_id=1, source_target_pairs={{0,2},{1,3},{2,0},{3,1},{4,6},{5,7},{6,4},{7,5},{8,10},{9,11},{10,... | collective-permute-start | bytes 442376 | tf_op jit(solution)/shard_map/ppermute | solution.py:645
  165.2 4.5 %copy-start.18 = (bf16[1,48,1152]{2,1,0:T(8,128)(2,1)}, bf16[1,48,1152]{2,1,0:T(8,128)(2,1)S(1)}, u32[]{:S(2)}) copy-start(bf16[1,48,1152]{2,1,0:T(8,128)(2,1)S(1)} %get-tuple-element.166._) | copy-start | bytes 331780
  165.2 15.3 %collective-permute-start.25 = (bf16[1,48,1152]{2,1,0:T(8,128)(2,1)S(1)}, bf16[1,48,1152]{2,1,0:T(8,128)(2,1)S(1)}, u32[]{:S(2)}, u32[]{:S(2)}) collective-permute-start(bf16[1,48,1152]{2,1,0:T(8,128)(2,1)S(1)} %get-tuple-element.164), channel_id=1, source_target_pairs={{0,24},{1,25},{2,26},{3,27},{4,28},{5,29},{6,30},{7,31},{8,16},{9,... | collective-permute-start | bytes 331784 | tf_op jit(solution)/shard_map/ppermute | solution.py:645
  167.8 12.7 %collective-permute-start.24 = (bf16[1,48,1152]{2,1,0:T(8,128)(2,1)S(1)}, bf16[1,48,1152]{2,1,0:T(8,128)(2,1)S(1)}, u32[]{:S(2)}, u32[]{:S(2)}) collective-permute-start(bf16[1,48,1152]{2,1,0:T(8,128)(2,1)S(1)} %get-tuple-element.165), channel_id=1, source_target_pairs={{0,16},{1,17},{2,18},{3,19},{4,20},{5,21},{6,22},{7,23},{8,24},{9,... | collective-permute-start | bytes 331784 | tf_op jit(solution)/shard_map/ppermute | solution.py:645
  167.8 12.7 %collective-permute-start.23 = (bf16[1,48,1152]{2,1,0:T(8,128)(2,1)S(1)}, bf16[1,48,1152]{2,1,0:T(8,128)(2,1)S(1)}, u32[]{:S(2)}, u32[]{:S(2)}) collective-permute-start(bf16[1,48,1152]{2,1,0:T(8,128)(2,1)S(1)} %get-tuple-element.166._), channel_id=1, source_target_pairs={{0,8},{1,9},{2,10},{3,11},{4,12},{5,13},{6,14},{7,15},{8,0},{9,1},... | collective-permute-start | bytes 331784 | tf_op jit(solution)/shard_map/ppermute | solution.py:645
  178.3 24.5 %collective-permute-start.27 = (bf16[576,384]{1,0:T(8,128)(2,1)}, bf16[576,384]{1,0:T(8,128)(2,1)S(1)}, u32[]{:S(2)}, u32[]{:S(2)}) collective-permute-start(bf16[576,384]{1,0:T(8,128)(2,1)} %get-tuple-element.132), channel_id=1, source_target_pairs={{0,2},{1,3},{2,0},{3,1},{4,6},{5,7},{6,4},{7,5},{8,10},{9,11},{10,... | collective-permute-start | bytes 1327112 | tf_op jit(solution)/shard_map/ppermute | solution.py:645
  180.5 22.7 %collective-permute-start.28 = (bf16[576,384]{1,0:T(8,128)(2,1)}, bf16[576,384]{1,0:T(8,128)(2,1)S(1)}, u32[]{:S(2)}, u32[]{:S(2)}) collective-permute-start(bf16[576,384]{1,0:T(8,128)(2,1)} %get-tuple-element.133), channel_id=1, source_target_pairs={{0,3},{1,2},{2,1},{3,0},{4,7},{5,6},{6,5},{7,4},{8,11},{9,10},{10,... | collective-permute-start | bytes 1327112 | tf_op jit(solution)/shard_map/ppermute | solution.py:645
  183.5 19.7 %collective-permute-start.26 = (bf16[576,384]{1,0:T(8,128)(2,1)}, bf16[576,384]{1,0:T(8,128)(2,1)S(1)}, u32[]{:S(2)}, u32[]{:S(2)}) collective-permute-start(bf16[576,384]{1,0:T(8,128)(2,1)} %shard_map.346), channel_id=1, source_target_pairs={{0,1},{1,0},{2,3},{3,2},{4,5},{5,4},{6,7},{7,6},{8,9},{9,8},{10,11... | collective-permute-start | bytes 1327112 | tf_op jit(solution)/shard_map/ppermute | solution.py:645
  184.2 5.1 %collective-permute-start.31 = (f32[24,384]{1,0:T(8,128)}, f32[24,384]{1,0:T(8,128)S(1)}, u32[]{:S(2)}, u32[]{:S(2)}) collective-permute-start(f32[24,384]{1,0:T(8,128)} %get-tuple-element.136), channel_id=1, source_target_pairs={{0,12},{1,13},{2,14},{3,15},{4,8},{5,9},{6,10},{7,11},{8,4},{9,5},... | collective-permute-start | bytes 110600 | tf_op jit(solution)/shard_map/ppermute | solution.py:645
  184.8 5.5 %collective-permute-start.30 = (f32[24,384]{1,0:T(8,128)}, f32[24,384]{1,0:T(8,128)S(1)}, u32[]{:S(2)}, u32[]{:S(2)}) collective-permute-start(f32[24,384]{1,0:T(8,128)} %get-tuple-element.136), channel_id=1, source_target_pairs={{0,8},{1,9},{2,10},{3,11},{4,12},{5,13},{6,14},{7,15},{8,0},{9,1},... | collective-permute-start | bytes 110600 | tf_op jit(solution)/shard_map/ppermute | solution.py:645
  189.3 4.2 %collective-permute-start.29 = (f32[24,384]{1,0:T(8,128)}, f32[24,384]{1,0:T(8,128)S(1)}, u32[]{:S(2)}, u32[]{:S(2)}) collective-permute-start(f32[24,384]{1,0:T(8,128)} %get-tuple-element.136), channel_id=1, source_target_pairs={{0,4},{1,5},{2,6},{3,7},{4,0},{5,1},{6,2},{7,3},{8,12},{9,13},{10,... | collective-permute-start | bytes 110600 | tf_op jit(solution)/shard_map/ppermute | solution.py:645
  194.3 4.9 %copy-start.14 = (f32[24,384]{1,0:T(8,128)}, f32[24,384]{1,0:T(8,128)S(1)}, u32[]{:S(2)}) copy-start(f32[24,384]{1,0:T(8,128)S(1)} %add_add_fusion.refs_0_) | copy-start | bytes 110596
  194.3 4.9 %collective-permute-start.32 = (f32[24,384]{1,0:T(8,128)S(1)}, f32[24,384]{1,0:T(8,128)S(1)}, u32[]{:S(2)}, u32[]{:S(2)}) collective-permute-start(f32[24,384]{1,0:T(8,128)S(1)} %add_add_fusion.refs_0_), channel_id=1, source_target_pairs={{0,16},{1,17},{2,18},{3,19},{4,20},{5,21},{6,22},{7,23},{8,24},{9,... | collective-permute-start | bytes 110600 | tf_op jit(solution)/shard_map/ppermute | solution.py:645
  201.3 5.6 %collective-permute-start.35 = (f32[64,128]{1,0:T(8,128)}, f32[64,128]{1,0:T(8,128)S(1)}, u32[]{:S(2)}, u32[]{:S(2)}) collective-permute-start(f32[64,128]{1,0:T(8,128)} %get-tuple-element.138.refs_0_), channel_id=1, source_target_pairs={{0,3},{1,2},{2,1},{3,0},{4,7},{5,6},{6,5},{7,4},{8,11},{9,10},{10,... | collective-permute-start | bytes 98312 | tf_op jit(solution)/shard_map/ppermute | solution.py:645
  201.3 5.6 %collective-permute-start.34 = (f32[64,128]{1,0:T(8,128)}, f32[64,128]{1,0:T(8,128)S(1)}, u32[]{:S(2)}, u32[]{:S(2)}) collective-permute-start(f32[64,128]{1,0:T(8,128)} %get-tuple-element.138.refs_0_), channel_id=1, source_target_pairs={{0,2},{1,3},{2,0},{3,1},{4,6},{5,7},{6,4},{7,5},{8,10},{9,11},{10,... | collective-permute-start | bytes 98312 | tf_op jit(solution)/shard_map/ppermute | solution.py:645
  202.8 4.1 %collective-permute-start.33 = (f32[64,128]{1,0:T(8,128)}, f32[64,128]{1,0:T(8,128)S(1)}, u32[]{:S(2)}, u32[]{:S(2)}) collective-permute-start(f32[64,128]{1,0:T(8,128)} %get-tuple-element.138.refs_0_), channel_id=1, source_target_pairs={{0,1},{1,0},{2,3},{3,2},{4,5},{5,4},{6,7},{7,6},{8,9},{9,8},{10,11... | collective-permute-start | bytes 98312 | tf_op jit(solution)/shard_map/ppermute | solution.py:645
  (21 other events, 17.0 us)
